TPU v7x, 128 devices: a whole 4x4x4 slice. The times are simulated.
128 devices in a mesh: gy: 16 (over y_hi, x, core), gx: 8 (over y_lo, z).
Axes of the slice: x: 4, y: 4 (y_hi: 2, y_lo: 2; y = y_hi * 2 + y_lo), z: 4, core: 2. Of those that a mesh axis runs over, the one named last changes fastest.
Arguments:
- latent: bfloat16 [1, 4, 384, 128, 128], P(None, None, 'gy', 'gx'), may hold values from -6 to 6
- conv_one: bfloat16 [3, 3, 3, 128, 128], replicated, may hold values from -0.109375 to 0.109375
- conv_two: bfloat16 [3, 3, 3, 128, 128], replicated, may hold values from -0.109375 to 0.109375
- to_rgb: bfloat16 [3, 3, 3, 128, 3], replicated, may hold values from -0.1875 to 0.1875
- disc_one: bfloat16 [3, 3, 3, 3, 64], replicated, may hold values from -0.625 to 0.625
- disc_two: bfloat16 [3, 3, 3, 64, 128], replicated, may hold values from -0.15625 to 0.15625
- disc_head: float32 [128], replicated, may hold values from -4 to 4
Outputs:
- grad_latent: bfloat16 [1, 4, 384, 128, 128], P(None, None, 'gy', 'gx')
- logits: bfloat16 [1, 4, 384, 128], P(None, None, 'gy', 'gx')
All inputs are finite; a program needn't handle non-finite values.
Results may differ from a plain program's by a relative error of at most 0.024.
Values may be sent and summed in bfloat16 or wider, within the bound.
No kernel may reach another device: no remote copies, remote signals or barrier semaphores. Data moves between devices by JAX's collectives and lax.ppermute only.
A program may use at most 64 MiB of HBM per device.

v0:
```python
import jax
import jax.numpy as jnp
from jax import lax
from jax.sharding import PartitionSpec as P

LAST_FORM = "btyxc,cd->btyxd"
TO_FIRST = "btyxc,cd->btdyx"
TO_LAST = "btcyx,cd->btyxd"


def padded_2(x, sides, width):
    for axis, dim in sides:
        count, length = (lax.axis_size(axis), x.shape[dim])
        up = [(i, (i + 1) % count) for i in range(count - 1)]
        down = [(j, i) for i, j in up]
        last = lax.slice_in_dim(x, length - width, length, axis=dim)
        leading = lax.slice_in_dim(x, 0, width, axis=dim)
        before = lax.ppermute(last, axis, up)
        after = lax.ppermute(leading, axis, down)
        x = jnp.concatenate([before, x, after], axis=dim)
    return x


def convolve(widened, kernel, form, row_dim, forward):
    if forward:
        frame_pad = (2, 0)
        taps = kernel
    else:
        frame_pad = (0, 2)
        taps = jnp.swapaxes(jnp.flip(kernel, (0, 1, 2)), 3, 4)
    widths = [(0, 0)] * widened.ndim
    widths[1] = frame_pad
    padded = jnp.pad(widened, widths)
    frames = widened.shape[1]
    rows = widened.shape[row_dim] - 2
    cols = widened.shape[row_dim + 1] - 2
    total = None
    for depth in range(3):
        for row_tap in range(3):
            for col_tap in range(3):
                piece = lax.slice_in_dim(padded, depth, depth + frames, axis=1)
                piece = lax.slice_in_dim(piece, row_tap, row_tap + rows, axis=row_dim)
                piece = lax.slice_in_dim(piece, col_tap, col_tap + cols, axis=row_dim + 1)
                term = jnp.einsum(
                    form, piece, taps[depth, row_tap, col_tap], preferred_element_type=jnp.float32
                )
                total = term if total is None else total + term
    return total


def dsilu(value):
    sigma = jax.nn.sigmoid(value)
    return sigma * (1.0 + value * (1.0 - sigma))


def decoder_widen(field):
    return padded_2(field, (("gy", 2), ("gx", 3)), 1)


def pixel_widen(field):
    return padded_2(field, (("gy", 3), ("gx", 4)), 1)


def tile_colour(field):
    return padded_2(field, (("gy", 3), ("gx", 4)), 1)


def tile_field(field):
    return padded_2(field, (("gy", 2), ("gx", 3)), 1)


def discriminate(image, widen_colour, widen_field, disc_one, disc_two, disc_head):
    pre_first = convolve(widen_colour(image), disc_one, TO_LAST, 3, True)
    act_first = jax.nn.silu(pre_first).astype(jnp.bfloat16)
    pre_second = convolve(widen_field(act_first), disc_two, LAST_FORM, 2, True)
    scores = jnp.einsum(
        "btyxd,d->btyx", jax.nn.silu(pre_second), disc_head, precision=lax.Precision.HIGHEST
    )
    push = -jax.nn.sigmoid(-scores)
    back_second = (push[..., None] * disc_head * dsilu(pre_second)).astype(jnp.bfloat16)
    back_act = convolve(widen_field(back_second), disc_two, LAST_FORM, 2, False)
    back_first = (back_act * dsilu(pre_first)).astype(jnp.bfloat16)
    pixel_grad = convolve(widen_field(back_first), disc_one, TO_FIRST, 2, False).astype(
        jnp.bfloat16
    )
    return (scores.astype(jnp.bfloat16), pixel_grad)


def per_device(latent, conv_one, conv_two, to_rgb, disc_one, disc_two, disc_head):
    pre_one = convolve(decoder_widen(latent), conv_one, LAST_FORM, 2, True)
    act_one = jax.nn.silu(pre_one).astype(jnp.bfloat16)
    pre_two = convolve(decoder_widen(act_one), conv_two, LAST_FORM, 2, True)
    act_two = jax.nn.silu(pre_two).astype(jnp.bfloat16)
    rgb = convolve(decoder_widen(act_two), to_rgb, TO_FIRST, 2, True).astype(jnp.bfloat16)
    logits, pixel_grad = discriminate(rgb, tile_colour, tile_field, disc_one, disc_two, disc_head)
    back_rgb = convolve(pixel_widen(pixel_grad), to_rgb, TO_LAST, 3, False)
    back_two = (back_rgb * dsilu(pre_two)).astype(jnp.bfloat16)
    back_mid = convolve(decoder_widen(back_two), conv_two, LAST_FORM, 2, False)
    back_one = (back_mid * dsilu(pre_one)).astype(jnp.bfloat16)
    grad_latent = convolve(decoder_widen(back_one), conv_one, LAST_FORM, 2, False).astype(
        jnp.bfloat16
    )
    return (grad_latent, logits)


def solution(mesh):
    placed = (P(None, None, "gy", "gx", None), P(), P(), P(), P(), P(), P())
    return jax.shard_map(
        per_device,
        mesh=mesh,
        in_specs=placed,
        out_specs=(P(None, None, "gy", "gx", None), P(None, None, "gy", "gx")),
        check_vma=False,
    )
```

profile of v0, /device:TPU:112, one launch (start us, length us, event | category | flops | bytes accessed | tf_op | source)
XLA Modules:
  0.0 403.8 jit_solution(9229919013968758118)
XLA Ops:
  3.3 7.3 %collective-permute-start.1 = (bf16[1,4,1,16,128]{4,3,2,1,0:T(8,128)(2,1)S(1)}, bf16[1,4,1,16,128]{4,3,2,1,0:T(8,128)(2,1)S(1)}, u32[]{:S(2)}, u32[]{:S(2)}) collective-permute-start(bf16[1,4,1,16,128]{4,3,2,1,0:T(8,128)(2,1)S(1)} %get-tuple-element.98), channel_id=1, source_target_pairs={{8,0},{16,8},{24,16},{32,24},{40,32},{48,40},{56,48},{64,56},{72,6... | collective-permute-start | bytes 49160 | tf_op jit(solution)/shard_map/ppermute | solution.py:19
  14.4 5.6 %collective-permute-start.2 = (bf16[1,4,26,1,128]{4,3,2,1,0:T(2,128)(2,1)S(1)}, bf16[1,4,26,1,128]{4,3,2,1,0:T(2,128)(2,1)S(1)}, u32[]{:S(2)}, u32[]{:S(2)}) collective-permute-start(bf16[1,4,26,1,128]{4,3,2,1,0:T(2,128)(2,1)S(1)} %get-tuple-element.78), channel_id=1, source_target_pairs={{0,1},{1,2},{2,3},{3,4},{4,5},{5,6},{6,7},{8,9},{9,10},{10,11},{11... | collective-permute-start | bytes 79880 | tf_op jit(solution)/shard_map/ppermute | solution.py:18
  29.5 6.8 %collective-permute-start.5 = (bf16[1,4,1,16,128]{4,3,2,1,0:T(8,128)(2,1)S(1)}, bf16[1,4,1,16,128]{4,3,2,1,0:T(8,128)(2,1)S(1)}, u32[]{:S(2)}, u32[]{:S(2)}) collective-permute-start(bf16[1,4,1,16,128]{4,3,2,1,0:T(8,128)(2,1)S(1)} %get-tuple-element.97), channel_id=1, source_target_pairs={{8,0},{16,8},{24,16},{32,24},{40,32},{48,40},{56,48},{64,56},{72,6... | collective-permute-start | bytes 49160 | tf_op jit(solution)/shard_map/ppermute | solution.py:19
  38.3 6.7 %collective-permute-done.4 = bf16[1,4,1,16,128]{4,3,2,1,0:T(8,128)(2,1)S(1)} collective-permute-done((bf16[1,4,1,16,128]{4,3,2,1,0:T(8,128)(2,1)S(1)}, bf16[1,4,1,16,128]{4,3,2,1,0:T(8,128)(2,1)S(1)}, u32[]{:S(2)}, u32[]{:S(2)}) %collective-permute-start.4) | collective-permute-done | bytes 16416 | tf_op jit(solution)/shard_map/ppermute | solution.py:18
  45.1 6.1 %collective-permute-start.6 = (bf16[1,4,26,1,128]{4,3,2,1,0:T(2,128)(2,1)S(1)}, bf16[1,4,26,1,128]{4,3,2,1,0:T(2,128)(2,1)S(1)}, u32[]{:S(2)}, u32[]{:S(2)}) collective-permute-start(bf16[1,4,26,1,128]{4,3,2,1,0:T(2,128)(2,1)S(1)} %get-tuple-element.76), channel_id=1, source_target_pairs={{0,1},{1,2},{2,3},{3,4},{4,5},{5,6},{6,7},{8,9},{9,10},{10,11},{11... | collective-permute-start | bytes 79880 | tf_op jit(solution)/shard_map/ppermute | solution.py:18
  54.8 4.6 %collective-permute-done.7 = bf16[1,4,26,1,128]{4,3,2,1,0:T(2,128)(2,1)S(1)} collective-permute-done((bf16[1,4,26,1,128]{4,3,2,1,0:T(2,128)(2,1)S(1)}, bf16[1,4,26,1,128]{4,3,2,1,0:T(2,128)(2,1)S(1)}, u32[]{:S(2)}, u32[]{:S(2)}) %collective-permute-start.7) | collective-permute-done | bytes 26656 | tf_op jit(solution)/shard_map/ppermute | solution.py:19
  74.6 5.2 %collective-permute-done.8 = bf16[1,4,1,16,128]{4,3,2,1,0:T(8,128)(2,1)S(1)} collective-permute-done((bf16[1,4,1,16,128]{4,3,2,1,0:T(8,128)(2,1)S(1)}, bf16[1,4,1,16,128]{4,3,2,1,0:T(8,128)(2,1)S(1)}, u32[]{:S(2)}, u32[]{:S(2)}) %collective-permute-start.8) | collective-permute-done | bytes 16416 | tf_op jit(solution)/shard_map/ppermute | solution.py:18
  81.9 4.3 %collective-permute-start.11 = (bf16[1,4,26,1,128]{4,3,2,1,0:T(2,128)(2,1)S(1)}, bf16[1,4,26,1,128]{4,3,2,1,0:T(2,128)(2,1)S(1)}, u32[]{:S(2)}, u32[]{:S(2)}) collective-permute-start(bf16[1,4,26,1,128]{4,3,2,1,0:T(2,128)(2,1)S(1)} %get-tuple-element.73), channel_id=1, source_target_pairs={{1,0},{2,1},{3,2},{4,3},{5,4},{6,5},{7,6},{9,8},{10,9},{11,10},{12... | collective-permute-start | bytes 79880 | tf_op jit(solution)/shard_map/ppermute | solution.py:19
  120.5 5.9 %collective-permute-done.12 = bf16[1,4,3,1,16]{4,2,3,1,0:T(4,128)(2,1)S(1)} collective-permute-done((bf16[1,4,3,1,16]{4,2,3,1,0:T(4,128)(2,1)S(1)}, bf16[1,4,3,1,16]{4,2,3,1,0:T(4,128)(2,1)S(1)}, u32[]{:S(2)}, u32[]{:S(2)}) %collective-permute-start.12) | collective-permute-done | bytes 416 | tf_op jit(solution)/shard_map/ppermute | solution.py:18
  128.5 6.0 %collective-permute-start.14 = (bf16[1,4,3,26,1]{4,2,3,1,0:T(4,128)(2,1)S(1)}, bf16[1,4,3,26,1]{4,2,3,1,0:T(4,128)(2,1)S(1)}, u32[]{:S(2)}, u32[]{:S(2)}) collective-permute-start(bf16[1,4,3,26,1]{4,2,3,1,0:T(4,128)(2,1)S(1)} %get-tuple-element.148), channel_id=1, source_target_pairs={{0,1},{1,2},{2,3},{3,4},{4,5},{5,6},{6,7},{8,9},{9,10},{10,11},{11... | collective-permute-start | bytes 1880 | tf_op jit(solution)/shard_map/ppermute | solution.py:18
  169.6 5.6 %collective-permute-done.16 = bf16[1,4,1,16,64]{4,2,3,1,0:T(2,128)(2,1)S(1)} collective-permute-done((bf16[1,4,1,16,64]{4,2,3,1,0:T(2,128)(2,1)S(1)}, bf16[1,4,1,16,64]{4,2,3,1,0:T(2,128)(2,1)S(1)}, u32[]{:S(2)}, u32[]{:S(2)}) %collective-permute-start.16) | collective-permute-done | bytes 8224 | tf_op jit(solution)/shard_map/ppermute | solution.py:18
  177.2 6.6 %collective-permute-start.18 = (bf16[1,4,26,1,64]{4,2,3,1,0:T(8,128)(2,1)S(1)}, bf16[1,4,26,1,64]{4,2,3,1,0:T(8,128)(2,1)S(1)}, u32[]{:S(2)}, u32[]{:S(2)}) collective-permute-start(bf16[1,4,26,1,64]{4,2,3,1,0:T(8,128)(2,1)S(1)} %get-tuple-element.56), channel_id=1, source_target_pairs={{0,1},{1,2},{2,3},{3,4},{4,5},{5,6},{6,7},{8,9},{9,10},{10,11},{11... | collective-permute-start | bytes 39944 | tf_op jit(solution)/shard_map/ppermute | solution.py:18
  194.7 5.6 %fusion.116 = f32[1,4,24,16]{3,0,2,1:T(1,128)S(1)} fusion(f32[4,24,16,128]{3,2,1,0:T(8,128)S(1)} %convolution_add_fusion.102, f32[128]{0:T(128)S(1)} %copy-done.41), kind=kOutput, calls=%fused_computation.379 | convolution fusion | flops 3145728 | bytes 793088 | tf_op jit(solution)/shard_map/btyxd,d->btyx/dot_general | solution.py:76
  206.1 5.9 %collective-permute-done.20 = bf16[1,4,1,16,128]{4,3,2,1,0:T(8,128)(2,1)S(1)} collective-permute-done((bf16[1,4,1,16,128]{4,3,2,1,0:T(8,128)(2,1)S(1)}, bf16[1,4,1,16,128]{4,3,2,1,0:T(8,128)(2,1)S(1)}, u32[]{:S(2)}, u32[]{:S(2)}) %collective-permute-start.20) | collective-permute-done | bytes 16416 | tf_op jit(solution)/shard_map/ppermute | solution.py:18
  214.0 6.8 %collective-permute-start.22 = (bf16[1,4,26,1,128]{4,3,2,1,0:T(2,128)(2,1)S(1)}, bf16[1,4,26,1,128]{4,3,2,1,0:T(2,128)(2,1)S(1)}, u32[]{:S(2)}, u32[]{:S(2)}) collective-permute-start(bf16[1,4,26,1,128]{4,3,2,1,0:T(2,128)(2,1)S(1)} %get-tuple-element.69), channel_id=1, source_target_pairs={{0,1},{1,2},{2,3},{3,4},{4,5},{5,6},{6,7},{8,9},{9,10},{10,11},{11... | collective-permute-start | bytes 79880 | tf_op jit(solution)/shard_map/ppermute | solution.py:18
  241.0 6.4 %collective-permute-done.24 = bf16[1,4,1,16,64]{4,2,3,1,0:T(2,128)(2,1)S(1)} collective-permute-done((bf16[1,4,1,16,64]{4,2,3,1,0:T(2,128)(2,1)S(1)}, bf16[1,4,1,16,64]{4,2,3,1,0:T(2,128)(2,1)S(1)}, u32[]{:S(2)}, u32[]{:S(2)}) %collective-permute-start.24) | collective-permute-done | bytes 8224 | tf_op jit(solution)/shard_map/ppermute | solution.py:18
  249.3 6.5 %collective-permute-start.26 = (bf16[1,4,26,1,64]{4,2,3,1,0:T(8,128)(2,1)S(1)}, bf16[1,4,26,1,64]{4,2,3,1,0:T(8,128)(2,1)S(1)}, u32[]{:S(2)}, u32[]{:S(2)}) collective-permute-start(bf16[1,4,26,1,64]{4,2,3,1,0:T(8,128)(2,1)S(1)} %get-tuple-element.52), channel_id=1, source_target_pairs={{0,1},{1,2},{2,3},{3,4},{4,5},{5,6},{6,7},{8,9},{9,10},{10,11},{11... | collective-permute-start | bytes 39944 | tf_op jit(solution)/shard_map/ppermute | solution.py:18
  285.4 4.6 %collective-permute-done.28 = bf16[1,4,3,1,16]{3,2,4,1,0:T(4,128)(2,1)S(1)} collective-permute-done((bf16[1,4,3,1,16]{3,2,4,1,0:T(4,128)(2,1)S(1)}, bf16[1,4,3,1,16]{3,2,4,1,0:T(4,128)(2,1)S(1)}, u32[]{:S(2)}, u32[]{:S(2)}) %collective-permute-start.28) | collective-permute-done | bytes 416 | tf_op jit(solution)/shard_map/ppermute | solution.py:18
  292.1 6.3 %collective-permute-start.30 = (bf16[1,4,3,26,1]{3,2,4,1,0:T(4,128)(2,1)S(1)}, bf16[1,4,3,26,1]{3,2,4,1,0:T(4,128)(2,1)S(1)}, u32[]{:S(2)}, u32[]{:S(2)}) collective-permute-start(bf16[1,4,3,26,1]{3,2,4,1,0:T(4,128)(2,1)S(1)} %get-tuple-element.103), channel_id=1, source_target_pairs={{0,1},{1,2},{2,3},{3,4},{4,5},{5,6},{6,7},{8,9},{9,10},{10,11},{11... | collective-permute-start | bytes 1880 | tf_op jit(solution)/shard_map/ppermute | solution.py:18
  344.6 6.2 %collective-permute-done.32 = bf16[1,4,1,16,128]{4,3,2,1,0:T(8,128)(2,1)S(1)} collective-permute-done((bf16[1,4,1,16,128]{4,3,2,1,0:T(8,128)(2,1)S(1)}, bf16[1,4,1,16,128]{4,3,2,1,0:T(8,128)(2,1)S(1)}, u32[]{:S(2)}, u32[]{:S(2)}) %collective-permute-start.32) | collective-permute-done | bytes 16416 | tf_op jit(solution)/shard_map/ppermute | solution.py:18
  350.8 6.3 %collective-permute-start.34 = (bf16[1,4,26,1,128]{4,3,2,1,0:T(2,128)(2,1)S(1)}, bf16[1,4,26,1,128]{4,3,2,1,0:T(2,128)(2,1)S(1)}, u32[]{:S(2)}, u32[]{:S(2)}) collective-permute-start(bf16[1,4,26,1,128]{4,3,2,1,0:T(2,128)(2,1)S(1)} %get-tuple-element.64), channel_id=1, source_target_pairs={{0,1},{1,2},{2,3},{3,4},{4,5},{5,6},{6,7},{8,9},{9,10},{10,11},{11... | collective-permute-start | bytes 79880 | tf_op jit(solution)/shard_map/ppermute | solution.py:18
  359.6 5.7 %collective-permute-done.35 = bf16[1,4,26,1,128]{4,3,2,1,0:T(2,128)(2,1)S(1)} collective-permute-done((bf16[1,4,26,1,128]{4,3,2,1,0:T(2,128)(2,1)S(1)}, bf16[1,4,26,1,128]{4,3,2,1,0:T(2,128)(2,1)S(1)}, u32[]{:S(2)}, u32[]{:S(2)}) %collective-permute-start.35) | collective-permute-done | bytes 26656 | tf_op jit(solution)/shard_map/ppermute | solution.py:19
  379.0 5.6 %collective-permute-done.36 = bf16[1,4,1,16,128]{4,3,2,1,0:T(8,128)(2,1)S(1)} collective-permute-done((bf16[1,4,1,16,128]{4,3,2,1,0:T(8,128)(2,1)S(1)}, bf16[1,4,1,16,128]{4,3,2,1,0:T(8,128)(2,1)S(1)}, u32[]{:S(2)}, u32[]{:S(2)}) %collective-permute-start.36) | collective-permute-done | bytes 16416 | tf_op jit(solution)/shard_map/ppermute | solution.py:18
  386.7 4.2 %collective-permute-start.39 = (bf16[1,4,26,1,128]{4,3,2,1,0:T(2,128)(2,1)S(1)}, bf16[1,4,26,1,128]{4,3,2,1,0:T(2,128)(2,1)S(1)}, u32[]{:S(2)}, u32[]{:S(2)}) collective-permute-start(bf16[1,4,26,1,128]{4,3,2,1,0:T(2,128)(2,1)S(1)} %get-tuple-element.61), channel_id=1, source_target_pairs={{1,0},{2,1},{3,2},{4,3},{5,4},{6,5},{7,6},{9,8},{10,9},{11,10},{12... | collective-permute-start | bytes 79880 | tf_op jit(solution)/shard_map/ppermute | solution.py:19
  (541 shorter events, 258.8 us)
Async XLA Ops:
  1.4 9.2 %collective-permute-start = (bf16[1,4,1,16,128]{4,3,2,1,0:T(8,128)(2,1)S(1)}, bf16[1,4,1,16,128]{4,3,2,1,0:T(8,128)(2,1)S(1)}, u32[]{:S(2)}, u32[]{:S(2)}) collective-permute-start(bf16[1,4,1,16,128]{4,3,2,1,0:T(8,128)(2,1)S(1)} %get-tuple-element.99), channel_id=1, source_target_pairs={{0,8},{8,16},{16,24},{24,32},{32,40},{40,48},{48,56},{56,64},{64,7... | collective-permute-start | bytes 49160 | tf_op jit(solution)/shard_map/ppermute | solution.py:18
  3.3 8.7 %collective-permute-start.1 = (bf16[1,4,1,16,128]{4,3,2,1,0:T(8,128)(2,1)S(1)}, bf16[1,4,1,16,128]{4,3,2,1,0:T(8,128)(2,1)S(1)}, u32[]{:S(2)}, u32[]{:S(2)}) collective-permute-start(bf16[1,4,1,16,128]{4,3,2,1,0:T(8,128)(2,1)S(1)} %get-tuple-element.98), channel_id=1, source_target_pairs={{8,0},{16,8},{24,16},{32,24},{40,32},{48,40},{56,48},{64,56},{72,6... | collective-permute-start | bytes 49160 | tf_op jit(solution)/shard_map/ppermute | solution.py:19
  12.1 9.0 %collective-permute-start.3 = (bf16[1,4,26,1,128]{4,3,2,1,0:T(2,128)(2,1)S(1)}, bf16[1,4,26,1,128]{4,3,2,1,0:T(2,128)(2,1)S(1)}, u32[]{:S(2)}, u32[]{:S(2)}) collective-permute-start(bf16[1,4,26,1,128]{4,3,2,1,0:T(2,128)(2,1)S(1)} %get-tuple-element.79), channel_id=1, source_target_pairs={{1,0},{2,1},{3,2},{4,3},{5,4},{6,5},{7,6},{9,8},{10,9},{11,10},{12... | collective-permute-start | bytes 79880 | tf_op jit(solution)/shard_map/ppermute | solution.py:19
  29.5 8.8 %collective-permute-start.5 = (bf16[1,4,1,16,128]{4,3,2,1,0:T(8,128)(2,1)S(1)}, bf16[1,4,1,16,128]{4,3,2,1,0:T(8,128)(2,1)S(1)}, u32[]{:S(2)}, u32[]{:S(2)}) collective-permute-start(bf16[1,4,1,16,128]{4,3,2,1,0:T(8,128)(2,1)S(1)} %get-tuple-element.97), channel_id=1, source_target_pairs={{8,0},{16,8},{24,16},{32,24},{40,32},{48,40},{56,48},{64,56},{72,6... | collective-permute-start | bytes 49160 | tf_op jit(solution)/shard_map/ppermute | solution.py:19
  36.4 8.7 %collective-permute-start.4 = (bf16[1,4,1,16,128]{4,3,2,1,0:T(8,128)(2,1)S(1)}, bf16[1,4,1,16,128]{4,3,2,1,0:T(8,128)(2,1)S(1)}, u32[]{:S(2)}, u32[]{:S(2)}) collective-permute-start(bf16[1,4,1,16,128]{4,3,2,1,0:T(8,128)(2,1)S(1)} %get-tuple-element.96), channel_id=1, source_target_pairs={{0,8},{8,16},{16,24},{24,32},{32,40},{40,48},{48,56},{56,64},{64,7... | collective-permute-start | bytes 49160 | tf_op jit(solution)/shard_map/ppermute | solution.py:18
  45.1 9.7 %collective-permute-start.6 = (bf16[1,4,26,1,128]{4,3,2,1,0:T(2,128)(2,1)S(1)}, bf16[1,4,26,1,128]{4,3,2,1,0:T(2,128)(2,1)S(1)}, u32[]{:S(2)}, u32[]{:S(2)}) collective-permute-start(bf16[1,4,26,1,128]{4,3,2,1,0:T(2,128)(2,1)S(1)} %get-tuple-element.76), channel_id=1, source_target_pairs={{0,1},{1,2},{2,3},{3,4},{4,5},{5,6},{6,7},{8,9},{9,10},{10,11},{11... | collective-permute-start | bytes 79880 | tf_op jit(solution)/shard_map/ppermute | solution.py:18
  71.2 8.7 %collective-permute-start.8 = (bf16[1,4,1,16,128]{4,3,2,1,0:T(8,128)(2,1)S(1)}, bf16[1,4,1,16,128]{4,3,2,1,0:T(8,128)(2,1)S(1)}, u32[]{:S(2)}, u32[]{:S(2)}) collective-permute-start(bf16[1,4,1,16,128]{4,3,2,1,0:T(8,128)(2,1)S(1)} %get-tuple-element.94), channel_id=1, source_target_pairs={{0,8},{8,16},{16,24},{24,32},{32,40},{40,48},{48,56},{56,64},{64,7... | collective-permute-start | bytes 49160 | tf_op jit(solution)/shard_map/ppermute | solution.py:18
  80.0 8.3 %collective-permute-start.10 = (bf16[1,4,26,1,128]{4,3,2,1,0:T(2,128)(2,1)S(1)}, bf16[1,4,26,1,128]{4,3,2,1,0:T(2,128)(2,1)S(1)}, u32[]{:S(2)}, u32[]{:S(2)}) collective-permute-start(bf16[1,4,26,1,128]{4,3,2,1,0:T(2,128)(2,1)S(1)} %get-tuple-element.72), channel_id=1, source_target_pairs={{0,1},{1,2},{2,3},{3,4},{4,5},{5,6},{6,7},{8,9},{9,10},{10,11},{11... | collective-permute-start | bytes 79880 | tf_op jit(solution)/shard_map/ppermute | solution.py:18
  81.9 8.1 %collective-permute-start.11 = (bf16[1,4,26,1,128]{4,3,2,1,0:T(2,128)(2,1)S(1)}, bf16[1,4,26,1,128]{4,3,2,1,0:T(2,128)(2,1)S(1)}, u32[]{:S(2)}, u32[]{:S(2)}) collective-permute-start(bf16[1,4,26,1,128]{4,3,2,1,0:T(2,128)(2,1)S(1)} %get-tuple-element.73), channel_id=1, source_target_pairs={{1,0},{2,1},{3,2},{4,3},{5,4},{6,5},{7,6},{9,8},{10,9},{11,10},{12... | collective-permute-start | bytes 79880 | tf_op jit(solution)/shard_map/ppermute | solution.py:19
  117.8 8.5 %collective-permute-start.12 = (bf16[1,4,3,1,16]{4,2,3,1,0:T(4,128)(2,1)S(1)}, bf16[1,4,3,1,16]{4,2,3,1,0:T(4,128)(2,1)S(1)}, u32[]{:S(2)}, u32[]{:S(2)}) collective-permute-start(bf16[1,4,3,1,16]{4,2,3,1,0:T(4,128)(2,1)S(1)} %get-tuple-element.152), channel_id=1, source_target_pairs={{0,8},{8,16},{16,24},{24,32},{32,40},{40,48},{48,56},{56,64},{64,7... | collective-permute-start | bytes 1160 | tf_op jit(solution)/shard_map/ppermute | solution.py:18
  126.6 9.5 %collective-permute-start.15 = (bf16[1,4,3,26,1]{4,2,3,1,0:T(4,128)(2,1)S(1)}, bf16[1,4,3,26,1]{4,2,3,1,0:T(4,128)(2,1)S(1)}, u32[]{:S(2)}, u32[]{:S(2)}) collective-permute-start(bf16[1,4,3,26,1]{4,2,3,1,0:T(4,128)(2,1)S(1)} %get-tuple-element.149), channel_id=1, source_target_pairs={{1,0},{2,1},{3,2},{4,3},{5,4},{6,5},{7,6},{9,8},{10,9},{11,10},{12... | collective-permute-start | bytes 1880 | tf_op jit(solution)/shard_map/ppermute | solution.py:19
  128.5 8.3 %collective-permute-start.14 = (bf16[1,4,3,26,1]{4,2,3,1,0:T(4,128)(2,1)S(1)}, bf16[1,4,3,26,1]{4,2,3,1,0:T(4,128)(2,1)S(1)}, u32[]{:S(2)}, u32[]{:S(2)}) collective-permute-start(bf16[1,4,3,26,1]{4,2,3,1,0:T(4,128)(2,1)S(1)} %get-tuple-element.148), channel_id=1, source_target_pairs={{0,1},{1,2},{2,3},{3,4},{4,5},{5,6},{6,7},{8,9},{9,10},{10,11},{11... | collective-permute-start | bytes 1880 | tf_op jit(solution)/shard_map/ppermute | solution.py:18
  166.3 8.8 %collective-permute-start.16 = (bf16[1,4,1,16,64]{4,2,3,1,0:T(2,128)(2,1)S(1)}, bf16[1,4,1,16,64]{4,2,3,1,0:T(2,128)(2,1)S(1)}, u32[]{:S(2)}, u32[]{:S(2)}) collective-permute-start(bf16[1,4,1,16,64]{4,2,3,1,0:T(2,128)(2,1)S(1)} %get-tuple-element.92), channel_id=1, source_target_pairs={{0,8},{8,16},{16,24},{24,32},{32,40},{40,48},{48,56},{56,64},{64,7... | collective-permute-start | bytes 24584 | tf_op jit(solution)/shard_map/ppermute | solution.py:18
  175.2 9.0 %collective-permute-start.19 = (bf16[1,4,26,1,64]{4,2,3,1,0:T(8,128)(2,1)S(1)}, bf16[1,4,26,1,64]{4,2,3,1,0:T(8,128)(2,1)S(1)}, u32[]{:S(2)}, u32[]{:S(2)}) collective-permute-start(bf16[1,4,26,1,64]{4,2,3,1,0:T(8,128)(2,1)S(1)} %get-tuple-element.57), channel_id=1, source_target_pairs={{1,0},{2,1},{3,2},{4,3},{5,4},{6,5},{7,6},{9,8},{10,9},{11,10},{12... | collective-permute-start | bytes 39944 | tf_op jit(solution)/shard_map/ppermute | solution.py:19
  203.3 8.7 %collective-permute-start.20 = (bf16[1,4,1,16,128]{4,3,2,1,0:T(8,128)(2,1)S(1)}, bf16[1,4,1,16,128]{4,3,2,1,0:T(8,128)(2,1)S(1)}, u32[]{:S(2)}, u32[]{:S(2)}) collective-permute-start(bf16[1,4,1,16,128]{4,3,2,1,0:T(8,128)(2,1)S(1)} %get-tuple-element.88), channel_id=1, source_target_pairs={{0,8},{8,16},{16,24},{24,32},{32,40},{40,48},{48,56},{56,64},{64,7... | collective-permute-start | bytes 49160 | tf_op jit(solution)/shard_map/ppermute | solution.py:18
  212.1 8.8 %collective-permute-start.23 = (bf16[1,4,26,1,128]{4,3,2,1,0:T(2,128)(2,1)S(1)}, bf16[1,4,26,1,128]{4,3,2,1,0:T(2,128)(2,1)S(1)}, u32[]{:S(2)}, u32[]{:S(2)}) collective-permute-start(bf16[1,4,26,1,128]{4,3,2,1,0:T(2,128)(2,1)S(1)} %get-tuple-element.68), channel_id=1, source_target_pairs={{1,0},{2,1},{3,2},{4,3},{5,4},{6,5},{7,6},{9,8},{10,9},{11,10},{12... | collective-permute-start | bytes 79880 | tf_op jit(solution)/shard_map/ppermute | solution.py:19
  214.0 8.2 %collective-permute-start.22 = (bf16[1,4,26,1,128]{4,3,2,1,0:T(2,128)(2,1)S(1)}, bf16[1,4,26,1,128]{4,3,2,1,0:T(2,128)(2,1)S(1)}, u32[]{:S(2)}, u32[]{:S(2)}) collective-permute-start(bf16[1,4,26,1,128]{4,3,2,1,0:T(2,128)(2,1)S(1)} %get-tuple-element.69), channel_id=1, source_target_pairs={{0,1},{1,2},{2,3},{3,4},{4,5},{5,6},{6,7},{8,9},{9,10},{10,11},{11... | collective-permute-start | bytes 79880 | tf_op jit(solution)/shard_map/ppermute | solution.py:18
  238.5 8.8 %collective-permute-start.24 = (bf16[1,4,1,16,64]{4,2,3,1,0:T(2,128)(2,1)S(1)}, bf16[1,4,1,16,64]{4,2,3,1,0:T(2,128)(2,1)S(1)}, u32[]{:S(2)}, u32[]{:S(2)}) collective-permute-start(bf16[1,4,1,16,64]{4,2,3,1,0:T(2,128)(2,1)S(1)} %get-tuple-element.84), channel_id=1, source_target_pairs={{0,8},{8,16},{16,24},{24,32},{32,40},{40,48},{48,56},{56,64},{64,7... | collective-permute-start | bytes 24584 | tf_op jit(solution)/shard_map/ppermute | solution.py:18
  247.4 9.2 %collective-permute-start.27 = (bf16[1,4,26,1,64]{4,2,3,1,0:T(8,128)(2,1)S(1)}, bf16[1,4,26,1,64]{4,2,3,1,0:T(8,128)(2,1)S(1)}, u32[]{:S(2)}, u32[]{:S(2)}) collective-permute-start(bf16[1,4,26,1,64]{4,2,3,1,0:T(8,128)(2,1)S(1)} %get-tuple-element.53), channel_id=1, source_target_pairs={{1,0},{2,1},{3,2},{4,3},{5,4},{6,5},{7,6},{9,8},{10,9},{11,10},{12... | collective-permute-start | bytes 39944 | tf_op jit(solution)/shard_map/ppermute | solution.py:19
  280.9 9.2 %collective-permute-start.28 = (bf16[1,4,3,1,16]{3,2,4,1,0:T(4,128)(2,1)S(1)}, bf16[1,4,3,1,16]{3,2,4,1,0:T(4,128)(2,1)S(1)}, u32[]{:S(2)}, u32[]{:S(2)}) collective-permute-start(bf16[1,4,3,1,16]{3,2,4,1,0:T(4,128)(2,1)S(1)} %get-tuple-element.162), channel_id=1, source_target_pairs={{0,8},{8,16},{16,24},{24,32},{32,40},{40,48},{48,56},{56,64},{64,7... | collective-permute-start | bytes 1160 | tf_op jit(solution)/shard_map/ppermute | solution.py:18
  290.1 8.8 %collective-permute-start.31 = (bf16[1,4,3,26,1]{3,2,4,1,0:T(4,128)(2,1)S(1)}, bf16[1,4,3,26,1]{3,2,4,1,0:T(4,128)(2,1)S(1)}, u32[]{:S(2)}, u32[]{:S(2)}) collective-permute-start(bf16[1,4,3,26,1]{3,2,4,1,0:T(4,128)(2,1)S(1)} %get-tuple-element.102), channel_id=1, source_target_pairs={{1,0},{2,1},{3,2},{4,3},{5,4},{6,5},{7,6},{9,8},{10,9},{11,10},{12... | collective-permute-start | bytes 1880 | tf_op jit(solution)/shard_map/ppermute | solution.py:19
  342.1 8.7 %collective-permute-start.32 = (bf16[1,4,1,16,128]{4,3,2,1,0:T(8,128)(2,1)S(1)}, bf16[1,4,1,16,128]{4,3,2,1,0:T(8,128)(2,1)S(1)}, u32[]{:S(2)}, u32[]{:S(2)}) collective-permute-start(bf16[1,4,1,16,128]{4,3,2,1,0:T(8,128)(2,1)S(1)} %get-tuple-element.82), channel_id=1, source_target_pairs={{0,8},{8,16},{16,24},{24,32},{32,40},{40,48},{48,56},{56,64},{64,7... | collective-permute-start | bytes 49160 | tf_op jit(solution)/shard_map/ppermute | solution.py:18
  350.8 8.7 %collective-permute-start.34 = (bf16[1,4,26,1,128]{4,3,2,1,0:T(2,128)(2,1)S(1)}, bf16[1,4,26,1,128]{4,3,2,1,0:T(2,128)(2,1)S(1)}, u32[]{:S(2)}, u32[]{:S(2)}) collective-permute-start(bf16[1,4,26,1,128]{4,3,2,1,0:T(2,128)(2,1)S(1)} %get-tuple-element.64), channel_id=1, source_target_pairs={{0,1},{1,2},{2,3},{3,4},{4,5},{5,6},{6,7},{8,9},{9,10},{10,11},{11... | collective-permute-start | bytes 79880 | tf_op jit(solution)/shard_map/ppermute | solution.py:18
  376.0 8.7 %collective-permute-start.36 = (bf16[1,4,1,16,128]{4,3,2,1,0:T(8,128)(2,1)S(1)}, bf16[1,4,1,16,128]{4,3,2,1,0:T(8,128)(2,1)S(1)}, u32[]{:S(2)}, u32[]{:S(2)}) collective-permute-start(bf16[1,4,1,16,128]{4,3,2,1,0:T(8,128)(2,1)S(1)} %get-tuple-element.80), channel_id=1, source_target_pairs={{0,8},{8,16},{16,24},{24,32},{32,40},{40,48},{48,56},{56,64},{64,7... | collective-permute-start | bytes 49160 | tf_op jit(solution)/shard_map/ppermute | solution.py:18
  (60 other events, 234.2 us)
where the time goes:
time: 412 us; the launch traced here: 404 us
  starting transfers between devices  132 us (32%)
  matrix products  123 us (30%)
  waiting for transfers between devices  73.5 us (18%)
  local copies, waits for them, and re-layouts  61.6 us (15%)
  other arithmetic  10.3 us (2%)
    dot_general x270, matrix products, convolve(): jnp.einsum(form, piece, taps[depth, row_tap, col_tap], preferred_element_...  117 us
    ppermute x20, starting transfers between devices, padded_2(): before = lax.ppermute(last, axis, up)  77.3 us
    ppermute x20, waiting for transfers between devices, padded_2(): before = lax.ppermute(last, axis, up)  57.4 us
    ppermute x20, starting transfers between devices, padded_2(): after = lax.ppermute(leading, axis, down)  54.2 us
    another operation x65, local copies, waits for them, and re-layouts  38.5 us
    unnamed x92, local copies, waits for them, and re-layouts  20.2 us
    ppermute x20, waiting for transfers between devices, padded_2(): after = lax.ppermute(leading, axis, down)  16.1 us
  transfers between devices with their start and end apart: 40, of which 20 were waited for; matrix products, arithmetic and copies ran while one was open for 4% of the time, Pallas kernels for 0%

commit v1 on v0

v1 whole, which is shorter than its diff:
```python
import jax
import jax.numpy as jnp
import numpy as np
from jax import lax
from jax.experimental import pallas as pl
from jax.experimental.pallas import tpu as pltpu
from jax.sharding import PartitionSpec as P

F32 = jnp.float32
BF16 = jnp.bfloat16

HALO = 10
ROWS, COLS = 24, 16
TALL = 48
SHORT = 32
WIDE = COLS + 2 * HALO
HIGH = ROWS + 2 * HALO
PAD = 64


def width(h):
    return COLS + 2 * h


def sigmoid(v):
    return 0.5 * jnp.tanh(0.5 * v) + 0.5


def silu(v):
    return v * sigmoid(v)


def dsilu(v):
    s = sigmoid(v)
    return s * (1.0 + v * (1.0 - s))


def pair_weights(k):
    k = jnp.transpose(k, (0, 2, 1, 3, 4))
    zero = jnp.zeros_like(k[0])
    far = jnp.stack([jnp.stack([k[0], zero], 3), jnp.stack([k[1], k[0]], 3)], 2)
    near = jnp.stack([jnp.stack([k[2], k[1]], 3), jnp.stack([zero, k[2]], 3)], 2)
    ci, co = k.shape[-2:]
    return jnp.concatenate([far.reshape(9 * 2 * ci, 2 * co), near.reshape(9 * 2 * ci, 2 * co)], 0)


def pair_weights_back(k):
    k = jnp.transpose(jnp.flip(k, (1, 2)), (0, 2, 1, 4, 3))
    zero = jnp.zeros_like(k[0])
    far = jnp.stack([jnp.stack([k[0], k[1]], 3), jnp.stack([zero, k[0]], 3)], 2)
    near = jnp.stack([jnp.stack([k[2], zero], 3), jnp.stack([k[1], k[2]], 3)], 2)
    ci, co = k.shape[-2:]
    return jnp.concatenate([far.reshape(9 * 2 * ci, 2 * co), near.reshape(9 * 2 * ci, 2 * co)], 0)


def frame_blocks(k, back):
    zero = jnp.zeros_like(k[0])

    def tap(i, o):
        d = o - i if not back else i - o
        return k[2 - d] if 0 <= d <= 2 else zero

    return jnp.stack([jnp.stack([tap(i, o) for o in range(4)]) for i in range(4)])


def fold_last(k, back):
    if back:
        k = jnp.swapaxes(jnp.flip(k, (1, 2)), 3, 4)
    b = frame_blocks(jnp.swapaxes(k, 1, 2), back)
    b = jnp.transpose(b, (0, 4, 2, 3, 1, 5))
    b = b.reshape(b.shape[0] * b.shape[1], -1)
    return jnp.pad(b, ((0, 0), (0, 128 - b.shape[1])))


def fold_first(k, back):
    if back:
        k = jnp.swapaxes(jnp.flip(k, (1, 2)), 3, 4)
    b = frame_blocks(jnp.swapaxes(k, 1, 2), back)
    b = jnp.transpose(b, (2, 3, 0, 4, 1, 5))
    b = b.reshape(-1, b.shape[-2] * b.shape[-1])
    return jnp.pad(b, ((0, 128 - b.shape[0]), (0, 0)))


def second_weights(k):
    b = frame_blocks(jnp.swapaxes(k, 1, 2), False)
    b = jnp.transpose(b, (2, 3, 0, 4, 1, 5))
    low = b[:, :, :2, :, :2].reshape(9 * 128, 256)
    high = b[:, :, :, :, 2:].reshape(9 * 256, 256)
    return jnp.concatenate([low, high], 0)


def second_weights_back(k):
    k = jnp.swapaxes(jnp.flip(k, (1, 2)), 3, 4)
    b = frame_blocks(jnp.swapaxes(k, 1, 2), True)
    b = jnp.transpose(b, (2, 3, 0, 4, 1, 5))
    return b.reshape(9 * 512, 256)


def kernel(
    x_ref, w1_hbm, w2_hbm, rgb_w, one_w, sec_hbm, head, secb_hbm, oneb_w, rgbb_w, w2b_hbm, w1b_hbm,
    out_ref, logit_ref,
    field, pre1, pre2, pref, taps, valid, valid_s, part, pix, w1, w2, sec, secb, w2b, w1b, sems,
):
    loads = [
        pltpu.make_async_copy(a, b, sems.at[n])
        for n, (a, b) in enumerate(
            [(w1_hbm, w1), (w2_hbm, w2), (sec_hbm, sec), (secb_hbm, secb), (w2b_hbm, w2b), (w1b_hbm, w1b)]
        )
    ]
    for c in loads:
        c.start()
    gy, gx = lax.axis_index("gy"), lax.axis_index("gx")
    ny, nx = lax.axis_size("gy"), lax.axis_size("gx")

    def validity(ref, stride, h):
        first_x, first_y = gx * COLS - h, gy * ROWS - h
        y = first_y + lax.broadcasted_iota(jnp.int32, (stride, 128), 0)
        good_y = jnp.where((y >= 0) & (y < ny * ROWS), 1.0, 0.0).astype(F32)

        def body(x, _):
            place = first_x + x
            good_x = jnp.where((place >= 0) & (place < nx * COLS), 1.0, 0.0).astype(F32)
            ref[pl.ds(pl.multiple_of(x * stride, 8), stride), :] = good_y * good_x
            return 0

        lax.fori_loop(0, width(h), body, 0)

    validity(valid, TALL, HALO)
    validity(valid_s, SHORT, 2)

    def spread(count, stride, tiles, mask=None):
        step = 96

        def body(n, _):
            r = pl.multiple_of(n * step, 32)
            for j in range(3):
                good = None if mask is None else mask[pl.ds(r + j, step), :] > 0
                for t in range(tiles):
                    v = field[t, pl.ds(r + j, step), :]
                    if good is not None:
                        v = jnp.where(good, v, 0.0)
                    taps[j, pl.ds(r, step), t * 128 : t * 128 + 128] = v.astype(BF16)
            return 0

        lax.fori_loop(0, -(-count * stride // step), body, 0)

    def operand(base, rows, stride, tiles):
        return jnp.concatenate(
            [
                taps[j, pl.ds(pl.multiple_of(base + l * stride, 16), rows), tiles[0] * 128 : tiles[1] * 128]
                for l in range(3)
                for j in range(3)
            ],
            1,
        )

    def dot(a, b):
        return jnp.dot(a, b, preferred_element_type=F32)

    for t in range(4):
        def body(y, _, t=t):
            field[t, pl.ds(y, WIDE, TALL), :] = x_ref[t, y].astype(F32)
            return 0

        lax.fori_loop(0, HIGH, body, 0)
    spread(WIDE, TALL, 4, valid)

    def decode(w, pre, h, columns):
        rows = columns * TALL
        off = (HALO - h) * (TALL + 1)

        def body(n, _):
            base = pl.multiple_of(n * rows, 16)
            good = valid[pl.ds(base + off, rows), :] > 0
            near, far = operand(base, rows, TALL, (0, 2)), operand(base, rows, TALL, (2, 4))
            low = dot(near, w[2304:])
            high = dot(near, w[:2304]) + dot(far, w[2304:])
            for t, (v, s) in enumerate(((low, 0), (low, 128), (high, 0), (high, 128))):
                v = v[:, s : s + 128]
                pre[t, pl.ds(base, rows), :] = v
                field[t, pl.ds(base, rows), :] = jnp.where(good, silu(v), 0.0)
            return 0

        lax.fori_loop(0, width(h) // columns, body, 0)

    loads[0].wait()
    decode(w1, pre1, 9, 17)
    spread(width(9), TALL, 4)
    loads[1].wait()
    decode(w2, pre2, 8, 16)

    def gather_taps(count, h):
        off = (HALO - h) * (TALL + 1)
        lane = lax.broadcasted_iota(jnp.int32, (TALL, 128), 1)

        def rows(x, _):
            base = pl.multiple_of(x * TALL, 8)
            total = None
            for l in range(3):
                q = None
                for j in range(3):
                    v = part[pl.ds(base + l * TALL + j, TALL), :]
                    v = pltpu.roll(v, (128 - 12 * j) % 128, 1) if j else v
                    q = v if q is None else q + v
                q = pltpu.roll(q, (128 - 36 * l) % 128, 1) if l else q
                total = q if total is None else total + q
            good = (valid[pl.ds(base + off, TALL), :] > 0) & (lane < 12)
            pix[pl.ds(base, TALL), :] = jnp.where(good, total, 0.0).astype(BF16).astype(F32)
            return 0

        lax.fori_loop(0, count, rows, 0)

    def scatter_taps(count, stride):
        def rows(x, _):
            base = pl.multiple_of(x * TALL, 8)
            total = None
            for l in range(3):
                q = None
                for j in range(3):
                    v = pix[pl.ds(base + l * TALL + j, stride), :]
                    v = pltpu.roll(v, 12 * j, 1) if j else v
                    q = v if q is None else q + v
                q = pltpu.roll(q, 36 * l, 1) if l else q
                total = q if total is None else total + q
            taps[0, pl.ds(pl.multiple_of(x * stride, 16), stride), 0:128] = total.astype(BF16)
            return 0

        lax.fori_loop(0, count, rows, 0)

    def rgb_part(n, _):
        rows = 16 * TALL
        base = pl.multiple_of(n * rows, 16)
        a = jnp.concatenate([field[t, pl.ds(base, rows), :].astype(BF16) for t in range(4)], 1)
        part[pl.ds(base, rows), :] = dot(a, rgb_w[...])
        return 0

    lax.fori_loop(0, width(8) // 16, rgb_part, 0)
    gather_taps(width(7), 7)

    scatter_taps(width(6), TALL)

    def first(n, _):
        rows = 14 * TALL
        base = pl.multiple_of(n * rows, 16)
        good = valid[pl.ds(base + 4 * (TALL + 1), rows), :] > 0
        v = dot(taps[0, pl.ds(base, rows), 0:128], one_w[...])
        for t in range(2):
            p = v[:, t * 128 : t * 128 + 128]
            pref[t, pl.ds(base, rows), :] = p
            field[t, pl.ds(base, rows), :] = jnp.where(good, silu(p), 0.0)
        return 0

    lax.fori_loop(0, 2, first, 0)
    spread(width(6), TALL, 2)
    loads[2].wait()

    def second(n, _):
        rows = 13 * TALL
        base = pl.multiple_of(n * rows, 16)
        good = valid[pl.ds(base + 5 * (TALL + 1), rows), :] > 0
        low = dot(operand(base, rows, TALL, (0, 1)), sec[:1152])
        high = dot(operand(base, rows, TALL, (0, 2)), sec[1152:])
        lane = lax.broadcasted_iota(jnp.int32, (rows, 128), 1)
        logits = jnp.zeros((rows, 128), F32)
        for t, (v, s) in enumerate(((low, 0), (low, 128), (high, 0), (high, 128))):
            v = v[:, s : s + 128]
            sg = sigmoid(v)
            score = jnp.sum(v * sg * head[...], axis=1, keepdims=True)
            push = -sigmoid(-score)
            logits = jnp.where(lane == t, score, logits)
            g = push * head[...] * (sg * (1.0 + v * (1.0 - sg)))
            field[t, pl.ds(base, rows), :] = jnp.where(good, g, 0.0)
        part[pl.ds(base, rows), :] = logits
        return 0

    lax.fori_loop(0, 2, second, 0)
    for x in range(COLS):
        logit_ref[x] = part[pl.ds((x + 5) * TALL + 5, ROWS), :]
    spread(width(5), TALL, 4)
    loads[3].wait()

    def second_back(n, _):
        rows = 12 * TALL
        base = pl.multiple_of(n * rows, 16)
        good = valid[pl.ds(base + 6 * (TALL + 1), rows), :] > 0
        v = dot(operand(base, rows, TALL, (0, 4)), secb[...])
        g = []
        for t in range(2):
            p = pref[t, pl.ds(base + 2 * (TALL + 1), rows), :]
            g.append(jnp.where(good, v[:, t * 128 : t * 128 + 128] * dsilu(p), 0.0).astype(BF16))
        part[pl.ds(base, rows), :] = dot(jnp.concatenate(g, 1), oneb_w[...])
        return 0

    lax.fori_loop(0, 2, second_back, 0)
    gather_taps(width(3), 3)

    scatter_taps(width(2), SHORT)
    back = dot(taps[0, 0 : width(2) * SHORT, 0:128], rgbb_w[...])
    for t in range(4):
        for x in range(width(2)):
            p = pre2[t, pl.ds((x + 6) * TALL + 6, SHORT), :]
            g = back[x * SHORT : (x + 1) * SHORT, t * 128 : t * 128 + 128] * dsilu(p)
            good = valid_s[pl.ds(x * SHORT, SHORT), :] > 0
            field[t, pl.ds(x * SHORT, SHORT), :] = jnp.where(good, g, 0.0)
    spread(width(2), SHORT, 4)

    def back_conv(w, count):
        rows = count * SHORT
        near, far = operand(0, rows, SHORT, (0, 2)), operand(0, rows, SHORT, (2, 4))
        high = dot(far, w[2304:])
        low = dot(far, w[:2304]) + dot(near, w[2304:])
        return [v[:, s : s + 128] for v in (low, high) for s in (0, 128)]

    loads[4].wait()
    back = back_conv(w2b, width(1))
    for t in range(4):
        for x in range(width(1)):
            p = pre1[t, pl.ds((x + 8) * TALL + 8, SHORT), :]
            g = back[t][x * SHORT : (x + 1) * SHORT] * dsilu(p)
            good = valid_s[pl.ds((x + 1) * SHORT + 1, SHORT), :] > 0
            field[t, pl.ds(x * SHORT, SHORT), :] = jnp.where(good, g, 0.0)
    spread(width(1), SHORT, 4)
    loads[5].wait()
    back = back_conv(w1b, width(0))
    for t in range(4):
        field[t, 0 : COLS * SHORT, :] = back[t]
    for t in range(4):
        for y in range(ROWS):
            out_ref[t, y] = field[t, pl.ds(y, COLS, SHORT), :].astype(BF16)


def per_device(latent, conv_one, conv_two, to_rgb, disc_one, disc_two, disc_head):
    x = latent[0]

    def widen(v, axis, dim):
        n = lax.axis_size(axis)
        size = v.shape[dim]
        before = lax.ppermute(
            lax.slice_in_dim(v, size - HALO, size, axis=dim), axis, [(i, (i + 1) % n) for i in range(n)]
        )
        after = lax.ppermute(
            lax.slice_in_dim(v, 0, HALO, axis=dim), axis, [((i + 1) % n, i) for i in range(n)]
        )
        return jnp.concatenate([before, v, after], dim)

    x = widen(x, "gx", 2)
    x = widen(x, "gy", 1)
    weights = (
        pair_weights(conv_one),
        pair_weights(conv_two),
        fold_last(to_rgb, False),
        fold_first(disc_one, False),
        second_weights(disc_two),
        disc_head.reshape(1, 128),
        second_weights_back(disc_two),
        fold_last(disc_one, True),
        fold_first(to_rgb, True),
        pair_weights_back(conv_two),
        pair_weights_back(conv_one),
    )
    vmem = pl.BlockSpec(memory_space=pltpu.VMEM)
    hbm = pl.BlockSpec(memory_space=pl.ANY)
    p = WIDE * TALL + PAD
    out, logits = pl.pallas_call(
        kernel,
        out_shape=[
            jax.ShapeDtypeStruct((4, ROWS, COLS, 128), BF16),
            jax.ShapeDtypeStruct((COLS, ROWS, 128), F32),
        ],
        in_specs=[vmem, hbm, hbm, vmem, vmem, hbm, vmem, hbm, vmem, vmem, hbm, hbm],
        out_specs=[vmem, vmem],
        scratch_shapes=[
            pltpu.VMEM((4, p, 128), F32),
            pltpu.VMEM((4, p, 128), F32),
            pltpu.VMEM((4, p, 128), F32),
            pltpu.VMEM((2, p, 128), F32),
            pltpu.VMEM((3, p, 512), BF16),
            pltpu.VMEM((p, 128), F32),
            pltpu.VMEM((p, 128), F32),
            pltpu.VMEM((p, 128), F32),
            pltpu.VMEM((p, 128), F32),
        ]
        + [pltpu.VMEM(weights[n].shape, BF16) for n in (0, 1, 4, 6, 9, 10)]
        + [pltpu.SemaphoreType.DMA((6,))],
        compiler_params=pltpu.CompilerParams(vmem_limit_bytes=56 << 20),
    )(x, *weights)
    logits = jnp.transpose(logits[:, :, :4], (2, 1, 0)).astype(BF16)
    return out[None], logits[None]


def solution(mesh):
    placed = (P(None, None, "gy", "gx", None), P(), P(), P(), P(), P(), P())
    return jax.shard_map(
        per_device,
        mesh=mesh,
        in_specs=placed,
        out_specs=(P(None, None, "gy", "gx", None), P(None, None, "gy", "gx")),
        check_vma=False,
    )
```

time: 412 us -> 165 us (0.40)
  the two profiles are of different devices: /device:TPU:112 before, /device:TPU:0 now
where the time goes in v1:
time: 165 us; the launch traced here: 163 us
  local copies, waits for them, and re-layouts  67.1 us (41%)
  Pallas kernels  54 us (33%)
  other arithmetic  22 us (13%)
  waiting for transfers between devices  9.65 us (6%)
  starting transfers between devices  9.46 us (6%)
    pallas_call x1, Pallas kernels, per_device(): pl.pallas_call(kernel, out_shape=[jax.ShapeDtypeStruct((4, ROWS, COLS, 12...  54 us
    unnamed x95, local copies, waits for them, and re-layouts  13.8 us
    reshape x2, local copies, waits for them, and re-layouts, second_weights_back(): return b.reshape(9 * 512, 256)  13.4 us
    ppermute x2, starting transfers between devices, widen(): lax.ppermute(lax.slice_in_dim(v, 0, HALO, axis=dim), axis, [((i + 1) % n,...  9.46 us
    another operation x4, local copies, waits for them, and re-layouts, pair_weights_back(): far = jnp.stack([jnp.stack([k[0], k[1]], 3), jnp.stack([zero, k[0]], 3)], 2)  7.21 us
    another operation x2, local copies, waits for them, and re-layouts, pair_weights_back(): jnp.stack([jnp.stack([k[2], zero], 3), jnp.stack([k[1], k[2]], 3)], 2)  7.1 us
    ppermute x2, waiting for transfers between devices, widen(): lax.ppermute(lax.slice_in_dim(v, size - HALO, size, axis=dim), axis, [(i,...  5.52 us
    ppermute x2, waiting for transfers between devices, widen(): lax.ppermute(lax.slice_in_dim(v, 0, HALO, axis=dim), axis, [((i + 1) % n,...  4.12 us
  transfers between devices with their start and end apart: 4, of which 2 were waited for; matrix products, arithmetic and copies ran while one was open for 46% of the time, Pallas kernels for 0%

profile of v1, /device:TPU:0, one launch (start us, length us, event | category | flops | bytes accessed | tf_op | source)
XLA Modules:
  0.0 163.5 jit_solution(8417632288913273438)
XLA Ops:
  0.7 2.2 %fusion.17 = (bf16[4,24,10,128]{3,2,1,0:T(8,128)(2,1)}, bf16[4,24,10,128]{3,2,1,0:T(8,128)(2,1)}) fusion(bf16[4,24,16,128]{3,2,1,0:T(8,128)(2,1)} %bitcast.203), kind=kLoop, calls=%fused_computation.108 | loop fusion | bytes 983040 | tf_op jit(solution)/shard_map/slice | solution.py:339
  2.9 5.1 %collective-permute-start.1 = (bf16[4,24,10,128]{3,2,1,0:T(8,128)(2,1)}, bf16[4,24,10,128]{3,2,1,0:T(8,128)(2,1)}, u32[]{:S(2)}, u32[]{:S(2)}) collective-permute-start(bf16[4,24,10,128]{3,2,1,0:T(8,128)(2,1)} %get-tuple-element.36), channel_id=1, source_target_pairs={{1,0},{2,1},{3,2},{4,3},{5,4},{6,5},{7,6},{0,7},{9,8},{10,9},{11,1... | collective-permute-start | bytes 737288 | tf_op jit(solution)/shard_map/ppermute | solution.py:341
  24.6 1.6 pad_maximum_fusion.10
  26.2 3.5 %copy.39 = bf16[3,3,2,128,2,128]{5,4,3,2,1,0:T(2,128)(2,1)S(1)} copy(bf16[3,3,2,128,2,128]{3,5,0,1,4,2:T(8,128)(2,1)} %get-tuple-element.83) | data formatting | bytes 2359296 | tf_op jit(solution)/shard_map/stack | solution.py:51
  31.0 3.5 %copy.38 = bf16[3,3,2,128,2,128]{5,4,3,2,1,0:T(2,128)(2,1)S(1)} copy(bf16[3,3,2,128,2,128]{3,5,0,1,4,2:T(8,128)(2,1)} %get-tuple-element.82) | data formatting | bytes 2359296 | tf_op jit(solution)/shard_map/stack | solution.py:50
  36.1 1.6 pad_maximum_fusion.12
  37.8 3.5 %copy.41 = bf16[3,3,2,128,2,128]{5,4,3,2,1,0:T(2,128)(2,1)S(1)} copy(bf16[3,3,2,128,2,128]{3,5,0,1,4,2:T(8,128)(2,1)} %get-tuple-element.85) | data formatting | bytes 2359296 | tf_op jit(solution)/shard_map/stack | solution.py:51
  42.5 3.5 %copy.40 = bf16[3,3,2,128,2,128]{5,4,3,2,1,0:T(2,128)(2,1)S(1)} copy(bf16[3,3,2,128,2,128]{3,5,0,1,4,2:T(8,128)(2,1)} %get-tuple-element.84) | data formatting | bytes 2359296 | tf_op jit(solution)/shard_map/stack | solution.py:50
  46.2 1.6 pad_maximum_fusion.w1_hbm
  48.7 1.6 pad_maximum_fusion.1.w2_hbm
  51.2 1.6 pad_maximum_fusion.2.w2b_hbm
  52.9 1.5 pad_maximum_fusion.3.w1b_hbm
  61.8 1.7 %copy.30 = bf16[512,108]{1,0:T(8,128)(2,1)} copy(bf16[512,108]{0,1:T(8,128)(2,1)} %bitcast.232) | data formatting | bytes 221184 | tf_op jit(solution)/shard_map/reshape | solution.py:71
  63.5 1.6 pad.33.rgb_w
  65.1 1.6 copy.31
  66.7 1.6 %reshape.57 = bf16[108,256]{1,0:T(8,128)(2,1)} reshape(bf16[3,3,4,3,4,64]{5,4,3,2,1,0:T(4,128)(2,1)} %copy.31) | data formatting | bytes 110592 | tf_op jit(solution)/shard_map/reshape | solution.py:80
  72.7 5.5 %copy.44 = bf16[3,3,4,128,4,64]{5,4,3,2,1,0:T(4,128)(2,1)} copy(bf16[3,3,4,128,4,64]{3,5,0,1,4,2:T(8,128)(2,1)S(1)} %maximum_bitcast_fusion.1) | data formatting | bytes 4718592 | tf_op jit(solution)/shard_map/reshape | solution.py:96
  78.2 7.9 %reshape.68.secb_hbm = bf16[4608,256]{1,0:T(8,128)(2,1)} reshape(bf16[3,3,4,128,4,64]{5,4,3,2,1,0:T(4,128)(2,1)} %copy.44) | data formatting | bytes 4718592 | tf_op jit(solution)/shard_map/reshape | solution.py:96
  88.1 1.5 pad_maximum_fusion.18
  89.6 4.3 %collective-permute-start.3 = (bf16[4,10,36,128]{3,2,1,0:T(8,128)(2,1)S(1)}, bf16[4,10,36,128]{3,2,1,0:T(8,128)(2,1)S(1)}, u32[]{:S(2)}, u32[]{:S(2)}) collective-permute-start(bf16[4,10,36,128]{3,2,1,0:T(8,128)(2,1)S(1)} %get-tuple-element.11), channel_id=1, source_target_pairs={{8,0},{16,8},{24,16},{32,24},{40,32},{48,40},{56,48},{64,56},{72,6... | collective-permute-start | bytes 1105928 | tf_op jit(solution)/shard_map/ppermute | solution.py:341
  95.3 4.1 %collective-permute-done.3 = bf16[4,10,36,128]{3,2,1,0:T(8,128)(2,1)S(1)} collective-permute-done((bf16[4,10,36,128]{3,2,1,0:T(8,128)(2,1)S(1)}, bf16[4,10,36,128]{3,2,1,0:T(8,128)(2,1)S(1)}, u32[]{:S(2)}, u32[]{:S(2)}) %collective-permute-start.3) | collective-permute-done | bytes 368672 | tf_op jit(solution)/shard_map/ppermute | solution.py:341
  99.4 5.5 %collective-permute-done.2 = bf16[4,10,36,128]{3,2,1,0:T(8,128)(2,1)S(1)} collective-permute-done((bf16[4,10,36,128]{3,2,1,0:T(8,128)(2,1)S(1)}, bf16[4,10,36,128]{3,2,1,0:T(8,128)(2,1)S(1)}, u32[]{:S(2)}, u32[]{:S(2)}) %collective-permute-start.2) | collective-permute-done | bytes 368672 | tf_op jit(solution)/shard_map/ppermute | solution.py:338
  104.9 2.9 %pad_maximum_fusion.4.x_ref = bf16[4,44,36,128]{3,2,1,0:T(8,128)(2,1)} fusion(bf16[4,10,36,128]{3,2,1,0:T(8,128)(2,1)S(1)} %collective-permute-done.3, bf16[4,24,10,128]{3,2,1,0:T(8,128)(2,1)} %collective-permute-done.1, bf16[4,24,16,128]{3,2,1,0:T(8,128)(2,1)S(1)} %bitcast.205, bf16[4,24,10,128]{3,2,1,0:T(8,128)(2,1)} %collective-permute-done, ...), kind=kLoop, calls=%fused_computation.6 | loop fusion | flops 8110080 | bytes 3244032 | tf_op jit(solution)/shard_map/concatenate | solution.py:344
  107.8 54.0 %shard_map.86 = (bf16[4,24,16,128]{3,2,1,0:T(8,128)(2,1)}, f32[16,24,128]{2,1,0:T(8,128)}) custom-call(bf16[4,44,36,128]{3,2,1,0:T(8,128)(2,1)} %pad_maximum_fusion.4.x_ref, bf16[4608,256]{1,0:T(8,128)(2,1)} %pad_maximum_fusion.w1_hbm, bf16[4608,256]{1,0:T(8,128)(2,1)} %pad_maximum_fusion.1.w2_hbm, bf16[512,128]{1,0:T(8,128)(2,1)} %pad.33.rgb_w, ...), custom_call_target="tpu_custom_call" | custom-call | tf_op jit(solution)/shard_map/pallas_call | solution.py:364
  (171 shorter events, 38.9 us)
Async XLA Ops:
  0.6 7.4 %copy-start.18 = (bf16[3,3,3,64,128]{4,3,2,1,0:T(8,128)(2,1)S(1)}, bf16[3,3,3,64,128]{4,3,2,1,0:T(8,128)(2,1)}, u32[]{:S(2)}) copy-start(bf16[3,3,3,64,128]{4,3,2,1,0:T(8,128)(2,1)} %param.12) | copy-start | bytes 1327108
  0.6 7.4 %copy-start.34 = (bf16[3,3,3,3,64]{4,3,2,1,0:T(4,128)(2,1)S(1)}, bf16[3,3,3,3,64]{4,3,2,1,0:T(4,128)(2,1)}, u32[]{:S(2)}) copy-start(bf16[3,3,3,3,64]{4,3,2,1,0:T(4,128)(2,1)} %param.11) | copy-start | bytes 31108
  0.7 7.4 %copy-start.9 = (bf16[3,3,3,128,128]{4,3,2,1,0:T(8,128)(2,1)S(1)}, bf16[3,3,3,128,128]{4,3,2,1,0:T(8,128)(2,1)}, u32[]{:S(2)}) copy-start(bf16[3,3,3,128,128]{4,3,2,1,0:T(8,128)(2,1)} %param.8) | copy-start | bytes 2654212
  2.9 85.2 %collective-permute-start.1 = (bf16[4,24,10,128]{3,2,1,0:T(8,128)(2,1)}, bf16[4,24,10,128]{3,2,1,0:T(8,128)(2,1)}, u32[]{:S(2)}, u32[]{:S(2)}) collective-permute-start(bf16[4,24,10,128]{3,2,1,0:T(8,128)(2,1)} %get-tuple-element.36), channel_id=1, source_target_pairs={{1,0},{2,1},{3,2},{4,3},{5,4},{6,5},{7,6},{0,7},{9,8},{10,9},{11,1... | collective-permute-start | bytes 737288 | tf_op jit(solution)/shard_map/ppermute | solution.py:341
  8.0 80.1 %collective-permute-start = (bf16[4,24,10,128]{3,2,1,0:T(8,128)(2,1)}, bf16[4,24,10,128]{3,2,1,0:T(8,128)(2,1)}, u32[]{:S(2)}, u32[]{:S(2)}) collective-permute-start(bf16[4,24,10,128]{3,2,1,0:T(8,128)(2,1)} %get-tuple-element.35), channel_id=1, source_target_pairs={{0,1},{1,2},{2,3},{3,4},{4,5},{5,6},{6,7},{7,0},{8,9},{9,10},{10,1... | collective-permute-start | bytes 737288 | tf_op jit(solution)/shard_map/ppermute | solution.py:338
  16.7 3.4 %slice-start.2 = ((bf16[3,3,3,128,64]{3,4,1,2,0:T(8,128)(2,1)}), bf16[2,3,3,128,64]{3,4,1,2,0:T(8,128)(2,1)S(1)}, s32[]{:S(2)}) async-start(bf16[3,3,3,128,64]{3,4,1,2,0:T(8,128)(2,1)} %copy-done.7), calls=%async_computation.2 | async-start | bytes 589824 | tf_op jit(solution)/shard_map/slice | solution.py:61
  16.7 4.4 %copy-start.8 = (bf16[3,3,3,128,64]{3,4,1,2,0:T(8,128)(2,1)S(1)}, bf16[3,3,3,128,64]{3,4,1,2,0:T(8,128)(2,1)}, u32[]{:S(2)}) copy-start(bf16[3,3,3,128,64]{3,4,1,2,0:T(8,128)(2,1)} %copy-done.7) | copy-start | bytes 1327108
  16.7 4.4 %slice-start.1 = ((bf16[3,3,3,128,64]{3,4,1,2,0:T(8,128)(2,1)}), bf16[1,3,3,128,64]{3,4,1,2,0:T(8,128)(2,1)S(1)}, s32[]{:S(2)}) async-start(bf16[3,3,3,128,64]{3,4,1,2,0:T(8,128)(2,1)} %copy-done.7), calls=%async_computation.1 | async-start | bytes 294912 | tf_op jit(solution)/shard_map/slice | solution.py:61
  17.9 5.7 %copy-start.23 = (bf16[3,3,3,3,128]{4,3,1,2,0:T(4,128)(2,1)}, bf16[3,3,3,3,128]{4,3,1,2,0:T(4,128)(2,1)S(1)}, u32[]{:S(2)}) copy-start(bf16[3,3,3,3,128]{4,3,1,2,0:T(4,128)(2,1)S(1)} %reverse_bitcast_fusion.3) | copy-start | bytes 62212
  20.0 3.1 %slice-start.5 = ((bf16[3,3,3,64,3]{3,4,1,2,0:T(4,128)(2,1)}), bf16[2,3,3,64,3]{3,4,1,2,0:T(4,128)(2,1)S(1)}, s32[]{:S(2)}) async-start(bf16[3,3,3,64,3]{3,4,1,2,0:T(4,128)(2,1)} %copy-done.24), calls=%async_computation.5 | async-start | bytes 36864 | tf_op jit(solution)/shard_map/slice | solution.py:61
  48.7 2.5 %copy-start.5 = (bf16[288,8,2,128]{3,1,2,0:T(8,128)(2,1)S(1)}, bf16[288,8,2,128]{3,1,2,0:T(8,128)(2,1)}, u32[]{:S(2)}) copy-start(bf16[288,8,2,128]{3,1,2,0:T(8,128)(2,1)} %copy.71) | copy-start | bytes 3538948
  52.9 2.9 %copy-start.19 = (bf16[1,3,3,64,128]{4,3,1,2,0:T(8,128)(2,1)S(1)}, bf16[1,3,3,64,128]{4,3,1,2,0:T(8,128)(2,1)}, u32[]{:S(2)}) copy-start(bf16[1,3,3,64,128]{4,3,1,2,0:T(8,128)(2,1)} %get-tuple-element.28) | copy-start | bytes 442372
  52.9 2.9 %copy-start.20 = (bf16[1,3,3,64,128]{4,3,1,2,0:T(8,128)(2,1)S(1)}, bf16[1,3,3,64,128]{4,3,1,2,0:T(8,128)(2,1)}, u32[]{:S(2)}) copy-start(bf16[1,3,3,64,128]{4,3,1,2,0:T(8,128)(2,1)} %get-tuple-element.29) | copy-start | bytes 442372
  52.9 2.9 %copy-start.21 = (bf16[1,3,3,64,128]{4,3,1,2,0:T(8,128)(2,1)S(1)}, bf16[1,3,3,64,128]{4,3,1,2,0:T(8,128)(2,1)}, u32[]{:S(2)}) copy-start(bf16[1,3,3,64,128]{4,3,1,2,0:T(8,128)(2,1)} %get-tuple-element.30) | copy-start | bytes 442372
  56.5 3.7 %copy-start = (bf16[3,3,4,64,4,128]{5,3,0,1,4,2:T(8,128)(2,1)}, bf16[3,3,4,64,4,128]{5,3,0,1,4,2:T(8,128)(2,1)S(1)}, u32[]{:S(2)}) copy-start(bf16[3,3,4,64,4,128]{5,3,0,1,4,2:T(8,128)(2,1)S(1)} %maximum_bitcast_fusion) | copy-start | bytes 7077892
  61.1 8.7 %slice-start = ((bf16[3,3,4,64,4,128]{5,3,0,1,4,2:T(8,128)(2,1)}), bf16[3,3,4,64,2,128]{5,3,0,1,4,2:T(8,128)(2,1)S(1)}, s32[]{:S(2)}) async-start(bf16[3,3,4,64,4,128]{5,3,0,1,4,2:T(8,128)(2,1)} %copy-done), calls=%async_computation | async-start | bytes 2359296 | tf_op jit(solution)/shard_map/slice | solution.py:88
  78.2 7.9 %copy-start.22 = (bf16[4,64,3,3,4,3]{1,5,2,3,4,0:T(4,128)(2,1)S(1)}, bf16[4,64,3,3,4,3]{1,5,2,3,4,0:T(4,128)(2,1)}, u32[]{:S(2)}) copy-start(bf16[4,64,3,3,4,3]{1,5,2,3,4,0:T(4,128)(2,1)} %maximum_bitcast_fusion.15) | copy-start | bytes 165892
  78.2 8.9 %slice-start.3 = ((bf16[3,3,3,3,128]{4,3,1,2,0:T(4,128)(2,1)}), bf16[2,3,3,3,128]{4,3,1,2,0:T(4,128)(2,1)S(1)}, s32[]{:S(2)}) async-start(bf16[3,3,3,3,128]{4,3,1,2,0:T(4,128)(2,1)} %copy-done.23), calls=%async_computation.3 | async-start | bytes 36864 | tf_op jit(solution)/shard_map/slice | solution.py:61
  78.2 8.9 %copy-start.27 = (bf16[1,4,3,3,3,128]{5,4,2,3,1,0:T(4,128)(2,1)S(1)}, bf16[1,4,3,3,3,128]{5,4,2,3,1,0:T(4,128)(2,1)}, u32[]{:S(2)}) copy-start(bf16[1,4,3,3,3,128]{5,4,2,3,1,0:T(4,128)(2,1)} %get-tuple-element.57) | copy-start | bytes 82948
  78.2 8.9 %copy-start.28 = (bf16[1,4,3,3,3,128]{5,4,2,3,1,0:T(4,128)(2,1)S(1)}, bf16[1,4,3,3,3,128]{5,4,2,3,1,0:T(4,128)(2,1)}, u32[]{:S(2)}) copy-start(bf16[1,4,3,3,3,128]{5,4,2,3,1,0:T(4,128)(2,1)} %get-tuple-element.58) | copy-start | bytes 82948
  78.2 8.9 %copy-start.29 = (bf16[1,4,3,3,3,128]{5,4,2,3,1,0:T(4,128)(2,1)S(1)}, bf16[1,4,3,3,3,128]{5,4,2,3,1,0:T(4,128)(2,1)}, u32[]{:S(2)}) copy-start(bf16[1,4,3,3,3,128]{5,4,2,3,1,0:T(4,128)(2,1)} %get-tuple-element.81) | copy-start | bytes 82948
  86.3 7.6 %copy-start.16 = (bf16[144,8,2,128]{3,1,2,0:T(8,128)(2,1)S(1)}, bf16[144,8,2,128]{3,1,2,0:T(8,128)(2,1)}, u32[]{:S(2)}) copy-start(bf16[144,8,2,128]{3,1,2,0:T(8,128)(2,1)} %copy.77) | copy-start | bytes 1769476
  89.6 9.8 %collective-permute-start.3 = (bf16[4,10,36,128]{3,2,1,0:T(8,128)(2,1)S(1)}, bf16[4,10,36,128]{3,2,1,0:T(8,128)(2,1)S(1)}, u32[]{:S(2)}, u32[]{:S(2)}) collective-permute-start(bf16[4,10,36,128]{3,2,1,0:T(8,128)(2,1)S(1)} %get-tuple-element.11), channel_id=1, source_target_pairs={{8,0},{16,8},{24,16},{32,24},{40,32},{48,40},{56,48},{64,56},{72,6... | collective-permute-start | bytes 1105928 | tf_op jit(solution)/shard_map/ppermute | solution.py:341
  93.9 11.0 %collective-permute-start.2 = (bf16[4,10,36,128]{3,2,1,0:T(8,128)(2,1)S(1)}, bf16[4,10,36,128]{3,2,1,0:T(8,128)(2,1)S(1)}, u32[]{:S(2)}, u32[]{:S(2)}) collective-permute-start(bf16[4,10,36,128]{3,2,1,0:T(8,128)(2,1)S(1)} %get-tuple-element.10), channel_id=1, source_target_pairs={{0,8},{8,16},{16,24},{24,32},{32,40},{40,48},{48,56},{56,64},{64,7... | collective-permute-start | bytes 1105928 | tf_op jit(solution)/shard_map/ppermute | solution.py:338
  (26 other events, 41.8 us)

commit v2 on v1

v2 whole, which is shorter than its diff:
```python
import jax
import jax.numpy as jnp
import numpy as np
from jax import lax
from jax.experimental import pallas as pl
from jax.experimental.pallas import tpu as pltpu
from jax.sharding import PartitionSpec as P

F32 = jnp.float32
BF16 = jnp.bfloat16

HALO = 10
ROWS, COLS = 24, 16
TALL = 48
SHORT = 32
WIDE = COLS + 2 * HALO
HIGH = ROWS + 2 * HALO
PAD = 64


def width(h):
    return COLS + 2 * h


def sigmoid(v):
    return 0.5 * jnp.tanh(0.5 * v) + 0.5


def silu(v):
    return v * sigmoid(v)


def dsilu(v):
    s = sigmoid(v)
    return s * (1.0 + v * (1.0 - s))


def kernel(
    x_ref, k1, k2, ks, rgb_rows, one_rows, head,
    out_ref, logit_ref,
    field, pre1, pre2, pref, taps, valid, valid_s, part, pix, w1, w2, sec, small, rgb_w, one_w, sems,
):
    loads = []
    for n, (k, w) in enumerate(((k1, w1), (k2, w2))):
        for far in range(2):
            for f in range(2):
                for t in range(2):
                    i = f - t + 2 - 2 * far
                    block = w.at[far, :, f * 128 : f * 128 + 128, t * 128 : t * 128 + 128]
                    if 0 <= i <= 2:
                        loads.append((n, pltpu.make_async_copy(k.at[i], block, sems.at[len(loads)])))
                    else:
                        block[...] = jnp.zeros(block.shape, BF16)
    for f in range(4):
        for t in range(4):
            i = f - t + 2
            block = sec.at[:, f * 64 : f * 64 + 64, t * 128 : t * 128 + 128]
            if 0 <= i <= 2:
                loads.append((2, pltpu.make_async_copy(ks.at[i], block, sems.at[len(loads)])))
            else:
                block[...] = jnp.zeros(block.shape, BF16)
    for _, c in loads:
        c.start()

    def arrived(which):
        for n, c in loads:
            if n == which:
                c.wait()

    small[...] = jnp.zeros_like(small)
    for rows, out, lanes in ((rgb_rows, rgb_w, 128), (one_rows, one_w, 64)):
        for f in range(4):
            for t in range(4):
                i = (t - f if out is rgb_w else f - t) + 2
                if 0 <= i <= 2:
                    for n in range(9):
                        small[n * 12 + f * 3 : n * 12 + f * 3 + 3, t * lanes : t * lanes + lanes] = rows[
                            (i * 9 + n) * 3 : (i * 9 + n) * 3 + 3, 0:lanes
                        ]
        out[...] = small[:, 0 : 4 * lanes].astype(BF16)
        if out is rgb_w:
            small[...] = jnp.zeros_like(small)

    gy, gx = lax.axis_index("gy"), lax.axis_index("gx")
    ny, nx = lax.axis_size("gy"), lax.axis_size("gx")

    def validity(ref, stride, h):
        first_x, first_y = gx * COLS - h, gy * ROWS - h
        y = first_y + lax.broadcasted_iota(jnp.int32, (stride, 128), 0)
        good_y = jnp.where((y >= 0) & (y < ny * ROWS), 1.0, 0.0).astype(F32)

        def body(x, _):
            place = first_x + x
            good_x = jnp.where((place >= 0) & (place < nx * COLS), 1.0, 0.0).astype(F32)
            ref[pl.ds(pl.multiple_of(x * stride, 8), stride), :] = good_y * good_x
            return 0

        lax.fori_loop(0, width(h), body, 0)

    validity(valid, TALL, HALO)
    validity(valid_s, SHORT, 2)

    def spread(count, stride, tiles, mask=None):
        step = 96

        def body(n, _):
            r = pl.multiple_of(n * step, 32)
            for j in range(3):
                good = None if mask is None else mask[pl.ds(r + j, step), :] > 0
                for t in range(tiles):
                    v = field[t, pl.ds(r + j, step), :]
                    if good is not None:
                        v = jnp.where(good, v, 0.0)
                    taps[j, pl.ds(r, step), t * 128 : t * 128 + 128] = v.astype(BF16)
            return 0

        lax.fori_loop(0, -(-count * stride // step), body, 0)

    def operand(base, rows, stride, tiles):
        return jnp.concatenate(
            [
                taps[j, pl.ds(pl.multiple_of(base + l * stride, 16), rows), tiles[0] * 128 : tiles[1] * 128]
                for j in range(3)
                for l in range(3)
            ],
            1,
        )

    def stack(w, rows=slice(None), lanes=slice(None)):
        v = w[:, rows, lanes]
        return v.reshape(-1, v.shape[-1])

    def across(w):
        return jnp.concatenate([w[8 - n] for n in range(9)], 1)

    def dot_t(a, b):
        return lax.dot_general(a, b, (((1,), (1,)), ((), ())), preferred_element_type=F32)

    def dot(a, b):
        return jnp.dot(a, b, preferred_element_type=F32)

    for t in range(4):
        def body(y, _, t=t):
            field[t, pl.ds(y, WIDE, TALL), :] = x_ref[t, y].astype(F32)
            return 0

        lax.fori_loop(0, HIGH, body, 0)
    spread(WIDE, TALL, 4, valid)

    def decode(w, pre, h, columns):
        rows = columns * TALL
        off = (HALO - h) * (TALL + 1)

        def body(n, _):
            base = pl.multiple_of(n * rows, 16)
            good = valid[pl.ds(base + off, rows), :] > 0
            near, far = operand(base, rows, TALL, (0, 2)), operand(base, rows, TALL, (2, 4))
            low = dot(near, stack(w.at[0]))
            high = dot(near, stack(w.at[1])) + dot(far, stack(w.at[0]))
            for t, (v, s) in enumerate(((low, 0), (low, 128), (high, 0), (high, 128))):
                v = v[:, s : s + 128]
                pre[t, pl.ds(base, rows), :] = v
                field[t, pl.ds(base, rows), :] = jnp.where(good, silu(v), 0.0)
            return 0

        lax.fori_loop(0, width(h) // columns, body, 0)

    arrived(0)
    decode(w1, pre1, 9, 17)
    spread(width(9), TALL, 4)
    arrived(1)
    decode(w2, pre2, 8, 16)

    def gather_taps(count, h, flip):
        off = (HALO - h) * (TALL + 1)
        lane = lax.broadcasted_iota(jnp.int32, (TALL, 128), 1)

        def rows(x, _):
            base = pl.multiple_of(x * TALL, 8)
            total = None
            for j in range(3):
                q = None
                for l in range(3):
                    v = part[pl.ds(base + l * TALL + j, TALL), :]
                    group = 2 - l if flip else l
                    v = pltpu.roll(v, 128 - 12 * group, 1) if group else v
                    q = v if q is None else q + v
                group = 2 - j if flip else j
                q = pltpu.roll(q, 128 - 36 * group, 1) if group else q
                total = q if total is None else total + q
            good = (valid[pl.ds(base + off, TALL), :] > 0) & (lane < 12)
            pix[pl.ds(base, TALL), :] = jnp.where(good, total, 0.0).astype(BF16).astype(F32)
            return 0

        lax.fori_loop(0, count, rows, 0)

    def scatter_taps(count, stride, flip):
        def rows(x, _):
            base = pl.multiple_of(x * TALL, 8)
            total = None
            for j in range(3):
                q = None
                for l in range(3):
                    v = pix[pl.ds(base + l * TALL + j, stride), :]
                    group = 2 - l if flip else l
                    v = pltpu.roll(v, 12 * group, 1) if group else v
                    q = v if q is None else q + v
                group = 2 - j if flip else j
                q = pltpu.roll(q, 36 * group, 1) if group else q
                total = q if total is None else total + q
            taps[0, pl.ds(pl.multiple_of(x * stride, 16), stride), 0:128] = total.astype(BF16)
            return 0

        lax.fori_loop(0, count, rows, 0)

    def rgb_part(n, _):
        rows = 16 * TALL
        base = pl.multiple_of(n * rows, 16)
        a = jnp.concatenate([field[t, pl.ds(base, rows), :].astype(BF16) for t in range(4)], 1)
        part[pl.ds(base, rows), :] = dot_t(a, rgb_w[...])
        return 0

    lax.fori_loop(0, width(8) // 16, rgb_part, 0)
    gather_taps(width(7), 7, False)

    scatter_taps(width(6), TALL, False)

    def first(n, _):
        rows = 14 * TALL
        base = pl.multiple_of(n * rows, 16)
        good = valid[pl.ds(base + 4 * (TALL + 1), rows), :] > 0
        v = dot(taps[0, pl.ds(base, rows), 0:128], one_w[...])
        for t in range(2):
            p = v[:, t * 128 : t * 128 + 128]
            pref[t, pl.ds(base, rows), :] = p
            field[t, pl.ds(base, rows), :] = jnp.where(good, silu(p), 0.0)
        return 0

    lax.fori_loop(0, 2, first, 0)
    spread(width(6), TALL, 2)
    arrived(2)

    def second(n, _):
        rows = 13 * TALL
        base = pl.multiple_of(n * rows, 16)
        good = valid[pl.ds(base + 5 * (TALL + 1), rows), :] > 0
        low = dot(operand(base, rows, TALL, (0, 1)), stack(sec, slice(0, 128), slice(0, 256)))
        high = dot(operand(base, rows, TALL, (0, 2)), stack(sec, slice(None), slice(256, 512)))
        lane = lax.broadcasted_iota(jnp.int32, (rows, 128), 1)
        logits = jnp.zeros((rows, 128), F32)
        for t, (v, s) in enumerate(((low, 0), (low, 128), (high, 0), (high, 128))):
            v = v[:, s : s + 128]
            sg = sigmoid(v)
            score = jnp.sum(v * sg * head[...], axis=1, keepdims=True)
            push = -sigmoid(-score)
            logits = jnp.where(lane == t, score, logits)
            g = push * head[...] * (sg * (1.0 + v * (1.0 - sg)))
            field[t, pl.ds(base, rows), :] = jnp.where(good, g, 0.0)
        part[pl.ds(base, rows), :] = logits
        return 0

    lax.fori_loop(0, 2, second, 0)
    for x in range(COLS):
        logit_ref[x] = part[pl.ds((x + 5) * TALL + 5, ROWS), :]
    spread(width(5), TALL, 4)

    def second_back(n, _):
        rows = 12 * TALL
        base = pl.multiple_of(n * rows, 16)
        good = valid[pl.ds(base + 6 * (TALL + 1), rows), :] > 0
        v = dot_t(operand(base, rows, TALL, (0, 4)), across(sec))
        g = []
        for t in range(2):
            p = pref[t, pl.ds(base + 2 * (TALL + 1), rows), :]
            g.append(jnp.where(good, v[:, t * 128 : t * 128 + 128] * dsilu(p), 0.0).astype(BF16))
        part[pl.ds(base, rows), :] = dot_t(jnp.concatenate(g, 1), one_w[...])
        return 0

    lax.fori_loop(0, 2, second_back, 0)
    gather_taps(width(3), 3, True)

    scatter_taps(width(2), SHORT, True)
    back = dot(taps[0, 0 : width(2) * SHORT, 0:128], rgb_w[...])
    for t in range(4):
        for x in range(width(2)):
            p = pre2[t, pl.ds((x + 6) * TALL + 6, SHORT), :]
            g = back[x * SHORT : (x + 1) * SHORT, t * 128 : t * 128 + 128] * dsilu(p)
            good = valid_s[pl.ds(x * SHORT, SHORT), :] > 0
            field[t, pl.ds(x * SHORT, SHORT), :] = jnp.where(good, g, 0.0)
    spread(width(2), SHORT, 4)

    def back_conv(w, count):
        rows = count * SHORT
        near, far = operand(0, rows, SHORT, (0, 2)), operand(0, rows, SHORT, (2, 4))
        high = dot_t(far, across(w.at[0]))
        low = dot_t(far, across(w.at[1])) + dot_t(near, across(w.at[0]))
        return [v[:, s : s + 128] for v in (low, high) for s in (0, 128)]

    back = back_conv(w2, width(1))
    for t in range(4):
        for x in range(width(1)):
            p = pre1[t, pl.ds((x + 8) * TALL + 8, SHORT), :]
            g = back[t][x * SHORT : (x + 1) * SHORT] * dsilu(p)
            good = valid_s[pl.ds((x + 1) * SHORT + 1, SHORT), :] > 0
            field[t, pl.ds(x * SHORT, SHORT), :] = jnp.where(good, g, 0.0)
    spread(width(1), SHORT, 4)
    back = back_conv(w1, width(0))
    for t in range(4):
        field[t, 0 : COLS * SHORT, :] = back[t]
    for t in range(4):
        for y in range(ROWS):
            out_ref[t, y] = field[t, pl.ds(y, COLS, SHORT), :].astype(BF16)


def per_device(latent, conv_one, conv_two, to_rgb, disc_one, disc_two, disc_head):
    x = latent[0]

    def widen(v, axis, dim):
        n = lax.axis_size(axis)
        size = v.shape[dim]
        before = lax.ppermute(
            lax.slice_in_dim(v, size - HALO, size, axis=dim), axis, [(i, (i + 1) % n) for i in range(n)]
        )
        after = lax.ppermute(
            lax.slice_in_dim(v, 0, HALO, axis=dim), axis, [((i + 1) % n, i) for i in range(n)]
        )
        return jnp.concatenate([before, v, after], dim)

    x = widen(x, "gx", 2)
    x = widen(x, "gy", 1)
    taps = lambda k: k.reshape(3, 9, *k.shape[3:])
    rgb_rows = jnp.swapaxes(to_rgb, 3, 4).reshape(81, 128).astype(F32)
    one_rows = jnp.pad(disc_one.reshape(81, 64).astype(F32), ((0, 0), (0, 64)))
    vmem = pl.BlockSpec(memory_space=pltpu.VMEM)
    hbm = pl.BlockSpec(memory_space=pl.ANY)
    p = WIDE * TALL + PAD
    out, logits = pl.pallas_call(
        kernel,
        out_shape=[
            jax.ShapeDtypeStruct((4, ROWS, COLS, 128), BF16),
            jax.ShapeDtypeStruct((COLS, ROWS, 128), F32),
        ],
        in_specs=[vmem, hbm, hbm, hbm, vmem, vmem, vmem],
        out_specs=[vmem, vmem],
        scratch_shapes=[
            pltpu.VMEM((4, p, 128), F32),
            pltpu.VMEM((4, p, 128), F32),
            pltpu.VMEM((4, p, 128), F32),
            pltpu.VMEM((2, p, 128), F32),
            pltpu.VMEM((3, p, 512), BF16),
            pltpu.VMEM((p, 128), F32),
            pltpu.VMEM((p, 128), F32),
            pltpu.VMEM((p, 128), F32),
            pltpu.VMEM((p, 128), F32),
        ]
        + [
            pltpu.VMEM((2, 9, 256, 256), BF16),
            pltpu.VMEM((2, 9, 256, 256), BF16),
            pltpu.VMEM((9, 256, 512), BF16),
            pltpu.VMEM((128, 512), F32),
            pltpu.VMEM((128, 512), BF16),
            pltpu.VMEM((128, 256), BF16),
            pltpu.SemaphoreType.DMA((24,)),
        ],
        compiler_params=pltpu.CompilerParams(vmem_limit_bytes=56 << 20),
    )(x, taps(conv_one), taps(conv_two), taps(disc_two), rgb_rows, one_rows, disc_head.reshape(1, 128))
    logits = jnp.transpose(logits[:, :, :4], (2, 1, 0)).astype(BF16)
    return out[None], logits[None]


def solution(mesh):
    placed = (P(None, None, "gy", "gx", None), P(), P(), P(), P(), P(), P())
    return jax.shard_map(
        per_device,
        mesh=mesh,
        in_specs=placed,
        out_specs=(P(None, None, "gy", "gx", None), P(None, None, "gy", "gx")),
        check_vma=False,
    )
```

time: 165 us -> 89.2 us (0.54)
  the two profiles are of different devices: /device:TPU:0 before, /device:TPU:7 now
where the time goes in v2:
time: 89.2 us; the launch traced here: 89 us
  Pallas kernels  54.8 us (61%)
  waiting for transfers between devices  18.5 us (21%)
  starting transfers between devices  8.64 us (10%)
  local copies, waits for them, and re-layouts  3.73 us (4%)
  other arithmetic  2.67 us (3%)
    pallas_call x1, Pallas kernels, per_device(): pl.pallas_call(kernel, out_shape=[jax.ShapeDtypeStruct((4, ROWS, COLS, 12...  54.8 us
    ppermute x2, waiting for transfers between devices, widen(): lax.ppermute(lax.slice_in_dim(v, size - HALO, size, axis=dim), axis, [(i,...  12.4 us
    ppermute x2, waiting for transfers between devices, widen(): lax.ppermute(lax.slice_in_dim(v, 0, HALO, axis=dim), axis, [((i + 1) % n,...  6.1 us
    ppermute x2, starting transfers between devices, widen(): lax.ppermute(lax.slice_in_dim(v, size - HALO, size, axis=dim), axis, [(i,...  5.42 us
    ppermute x2, starting transfers between devices, widen(): lax.ppermute(lax.slice_in_dim(v, 0, HALO, axis=dim), axis, [((i + 1) % n,...  3.22 us
  transfers between devices with their start and end apart: 4, of which 3 were waited for; matrix products, arithmetic and copies ran while one was open for 1% of the time, Pallas kernels for 0%

profile of v2, /device:TPU:7, one launch (start us, length us, event | category | flops | bytes accessed | tf_op | source)
XLA Modules:
  0.0 89.0 jit_solution(18355258427939337364)
XLA Ops:
  0.6 0.0 copy-start
  0.6 0.0 copy-start.2
  0.6 0.0 copy-start.1
  0.7 1.3 %fusion.1 = (bf16[4,24,10,128]{3,2,1,0:T(8,128)(2,1)S(1)}, bf16[4,24,10,128]{3,2,1,0:T(8,128)(2,1)S(1)}) fusion(bf16[4,24,16,128]{3,2,1,0:T(8,128)(2,1)} %bitcast.12), kind=kLoop, calls=%fused_computation.8 | loop fusion | bytes 983040 | tf_op jit(solution)/shard_map/slice | solution.py:322
  2.0 1.7 %collective-permute-start = (bf16[4,24,10,128]{3,2,1,0:T(8,128)(2,1)S(1)}, bf16[4,24,10,128]{3,2,1,0:T(8,128)(2,1)S(1)}, u32[]{:S(2)}, u32[]{:S(2)}) collective-permute-start(bf16[4,24,10,128]{3,2,1,0:T(8,128)(2,1)S(1)} %get-tuple-element.12), channel_id=1, source_target_pairs={{0,1},{1,2},{2,3},{3,4},{4,5},{5,6},{6,7},{7,0},{8,9},{9,10},{10,1... | collective-permute-start | bytes 737288 | tf_op jit(solution)/shard_map/ppermute | solution.py:321
  3.7 3.2 %collective-permute-start.1 = (bf16[4,24,10,128]{3,2,1,0:T(8,128)(2,1)S(1)}, bf16[4,24,10,128]{3,2,1,0:T(8,128)(2,1)S(1)}, u32[]{:S(2)}, u32[]{:S(2)}) collective-permute-start(bf16[4,24,10,128]{3,2,1,0:T(8,128)(2,1)S(1)} %get-tuple-element.13), channel_id=1, source_target_pairs={{1,0},{2,1},{3,2},{4,3},{5,4},{6,5},{7,6},{0,7},{9,8},{10,9},{11,1... | collective-permute-start | bytes 737288 | tf_op jit(solution)/shard_map/ppermute | solution.py:324
  6.9 8.8 %collective-permute-done = bf16[4,24,10,128]{3,2,1,0:T(8,128)(2,1)S(1)} collective-permute-done((bf16[4,24,10,128]{3,2,1,0:T(8,128)(2,1)S(1)}, bf16[4,24,10,128]{3,2,1,0:T(8,128)(2,1)S(1)}, u32[]{:S(2)}, u32[]{:S(2)}) %collective-permute-start) | collective-permute-done | bytes 245792 | tf_op jit(solution)/shard_map/ppermute | solution.py:321
  15.7 0.0 collective-permute-done.1
  15.7 0.0 copy-done
  15.7 0.3 pad_maximum_fusion.3
  16.0 3.7 %collective-permute-start.2 = (bf16[4,10,36,128]{3,2,1,0:T(8,128)(2,1)S(1)}, bf16[4,10,36,128]{3,2,1,0:T(8,128)(2,1)S(1)}, u32[]{:S(2)}, u32[]{:S(2)}) collective-permute-start(bf16[4,10,36,128]{3,2,1,0:T(8,128)(2,1)S(1)} %get-tuple-element.10), channel_id=1, source_target_pairs={{0,8},{8,16},{16,24},{24,32},{32,40},{40,48},{48,56},{56,64},{64,7... | collective-permute-start | bytes 1105928 | tf_op jit(solution)/shard_map/ppermute | solution.py:321
  19.7 0.0 collective-permute-start.3
  19.7 0.0 copy-done.2
  19.7 0.6 reshape.26.rgb_rows
  20.4 0.0 copy-done.1
  20.4 0.6 pad_convert_fusion.one_rows
  21.0 3.6 %collective-permute-done.2 = bf16[4,10,36,128]{3,2,1,0:T(8,128)(2,1)S(1)} collective-permute-done((bf16[4,10,36,128]{3,2,1,0:T(8,128)(2,1)S(1)}, bf16[4,10,36,128]{3,2,1,0:T(8,128)(2,1)S(1)}, u32[]{:S(2)}, u32[]{:S(2)}) %collective-permute-start.2) | collective-permute-done | bytes 368672 | tf_op jit(solution)/shard_map/ppermute | solution.py:321
  24.6 6.1 %collective-permute-done.3 = bf16[4,10,36,128]{3,2,1,0:T(8,128)(2,1)S(1)} collective-permute-done((bf16[4,10,36,128]{3,2,1,0:T(8,128)(2,1)S(1)}, bf16[4,10,36,128]{3,2,1,0:T(8,128)(2,1)S(1)}, u32[]{:S(2)}, u32[]{:S(2)}) %collective-permute-start.3) | collective-permute-done | bytes 368672 | tf_op jit(solution)/shard_map/ppermute | solution.py:324
  30.7 1.7 %pad_maximum_fusion.x_ref = bf16[4,44,36,128]{3,2,1,0:T(8,128)(2,1)} fusion(bf16[4,10,36,128]{3,2,1,0:T(8,128)(2,1)S(1)} %collective-permute-done.3, bf16[4,24,10,128]{3,2,1,0:T(8,128)(2,1)S(1)} %collective-permute-done.1, bf16[4,24,16,128]{3,2,1,0:T(8,128)(2,1)S(1)} %bitcast.14, bf16[4,24,10,128]{3,2,1,0:T(8,128)(2,1)S(1)} %collective-permute-done, ...), kind=kLoop, calls=%fused_computation | loop fusion | flops 8110080 | bytes 3244032 | tf_op jit(solution)/shard_map/concatenate | solution.py:327
  32.4 54.8 %shard_map.86 = (bf16[4,24,16,128]{3,2,1,0:T(8,128)(2,1)}, f32[16,24,128]{2,1,0:T(8,128)}) custom-call(bf16[4,44,36,128]{3,2,1,0:T(8,128)(2,1)} %pad_maximum_fusion.x_ref, bf16[3,9,128,128]{3,2,1,0:T(8,128)(2,1)} %bitcast.15, bf16[3,9,128,128]{3,2,1,0:T(8,128)(2,1)} %bitcast.16, bf16[3,9,64,128]{3,2,1,0:T(8,128)(2,1)} %bitcast.17, ...), custom_call_target="tpu_custom_call" | custom-call | tf_op jit(solution)/shard_map/pallas_call | solution.py:337
  87.3 0.9 %fusion = bf16[1,4,24,16]{1,2,3,0:T(8,128)(2,1)S(1)} fusion(f32[16,24,128]{2,1,0:T(8,128)} %get-tuple-element.5), kind=kLoop, calls=%fused_computation.5 | loop fusion | bytes 6144 | tf_op jit(solution)/shard_map/broadcast_in_dim | solution.py:368
  88.2 0.8 copy.10
  (2 shorter events, 0.0 us)
Async XLA Ops:
  0.6 15.0 %copy-start = (bf16[1,4,24,16,128]{4,3,2,1,0:T(8,128)(2,1)S(1)}, bf16[1,4,24,16,128]{4,3,2,1,0:T(8,128)(2,1)}, u32[]{:S(2)}) copy-start(bf16[1,4,24,16,128]{4,3,2,1,0:T(8,128)(2,1)} %param.7) | copy-start | bytes 1179652
  0.6 19.1 %copy-start.2 = (bf16[3,3,3,128,3]{3,4,2,1,0:T(4,128)(2,1)S(1)}, bf16[3,3,3,128,3]{3,4,2,1,0:T(4,128)(2,1)}, u32[]{:S(2)}) copy-start(bf16[3,3,3,128,3]{3,4,2,1,0:T(4,128)(2,1)} %param.10) | copy-start | bytes 62212
  0.6 19.7 %copy-start.1 = (bf16[3,3,3,3,64]{4,3,2,1,0:T(4,128)(2,1)S(1)}, bf16[3,3,3,3,64]{4,3,2,1,0:T(4,128)(2,1)}, u32[]{:S(2)}) copy-start(bf16[3,3,3,3,64]{4,3,2,1,0:T(4,128)(2,1)} %param.11) | copy-start | bytes 31108
  2.0 13.7 %collective-permute-start = (bf16[4,24,10,128]{3,2,1,0:T(8,128)(2,1)S(1)}, bf16[4,24,10,128]{3,2,1,0:T(8,128)(2,1)S(1)}, u32[]{:S(2)}, u32[]{:S(2)}) collective-permute-start(bf16[4,24,10,128]{3,2,1,0:T(8,128)(2,1)S(1)} %get-tuple-element.12), channel_id=1, source_target_pairs={{0,1},{1,2},{2,3},{3,4},{4,5},{5,6},{6,7},{7,0},{8,9},{9,10},{10,1... | collective-permute-start | bytes 737288 | tf_op jit(solution)/shard_map/ppermute | solution.py:321
  3.7 12.0 %collective-permute-start.1 = (bf16[4,24,10,128]{3,2,1,0:T(8,128)(2,1)S(1)}, bf16[4,24,10,128]{3,2,1,0:T(8,128)(2,1)S(1)}, u32[]{:S(2)}, u32[]{:S(2)}) collective-permute-start(bf16[4,24,10,128]{3,2,1,0:T(8,128)(2,1)S(1)} %get-tuple-element.13), channel_id=1, source_target_pairs={{1,0},{2,1},{3,2},{4,3},{5,4},{6,5},{7,6},{0,7},{9,8},{10,9},{11,1... | collective-permute-start | bytes 737288 | tf_op jit(solution)/shard_map/ppermute | solution.py:324
  16.0 8.6 %collective-permute-start.2 = (bf16[4,10,36,128]{3,2,1,0:T(8,128)(2,1)S(1)}, bf16[4,10,36,128]{3,2,1,0:T(8,128)(2,1)S(1)}, u32[]{:S(2)}, u32[]{:S(2)}) collective-permute-start(bf16[4,10,36,128]{3,2,1,0:T(8,128)(2,1)S(1)} %get-tuple-element.10), channel_id=1, source_target_pairs={{0,8},{8,16},{16,24},{24,32},{32,40},{40,48},{48,56},{56,64},{64,7... | collective-permute-start | bytes 1105928 | tf_op jit(solution)/shard_map/ppermute | solution.py:321
  19.7 11.0 %collective-permute-start.3 = (bf16[4,10,36,128]{3,2,1,0:T(8,128)(2,1)S(1)}, bf16[4,10,36,128]{3,2,1,0:T(8,128)(2,1)S(1)}, u32[]{:S(2)}, u32[]{:S(2)}) collective-permute-start(bf16[4,10,36,128]{3,2,1,0:T(8,128)(2,1)S(1)} %get-tuple-element.11), channel_id=1, source_target_pairs={{8,0},{16,8},{24,16},{32,24},{40,32},{48,40},{56,48},{64,56},{72,6... | collective-permute-start | bytes 1105928 | tf_op jit(solution)/shard_map/ppermute | solution.py:324

commit v3 on v2

--- a/solution.py
+++ b/solution.py
@@ -15,7 +15,7 @@
 SHORT = 32
 WIDE = COLS + 2 * HALO
 HIGH = ROWS + 2 * HALO
-PAD = 64
+PAD = 256
 
 
 def width(h):
@@ -35,20 +35,16 @@
     return s * (1.0 + v * (1.0 - s))
 
 
-def kernel(
-    x_ref, k1, k2, ks, rgb_rows, one_rows, head,
-    out_ref, logit_ref,
-    field, pre1, pre2, pref, taps, valid, valid_s, part, pix, w1, w2, sec, small, rgb_w, one_w, sems,
-):
+def lay_out(k1, k2, ks, rgb_rows, one_rows, w1, w2, sec, rgb_w, one_w, small, sems):
     loads = []
-    for n, (k, w) in enumerate(((k1, w1), (k2, w2))):
+    for k, w in ((k1, w1), (k2, w2)):
         for far in range(2):
             for f in range(2):
                 for t in range(2):
                     i = f - t + 2 - 2 * far
                     block = w.at[far, :, f * 128 : f * 128 + 128, t * 128 : t * 128 + 128]
                     if 0 <= i <= 2:
-                        loads.append((n, pltpu.make_async_copy(k.at[i], block, sems.at[len(loads)])))
+                        loads.append(pltpu.make_async_copy(k.at[i], block, sems.at[len(loads)]))
                     else:
                         block[...] = jnp.zeros(block.shape, BF16)
     for f in range(4):
@@ -56,30 +52,41 @@
             i = f - t + 2
             block = sec.at[:, f * 64 : f * 64 + 64, t * 128 : t * 128 + 128]
             if 0 <= i <= 2:
-                loads.append((2, pltpu.make_async_copy(ks.at[i], block, sems.at[len(loads)])))
+                loads.append(pltpu.make_async_copy(ks.at[i], block, sems.at[len(loads)]))
             else:
                 block[...] = jnp.zeros(block.shape, BF16)
-    for _, c in loads:
+    for c in loads:
         c.start()
 
-    def arrived(which):
-        for n, c in loads:
-            if n == which:
-                c.wait()
-
-    small[...] = jnp.zeros_like(small)
-    for rows, out, lanes in ((rgb_rows, rgb_w, 128), (one_rows, one_w, 64)):
+    for rows, out, lanes, first in ((rgb_rows, rgb_w, 128, True), (one_rows, one_w, 64, False)):
+        small[...] = jnp.zeros_like(small)
         for f in range(4):
             for t in range(4):
-                i = (t - f if out is rgb_w else f - t) + 2
+                i = (t - f if first else f - t) + 2
                 if 0 <= i <= 2:
                     for n in range(9):
                         small[n * 12 + f * 3 : n * 12 + f * 3 + 3, t * lanes : t * lanes + lanes] = rows[
                             (i * 9 + n) * 3 : (i * 9 + n) * 3 + 3, 0:lanes
                         ]
         out[...] = small[:, 0 : 4 * lanes].astype(BF16)
-        if out is rgb_w:
-            small[...] = jnp.zeros_like(small)
+    for c in loads:
+        c.wait()
+
+
+def kernel(
+    own, left, right, top, bottom, w1_hbm, w2_hbm, sec_hbm, rgb_w, one_w, head,
+    out_ref, logit_ref,
+    field, pre1, pre2, pref, taps, valid, valid_s, part, pix, mid, line, w1, w2, sec, sems,
+):
+    loads = [
+        pltpu.make_async_copy(a, b, sems.at[n])
+        for n, (a, b) in enumerate(((w1_hbm, w1), (w2_hbm, w2), (sec_hbm, sec)))
+    ]
+    for c in loads:
+        c.start()
+
+    def arrived(which):
+        loads[which].wait()
 
     gy, gx = lax.axis_index("gy"), lax.axis_index("gx")
     ny, nx = lax.axis_size("gy"), lax.axis_size("gx")
@@ -139,12 +146,19 @@
     def dot(a, b):
         return jnp.dot(a, b, preferred_element_type=F32)
 
-    for t in range(4):
-        def body(y, _, t=t):
-            field[t, pl.ds(y, WIDE, TALL), :] = x_ref[t, y].astype(F32)
-            return 0
-
-        lax.fori_loop(0, HIGH, body, 0)
+    def place(ref, x, y, count):
+        def body(n, _):
+            for t in range(4):
+                field[t, pl.ds(x * TALL + y + n, ref.shape[2], TALL), :] = ref[t, n].astype(F32)
+            return 0
+
+        lax.fori_loop(0, count, body, 0, unroll=2)
+
+    place(left, 0, HALO, ROWS)
+    place(own, HALO, HALO, ROWS)
+    place(right, HALO + COLS, HALO, ROWS)
+    place(top, 0, 0, HALO)
+    place(bottom, 0, HALO + ROWS, HALO)
     spread(WIDE, TALL, 4, valid)
 
     def decode(w, pre, h, columns):
@@ -171,47 +185,57 @@
     arrived(1)
     decode(w2, pre2, 8, 16)
 
+    def sum_columns(src, count, turn):
+        rows = 6 * TALL
+
+        def body(n, _):
+            base = pl.multiple_of(n * rows, 8)
+            total = None
+            for l in range(3):
+                v = src[pl.ds(base + l * TALL, rows), :]
+                v = pltpu.roll(v, turn(l), 1) if turn(l) else v
+                total = v if total is None else total + v
+            mid[pl.ds(base, rows), :] = total
+            return 0
+
+        lax.fori_loop(0, -(-(count + 1) // 6), body, 0)
+
+    def sum_rows(base, rows, turn):
+        total = None
+        for j in range(3):
+            v = mid[pl.ds(base + j, rows), :]
+            v = pltpu.roll(v, turn(j), 1) if turn(j) else v
+            total = v if total is None else total + v
+        return total
+
     def gather_taps(count, h, flip):
         off = (HALO - h) * (TALL + 1)
-        lane = lax.broadcasted_iota(jnp.int32, (TALL, 128), 1)
-
-        def rows(x, _):
-            base = pl.multiple_of(x * TALL, 8)
-            total = None
-            for j in range(3):
-                q = None
-                for l in range(3):
-                    v = part[pl.ds(base + l * TALL + j, TALL), :]
-                    group = 2 - l if flip else l
-                    v = pltpu.roll(v, 128 - 12 * group, 1) if group else v
-                    q = v if q is None else q + v
-                group = 2 - j if flip else j
-                q = pltpu.roll(q, 128 - 36 * group, 1) if group else q
-                total = q if total is None else total + q
-            good = (valid[pl.ds(base + off, TALL), :] > 0) & (lane < 12)
-            pix[pl.ds(base, TALL), :] = jnp.where(good, total, 0.0).astype(BF16).astype(F32)
-            return 0
-
-        lax.fori_loop(0, count, rows, 0)
+        turn = lambda size: lambda n: (128 - size * (2 - n if flip else n)) % 128
+        sum_columns(part, count, turn(12))
+        rows = 6 * TALL
+        lane = lax.broadcasted_iota(jnp.int32, (rows, 128), 1)
+
+        def body(n, _):
+            base = pl.multiple_of(n * rows, 8)
+            total = sum_rows(base, rows, turn(36))
+            good = (valid[pl.ds(base + off, rows), :] > 0) & (lane < 12)
+            pix[pl.ds(base, rows), :] = jnp.where(good, total, 0.0).astype(BF16).astype(F32)
+            return 0
+
+        lax.fori_loop(0, -(-count // 6), body, 0)
 
     def scatter_taps(count, stride, flip):
-        def rows(x, _):
-            base = pl.multiple_of(x * TALL, 8)
-            total = None
-            for j in range(3):
-                q = None
-                for l in range(3):
-                    v = pix[pl.ds(base + l * TALL + j, stride), :]
-                    group = 2 - l if flip else l
-                    v = pltpu.roll(v, 12 * group, 1) if group else v
-                    q = v if q is None else q + v
-                group = 2 - j if flip else j
-                q = pltpu.roll(q, 36 * group, 1) if group else q
-                total = q if total is None else total + q
-            taps[0, pl.ds(pl.multiple_of(x * stride, 16), stride), 0:128] = total.astype(BF16)
-            return 0
-
-        lax.fori_loop(0, count, rows, 0)
+        turn = lambda size: lambda n: size * (2 - n if flip else n)
+        sum_columns(pix, count, turn(12))
+
+        def body(n, _):
+            for c in range(4):
+                x = n * 4 + c
+                v = sum_rows(pl.multiple_of(x * TALL, 8), stride, turn(36))
+                taps[0, pl.ds(pl.multiple_of(x * stride, 16), stride), 0:128] = v.astype(BF16)
+            return 0
+
+        lax.fori_loop(0, count // 4, body, 0)
 
     def rgb_part(n, _):
         rows = 16 * TALL
@@ -260,8 +284,14 @@
         return 0
 
     lax.fori_loop(0, 2, second, 0)
+    pick = jnp.where(
+        lax.broadcasted_iota(jnp.int32, (16, 128), 0) == lax.broadcasted_iota(jnp.int32, (16, 128), 1), 1.0, 0.0
+    ).astype(BF16)
     for x in range(COLS):
-        logit_ref[x] = part[pl.ds((x + 5) * TALL + 5, ROWS), :]
+        v = dot_t(pick, part[pl.ds((x + 5) * TALL + 5, 128), :].astype(BF16))
+        for t in range(4):
+            line[t, x : x + 1, :] = v[t : t + 1]
+    logit_ref[...] = line[:, :, 0:ROWS].astype(BF16)
     spread(width(5), TALL, 4)
 
     def second_back(n, _):
@@ -315,7 +345,7 @@
 def per_device(latent, conv_one, conv_two, to_rgb, disc_one, disc_two, disc_head):
     x = latent[0]
 
-    def widen(v, axis, dim):
+    def sides(v, axis, dim):
         n = lax.axis_size(axis)
         size = v.shape[dim]
         before = lax.ppermute(
@@ -324,23 +354,33 @@
         after = lax.ppermute(
             lax.slice_in_dim(v, 0, HALO, axis=dim), axis, [((i + 1) % n, i) for i in range(n)]
         )
-        return jnp.concatenate([before, v, after], dim)
-
-    x = widen(x, "gx", 2)
-    x = widen(x, "gy", 1)
+        return before, after
+
+    left, right = sides(x, "gx", 2)
+    top, bottom = sides(jnp.concatenate([left, x, right], 2), "gy", 1)
     taps = lambda k: k.reshape(3, 9, *k.shape[3:])
     rgb_rows = jnp.swapaxes(to_rgb, 3, 4).reshape(81, 128).astype(F32)
     one_rows = jnp.pad(disc_one.reshape(81, 64).astype(F32), ((0, 0), (0, 64)))
     vmem = pl.BlockSpec(memory_space=pltpu.VMEM)
     hbm = pl.BlockSpec(memory_space=pl.ANY)
     p = WIDE * TALL + PAD
+    shapes = [(2, 9, 256, 256), (2, 9, 256, 256), (9, 256, 512), (128, 512), (128, 256)]
+    weights = pl.pallas_call(
+        lay_out,
+        out_shape=[jax.ShapeDtypeStruct(n, BF16) for n in shapes],
+        in_specs=[hbm, hbm, hbm, vmem, vmem],
+        out_specs=[vmem] * 5,
+        scratch_shapes=[pltpu.VMEM((128, 512), F32), pltpu.SemaphoreType.DMA((24,))],
+        compiler_params=pltpu.CompilerParams(vmem_limit_bytes=16 << 20),
+        cost_estimate=pl.CostEstimate(flops=0, bytes_accessed=12 << 20, transcendentals=0),
+    )(taps(conv_one), taps(conv_two), taps(disc_two), rgb_rows, one_rows)
     out, logits = pl.pallas_call(
         kernel,
         out_shape=[
             jax.ShapeDtypeStruct((4, ROWS, COLS, 128), BF16),
-            jax.ShapeDtypeStruct((COLS, ROWS, 128), F32),
+            jax.ShapeDtypeStruct((4, COLS, ROWS), BF16),
         ],
-        in_specs=[vmem, hbm, hbm, hbm, vmem, vmem, vmem],
+        in_specs=[vmem] * 5 + [hbm] * 3 + [vmem] * 3,
         out_specs=[vmem, vmem],
         scratch_shapes=[
             pltpu.VMEM((4, p, 128), F32),
@@ -352,20 +392,14 @@
             pltpu.VMEM((p, 128), F32),
             pltpu.VMEM((p, 128), F32),
             pltpu.VMEM((p, 128), F32),
+            pltpu.VMEM((p, 128), F32),
+            pltpu.VMEM((4, COLS, 128), F32),
         ]
-        + [
-            pltpu.VMEM((2, 9, 256, 256), BF16),
-            pltpu.VMEM((2, 9, 256, 256), BF16),
-            pltpu.VMEM((9, 256, 512), BF16),
-            pltpu.VMEM((128, 512), F32),
-            pltpu.VMEM((128, 512), BF16),
-            pltpu.VMEM((128, 256), BF16),
-            pltpu.SemaphoreType.DMA((24,)),
-        ],
+        + [pltpu.VMEM(n, BF16) for n in shapes[:3]]
+        + [pltpu.SemaphoreType.DMA((3,))],
         compiler_params=pltpu.CompilerParams(vmem_limit_bytes=56 << 20),
-    )(x, taps(conv_one), taps(conv_two), taps(disc_two), rgb_rows, one_rows, disc_head.reshape(1, 128))
-    logits = jnp.transpose(logits[:, :, :4], (2, 1, 0)).astype(BF16)
-    return out[None], logits[None]
+    )(x, left, right, top, bottom, *weights, disc_head.reshape(1, 128))
+    return out[None], jnp.swapaxes(logits, 1, 2)[None]
 
 
 def solution(mesh):

time: 89.2 us -> 79.9 us (0.90)
  the two profiles are of different devices: /device:TPU:7 before, /device:TPU:0 now
where the time goes in v3:
time: 79.9 us; the launch traced here: 79.6 us
  Pallas kernels  44.4 us (56%)
  waiting for transfers between devices  15.8 us (20%)
  starting transfers between devices  8.55 us (11%)
  local copies, waits for them, and re-layouts  7.04 us (9%)
  other arithmetic  3.01 us (4%)
    pallas_call x1, Pallas kernels, per_device(): pl.pallas_call(kernel, out_shape=[jax.ShapeDtypeStruct((4, ROWS, COLS, 12...  42.9 us
    ppermute x2, starting transfers between devices, sides(): lax.ppermute(lax.slice_in_dim(v, 0, HALO, axis=dim), axis, [((i + 1) % n,...  8.55 us
    ppermute x2, waiting for transfers between devices, sides(): lax.ppermute(lax.slice_in_dim(v, 0, HALO, axis=dim), axis, [((i + 1) % n,...  8.37 us
    ppermute x2, waiting for transfers between devices, sides(): lax.ppermute(lax.slice_in_dim(v, size - HALO, size, axis=dim), axis, [(i,...  7.46 us
    unnamed x22, local copies, waits for them, and re-layouts  5.56 us
    concatenate x1, other arithmetic, per_device(): top, bottom = sides(jnp.concatenate([left, x, right], 2), 'gy', 1)  2.25 us
  transfers between devices with their start and end apart: 4, of which 3 were waited for; matrix products, arithmetic and copies ran while one was open for 1% of the time, Pallas kernels for 2%

profile of v3, /device:TPU:0, one launch (start us, length us, event | category | flops | bytes accessed | tf_op | source)
XLA Modules:
  0.0 79.6 jit_solution(9111030712895923489)
XLA Ops:
  0.6 0.0 copy-start.10
  0.6 0.0 copy-start.5
  0.7 1.4 %fusion = (bf16[4,24,10,128]{3,2,1,0:T(8,128)(2,1)S(1)}, bf16[4,24,10,128]{3,2,1,0:T(8,128)(2,1)S(1)}) fusion(bf16[4,24,16,128]{3,2,1,0:T(8,128)(2,1)} %bitcast.14), kind=kLoop, calls=%fused_computation.5 | loop fusion | bytes 983040 | tf_op jit(solution)/shard_map/slice | solution.py:355
  2.1 5.2 %collective-permute-start.1 = (bf16[4,24,10,128]{3,2,1,0:T(8,128)(2,1)S(1)}, bf16[4,24,10,128]{3,2,1,0:T(8,128)(2,1)S(1)}, u32[]{:S(2)}, u32[]{:S(2)}) collective-permute-start(bf16[4,24,10,128]{3,2,1,0:T(8,128)(2,1)S(1)} %get-tuple-element.18), channel_id=1, source_target_pairs={{1,0},{2,1},{3,2},{4,3},{5,4},{6,5},{7,6},{0,7},{9,8},{10,9},{11,1... | collective-permute-start | bytes 737288 | tf_op jit(solution)/shard_map/ppermute | solution.py:354
  7.3 0.0 collective-permute-start
  7.3 8.4 %collective-permute-done.1.right = bf16[4,24,10,128]{3,2,1,0:T(8,128)(2,1)S(1)} collective-permute-done((bf16[4,24,10,128]{3,2,1,0:T(8,128)(2,1)S(1)}, bf16[4,24,10,128]{3,2,1,0:T(8,128)(2,1)S(1)}, u32[]{:S(2)}, u32[]{:S(2)}) %collective-permute-start.1) | collective-permute-done | bytes 245792 | tf_op jit(solution)/shard_map/ppermute | solution.py:354
  15.7 4.3 %collective-permute-done.left = bf16[4,24,10,128]{3,2,1,0:T(8,128)(2,1)S(1)} collective-permute-done((bf16[4,24,10,128]{3,2,1,0:T(8,128)(2,1)S(1)}, bf16[4,24,10,128]{3,2,1,0:T(8,128)(2,1)S(1)}, u32[]{:S(2)}, u32[]{:S(2)}) %collective-permute-start) | collective-permute-done | bytes 245792 | tf_op jit(solution)/shard_map/ppermute | solution.py:351
  20.0 2.3 %pad_maximum_fusion = (bf16[4,10,36,128]{3,2,1,0:T(8,128)(2,1)}, bf16[4,10,36,128]{3,2,1,0:T(8,128)(2,1)S(1)}) fusion(bf16[4,24,10,128]{3,2,1,0:T(8,128)(2,1)S(1)} %collective-permute-done.1.right, bf16[4,24,16,128]{3,2,1,0:T(8,128)(2,1)} %bitcast.15, bf16[4,24,10,128]{3,2,1,0:T(8,128)(2,1)S(1)} %collective-permute-done.left), kind=kLoop, calls=%fused_computation | loop fusion | flops 2211840 | bytes 1622016 | tf_op jit(solution)/shard_map/concatenate | solution.py:360
  22.2 3.3 %collective-permute-start.3 = (bf16[4,10,36,128]{3,2,1,0:T(8,128)(2,1)}, bf16[4,10,36,128]{3,2,1,0:T(8,128)(2,1)}, u32[]{:S(2)}, u32[]{:S(2)}) collective-permute-start(bf16[4,10,36,128]{3,2,1,0:T(8,128)(2,1)} %get-tuple-element.16), channel_id=1, source_target_pairs={{8,0},{16,8},{24,16},{32,24},{40,32},{48,40},{56,48},{64,56},{72,6... | collective-permute-start | bytes 1105928 | tf_op jit(solution)/shard_map/ppermute | solution.py:354
  25.6 0.0 collective-permute-start.2
  25.6 0.8 convert_bitcast_fusion
  26.4 0.0 copy-done.5
  26.4 0.0 copy-done.4
  26.4 0.0 copy-done.3
  26.4 1.5 %shard_map.86 = (bf16[2,9,256,256]{3,2,1,0:T(8,128)(2,1)S(1)}, bf16[2,9,256,256]{3,2,1,0:T(8,128)(2,1)S(1)}, bf16[9,256,512]{2,1,0:T(8,128)(2,1)S(1)}, bf16[128,512]{1,0:T(8,128)(2,1)S(1)}, bf16[128,256]{1,0:T(8,128)(2,1)S(1)}) custom-call(bf16[3,9,128,128]{3,2,1,0:T(8,128)(2,1)S(1)} %bitcast.11, bf16[3,9,128,128]{3,2,1,0:T(8,128)(2,1)S(1)} %bitcast.12, ...), custom_call_target="tpu_custom_call" | custom-call | bytes 12582912 | tf_op jit(solution)/shard_map/pallas_call | solution.py:368
  28.0 1.4 %copy-done = bf16[2,9,256,256]{3,2,1,0:T(8,128)(2,1)} copy-done((bf16[2,9,256,256]{3,2,1,0:T(8,128)(2,1)}, bf16[2,9,256,256]{3,2,1,0:T(8,128)(2,1)S(1)}, u32[]{:S(2)}) %copy-start) | copy-done | bytes 2359320
  29.4 1.4 %copy-done.1 = bf16[2,9,256,256]{3,2,1,0:T(8,128)(2,1)} copy-done((bf16[2,9,256,256]{3,2,1,0:T(8,128)(2,1)}, bf16[2,9,256,256]{3,2,1,0:T(8,128)(2,1)S(1)}, u32[]{:S(2)}) %copy-start.1) | copy-done | bytes 2359320
  30.8 1.4 %copy-done.2 = bf16[9,256,512]{2,1,0:T(8,128)(2,1)} copy-done((bf16[9,256,512]{2,1,0:T(8,128)(2,1)}, bf16[9,256,512]{2,1,0:T(8,128)(2,1)S(1)}, u32[]{:S(2)}) %copy-start.2) | copy-done | bytes 2359320
  32.3 0.6 copy-done.6
  32.9 0.6 copy-done.7
  33.5 0.0 collective-permute-done.3.bottom
  33.5 3.2 %collective-permute-done.2.top = bf16[4,10,36,128]{3,2,1,0:T(8,128)(2,1)} collective-permute-done((bf16[4,10,36,128]{3,2,1,0:T(8,128)(2,1)S(1)}, bf16[4,10,36,128]{3,2,1,0:T(8,128)(2,1)}, u32[]{:S(2)}, u32[]{:S(2)}) %collective-permute-start.2) | collective-permute-done | bytes 368672 | tf_op jit(solution)/shard_map/ppermute | solution.py:351
  36.7 0.0 copy-done.8
  36.7 42.9 %shard_map.87 = (bf16[4,24,16,128]{3,2,1,0:T(8,128)(2,1)}, bf16[4,16,24]{2,1,0:T(8,128)(2,1)}) custom-call(bf16[4,24,16,128]{3,2,1,0:T(8,128)(2,1)} %bitcast.16, bf16[4,24,10,128]{3,2,1,0:T(8,128)(2,1)} %copy-done.9, bf16[4,24,10,128]{3,2,1,0:T(8,128)(2,1)} %copy-done.8, bf16[4,10,36,128]{3,2,1,0:T(8,128)(2,1)} %collective-permute-done.2.top, ...), custom_call_target="tpu_custom_call" | custom-call | tf_op jit(solution)/shard_map/pallas_call | solution.py:377
  (14 shorter events, 0.1 us)
Async XLA Ops:
  0.6 25.0 %copy-start.10 = (bf16[3,3,3,3,64]{4,3,2,1,0:T(4,128)(2,1)S(1)}, bf16[3,3,3,3,64]{4,3,2,1,0:T(4,128)(2,1)}, u32[]{:S(2)}) copy-start(bf16[3,3,3,3,64]{4,3,2,1,0:T(4,128)(2,1)} %param.11) | copy-start | bytes 31108
  0.6 25.8 %copy-start.5 = (bf16[3,3,3,64,128]{4,3,2,1,0:T(8,128)(2,1)S(1)}, bf16[3,3,3,64,128]{4,3,2,1,0:T(8,128)(2,1)}, u32[]{:S(2)}) copy-start(bf16[3,3,3,64,128]{4,3,2,1,0:T(8,128)(2,1)} %param.12) | copy-start | bytes 1327108
  0.7 25.8 %copy-start.4 = (bf16[3,3,3,128,128]{4,3,2,1,0:T(8,128)(2,1)S(1)}, bf16[3,3,3,128,128]{4,3,2,1,0:T(8,128)(2,1)}, u32[]{:S(2)}) copy-start(bf16[3,3,3,128,128]{4,3,2,1,0:T(8,128)(2,1)} %param.9) | copy-start | bytes 2654212
  0.7 25.8 %copy-start.3 = (bf16[3,3,3,128,128]{4,3,2,1,0:T(8,128)(2,1)S(1)}, bf16[3,3,3,128,128]{4,3,2,1,0:T(8,128)(2,1)}, u32[]{:S(2)}) copy-start(bf16[3,3,3,128,128]{4,3,2,1,0:T(8,128)(2,1)} %param.8) | copy-start | bytes 2654212
  2.1 13.6 %collective-permute-start.1 = (bf16[4,24,10,128]{3,2,1,0:T(8,128)(2,1)S(1)}, bf16[4,24,10,128]{3,2,1,0:T(8,128)(2,1)S(1)}, u32[]{:S(2)}, u32[]{:S(2)}) collective-permute-start(bf16[4,24,10,128]{3,2,1,0:T(8,128)(2,1)S(1)} %get-tuple-element.18), channel_id=1, source_target_pairs={{1,0},{2,1},{3,2},{4,3},{5,4},{6,5},{7,6},{0,7},{9,8},{10,9},{11,1... | collective-permute-start | bytes 737288 | tf_op jit(solution)/shard_map/ppermute | solution.py:354
  7.3 12.7 %collective-permute-start = (bf16[4,24,10,128]{3,2,1,0:T(8,128)(2,1)S(1)}, bf16[4,24,10,128]{3,2,1,0:T(8,128)(2,1)S(1)}, u32[]{:S(2)}, u32[]{:S(2)}) collective-permute-start(bf16[4,24,10,128]{3,2,1,0:T(8,128)(2,1)S(1)} %get-tuple-element.19), channel_id=1, source_target_pairs={{0,1},{1,2},{2,3},{3,4},{4,5},{5,6},{6,7},{7,0},{8,9},{9,10},{10,1... | collective-permute-start | bytes 737288 | tf_op jit(solution)/shard_map/ppermute | solution.py:351
  15.7 21.0 %copy-start.8 = (bf16[4,24,10,128]{3,2,1,0:T(8,128)(2,1)}, bf16[4,24,10,128]{3,2,1,0:T(8,128)(2,1)S(1)}, u32[]{:S(2)}) copy-start(bf16[4,24,10,128]{3,2,1,0:T(8,128)(2,1)S(1)} %collective-permute-done.1.right) | copy-start | bytes 737284
  20.0 16.7 %copy-start.9 = (bf16[4,24,10,128]{3,2,1,0:T(8,128)(2,1)}, bf16[4,24,10,128]{3,2,1,0:T(8,128)(2,1)S(1)}, u32[]{:S(2)}) copy-start(bf16[4,24,10,128]{3,2,1,0:T(8,128)(2,1)S(1)} %collective-permute-done.left) | copy-start | bytes 737284
  22.2 11.3 %collective-permute-start.3 = (bf16[4,10,36,128]{3,2,1,0:T(8,128)(2,1)}, bf16[4,10,36,128]{3,2,1,0:T(8,128)(2,1)}, u32[]{:S(2)}, u32[]{:S(2)}) collective-permute-start(bf16[4,10,36,128]{3,2,1,0:T(8,128)(2,1)} %get-tuple-element.16), channel_id=1, source_target_pairs={{8,0},{16,8},{24,16},{32,24},{40,32},{48,40},{56,48},{64,56},{72,6... | collective-permute-start | bytes 1105928 | tf_op jit(solution)/shard_map/ppermute | solution.py:354
  25.6 11.1 %collective-permute-start.2 = (bf16[4,10,36,128]{3,2,1,0:T(8,128)(2,1)S(1)}, bf16[4,10,36,128]{3,2,1,0:T(8,128)(2,1)}, u32[]{:S(2)}, u32[]{:S(2)}) collective-permute-start(bf16[4,10,36,128]{3,2,1,0:T(8,128)(2,1)S(1)} %get-tuple-element.17), channel_id=1, source_target_pairs={{0,8},{8,16},{16,24},{24,32},{32,40},{40,48},{48,56},{56,64},{64,7... | collective-permute-start | bytes 1105928 | tf_op jit(solution)/shard_map/ppermute | solution.py:351
  28.0 1.4 %copy-start = (bf16[2,9,256,256]{3,2,1,0:T(8,128)(2,1)}, bf16[2,9,256,256]{3,2,1,0:T(8,128)(2,1)S(1)}, u32[]{:S(2)}) copy-start(bf16[2,9,256,256]{3,2,1,0:T(8,128)(2,1)S(1)} %get-tuple-element.9.w1_hbm) | copy-start | bytes 7077892
  29.4 1.4 %copy-start.1 = (bf16[2,9,256,256]{3,2,1,0:T(8,128)(2,1)}, bf16[2,9,256,256]{3,2,1,0:T(8,128)(2,1)S(1)}, u32[]{:S(2)}) copy-start(bf16[2,9,256,256]{3,2,1,0:T(8,128)(2,1)S(1)} %get-tuple-element.10.w2_hbm) | copy-start | bytes 7077892
  30.8 1.4 %copy-start.2 = (bf16[9,256,512]{2,1,0:T(8,128)(2,1)}, bf16[9,256,512]{2,1,0:T(8,128)(2,1)S(1)}, u32[]{:S(2)}) copy-start(bf16[9,256,512]{2,1,0:T(8,128)(2,1)S(1)} %get-tuple-element.11.sec_hbm) | copy-start | bytes 7077892
  32.3 0.6 copy-start.6
  32.9 0.6 copy-start.7

commit v4 on v3

--- a/solution.py
+++ b/solution.py
@@ -73,21 +73,36 @@
         c.wait()
 
 
+def cut_columns(own, first, last, rows):
+    for t in range(4):
+        rows[t] = own[t].reshape(ROWS * COLS, 128).astype(F32)
+    for x in range(HALO):
+        for t in range(4):
+            first[x, t] = rows[t, pl.ds(x, ROWS, COLS), :].astype(BF16)
+            last[x, t] = rows[t, pl.ds(COLS - HALO + x, ROWS, COLS), :].astype(BF16)
+
+
+def cut_rows(own, left, right, first, last, rows):
+    low = ROWS - HALO
+    for t in range(4):
+        for y in range(HALO):
+            rows[0, t, pl.ds(HALO * HALO + y, COLS, HALO), :] = own[t, y].astype(F32)
+            rows[1, t, pl.ds(HALO * HALO + y, COLS, HALO), :] = own[t, low + y].astype(F32)
+        for ref, start in ((left, 0), (right, HALO + COLS)):
+            for x in range(HALO):
+                v = ref[x, t].astype(F32)
+                at = (start + x) * HALO
+                rows[0, t, at : at + HALO, :] = v[0:HALO]
+                rows[1, t, at : at + HALO, :] = v[low:ROWS]
+        first[t] = rows[0, t].astype(BF16)
+        last[t] = rows[1, t].astype(BF16)
+
+
 def kernel(
-    own, left, right, top, bottom, w1_hbm, w2_hbm, sec_hbm, rgb_w, one_w, head,
+    own, left, right, top, bottom, w1, w2, sec, rgb_w, one_w, head,
     out_ref, logit_ref,
-    field, pre1, pre2, pref, taps, valid, valid_s, part, pix, mid, line, w1, w2, sec, sems,
+    field, pre1, pre2, pref, taps, valid, valid_s, part, pix, mid, line, edge,
 ):
-    loads = [
-        pltpu.make_async_copy(a, b, sems.at[n])
-        for n, (a, b) in enumerate(((w1_hbm, w1), (w2_hbm, w2), (sec_hbm, sec)))
-    ]
-    for c in loads:
-        c.start()
-
-    def arrived(which):
-        loads[which].wait()
-
     gy, gx = lax.axis_index("gy"), lax.axis_index("gx")
     ny, nx = lax.axis_size("gy"), lax.axis_size("gx")
 
@@ -146,19 +161,21 @@
     def dot(a, b):
         return jnp.dot(a, b, preferred_element_type=F32)
 
-    def place(ref, x, y, count):
-        def body(n, _):
-            for t in range(4):
-                field[t, pl.ds(x * TALL + y + n, ref.shape[2], TALL), :] = ref[t, n].astype(F32)
-            return 0
-
-        lax.fori_loop(0, count, body, 0, unroll=2)
-
-    place(left, 0, HALO, ROWS)
-    place(own, HALO, HALO, ROWS)
-    place(right, HALO + COLS, HALO, ROWS)
-    place(top, 0, 0, HALO)
-    place(bottom, 0, HALO + ROWS, HALO)
+    def place(n, _):
+        for t in range(4):
+            field[t, pl.ds(HALO * TALL + HALO + n, COLS, TALL), :] = own[t, n].astype(F32)
+        return 0
+
+    lax.fori_loop(0, ROWS, place, 0, unroll=4)
+    for t in range(4):
+        for x in range(HALO):
+            for ref, start in ((left, 0), (right, HALO + COLS)):
+                at = (start + x) * TALL + HALO
+                field[t, at : at + ROWS, :] = ref[x, t].astype(F32)
+        for n, (ref, y) in enumerate(((top, 0), (bottom, HALO + ROWS))):
+            edge[n, t] = ref[t].astype(F32)
+            for x in range(WIDE):
+                field[t, x * TALL + y : x * TALL + y + HALO, :] = edge[n, t, x * HALO : x * HALO + HALO, :]
     spread(WIDE, TALL, 4, valid)
 
     def decode(w, pre, h, columns):
@@ -179,10 +196,8 @@
 
         lax.fori_loop(0, width(h) // columns, body, 0)
 
-    arrived(0)
     decode(w1, pre1, 9, 17)
     spread(width(9), TALL, 4)
-    arrived(1)
     decode(w2, pre2, 8, 16)
 
     def sum_columns(src, count, turn):
@@ -262,7 +277,6 @@
 
     lax.fori_loop(0, 2, first, 0)
     spread(width(6), TALL, 2)
-    arrived(2)
 
     def second(n, _):
         rows = 13 * TALL
@@ -345,24 +359,36 @@
 def per_device(latent, conv_one, conv_two, to_rgb, disc_one, disc_two, disc_head):
     x = latent[0]
 
-    def sides(v, axis, dim):
+    vmem = pl.BlockSpec(memory_space=pltpu.VMEM)
+    hbm = pl.BlockSpec(memory_space=pl.ANY)
+
+    def exchange(first, last, axis):
         n = lax.axis_size(axis)
-        size = v.shape[dim]
-        before = lax.ppermute(
-            lax.slice_in_dim(v, size - HALO, size, axis=dim), axis, [(i, (i + 1) % n) for i in range(n)]
-        )
-        after = lax.ppermute(
-            lax.slice_in_dim(v, 0, HALO, axis=dim), axis, [((i + 1) % n, i) for i in range(n)]
-        )
+        before = lax.ppermute(last, axis, [(i, (i + 1) % n) for i in range(n)])
+        after = lax.ppermute(first, axis, [((i + 1) % n, i) for i in range(n)])
         return before, after
 
-    left, right = sides(x, "gx", 2)
-    top, bottom = sides(jnp.concatenate([left, x, right], 2), "gy", 1)
+    first, last = pl.pallas_call(
+        cut_columns,
+        out_shape=[jax.ShapeDtypeStruct((HALO, 4, ROWS, 128), BF16)] * 2,
+        in_specs=[vmem],
+        out_specs=[vmem] * 2,
+        scratch_shapes=[pltpu.VMEM((4, ROWS * COLS, 128), F32)],
+        compiler_params=pltpu.CompilerParams(vmem_limit_bytes=8 << 20),
+    )(x)
+    left, right = exchange(first, last, "gx")
+    first, last = pl.pallas_call(
+        cut_rows,
+        out_shape=[jax.ShapeDtypeStruct((4, WIDE * HALO, 128), BF16)] * 2,
+        in_specs=[vmem] * 3,
+        out_specs=[vmem] * 2,
+        scratch_shapes=[pltpu.VMEM((2, 4, WIDE * HALO, 128), F32)],
+        compiler_params=pltpu.CompilerParams(vmem_limit_bytes=8 << 20),
+    )(x, left, right)
+    top, bottom = exchange(first, last, "gy")
     taps = lambda k: k.reshape(3, 9, *k.shape[3:])
     rgb_rows = jnp.swapaxes(to_rgb, 3, 4).reshape(81, 128).astype(F32)
     one_rows = jnp.pad(disc_one.reshape(81, 64).astype(F32), ((0, 0), (0, 64)))
-    vmem = pl.BlockSpec(memory_space=pltpu.VMEM)
-    hbm = pl.BlockSpec(memory_space=pl.ANY)
     p = WIDE * TALL + PAD
     shapes = [(2, 9, 256, 256), (2, 9, 256, 256), (9, 256, 512), (128, 512), (128, 256)]
     weights = pl.pallas_call(
@@ -380,7 +406,7 @@
             jax.ShapeDtypeStruct((4, ROWS, COLS, 128), BF16),
             jax.ShapeDtypeStruct((4, COLS, ROWS), BF16),
         ],
-        in_specs=[vmem] * 5 + [hbm] * 3 + [vmem] * 3,
+        in_specs=[vmem] * 11,
         out_specs=[vmem, vmem],
         scratch_shapes=[
             pltpu.VMEM((4, p, 128), F32),
@@ -394,10 +420,9 @@
             pltpu.VMEM((p, 128), F32),
             pltpu.VMEM((p, 128), F32),
             pltpu.VMEM((4, COLS, 128), F32),
-        ]
-        + [pltpu.VMEM(n, BF16) for n in shapes[:3]]
-        + [pltpu.SemaphoreType.DMA((3,))],
-        compiler_params=pltpu.CompilerParams(vmem_limit_bytes=56 << 20),
+            pltpu.VMEM((2, 4, WIDE * HALO, 128), F32),
+        ],
+        compiler_params=pltpu.CompilerParams(vmem_limit_bytes=34 << 20),
     )(x, left, right, top, bottom, *weights, disc_head.reshape(1, 128))
     return out[None], jnp.swapaxes(logits, 1, 2)[None]
 

time: 79.9 us -> 67.9 us (0.85)
  the two profiles are of different devices: /device:TPU:0 before, /device:TPU:7 now
where the time goes in v4:
time: 67.9 us; the launch traced here: 67.5 us
  Pallas kernels  42.6 us (63%)
  waiting for transfers between devices  9.7 us (14%)
  starting transfers between devices  8.64 us (13%)
  local copies, waits for them, and re-layouts  5.14 us (8%)
  other arithmetic  0.76 us (1%)
  between operations  0.7 us (1%)
    pallas_call x1, Pallas kernels, per_device(): pl.pallas_call(kernel, out_shape=[jax.ShapeDtypeStruct((4, ROWS, COLS, 12...  40.5 us
    ppermute x2, waiting for transfers between devices, exchange(): before = lax.ppermute(last, axis, [(i, (i + 1) % n) for i in range(n)])  5.6 us
    ppermute x2, starting transfers between devices, exchange(): before = lax.ppermute(last, axis, [(i, (i + 1) % n) for i in range(n)])  5.42 us
    unnamed x12, local copies, waits for them, and re-layouts  4.34 us
    ppermute x2, waiting for transfers between devices, exchange(): after = lax.ppermute(first, axis, [((i + 1) % n, i) for i in range(n)])  4.09 us
    ppermute x2, starting transfers between devices, exchange(): after = lax.ppermute(first, axis, [((i + 1) % n, i) for i in range(n)])  3.22 us
    pallas_call x1, Pallas kernels, per_device(): pl.pallas_call(lay_out, out_shape=[jax.ShapeDtypeStruct(n, BF16) for n in...  1.52 us
  transfers between devices with their start and end apart: 4, of which 2 were waited for; matrix products, arithmetic and copies ran while one was open for 2% of the time, Pallas kernels for 2%

profile of v4, /device:TPU:7, one launch (start us, length us, event | category | flops | bytes accessed | tf_op | source)
XLA Modules:
  0.0 67.5 jit_solution(14611846084313254376)
XLA Ops:
  0.6 0.0 copy-start.5
  0.6 0.0 copy-start
  0.6 1.0 %copy-done = bf16[1,4,24,16,128]{4,3,2,1,0:T(8,128)(2,1)S(1)} copy-done((bf16[1,4,24,16,128]{4,3,2,1,0:T(8,128)(2,1)S(1)}, bf16[1,4,24,16,128]{4,3,2,1,0:T(8,128)(2,1)}, u32[]{:S(2)}) %copy-start) | copy-done | bytes 393240
  1.6 0.0 copy-start.1
  1.6 0.3 shard_map.86
  2.0 1.7 %collective-permute-start = (bf16[10,4,24,128]{3,2,1,0:T(8,128)(2,1)S(1)}, bf16[10,4,24,128]{3,2,1,0:T(8,128)(2,1)S(1)}, u32[]{:S(2)}, u32[]{:S(2)}) collective-permute-start(bf16[10,4,24,128]{3,2,1,0:T(8,128)(2,1)S(1)} %get-tuple-element.13), channel_id=1, source_target_pairs={{0,1},{1,2},{2,3},{3,4},{4,5},{5,6},{6,7},{7,0},{8,9},{9,10},{10,1... | collective-permute-start | bytes 737288 | tf_op jit(solution)/shard_map/ppermute | solution.py:367
  3.7 3.2 %collective-permute-start.1 = (bf16[10,4,24,128]{3,2,1,0:T(8,128)(2,1)S(1)}, bf16[10,4,24,128]{3,2,1,0:T(8,128)(2,1)S(1)}, u32[]{:S(2)}, u32[]{:S(2)}) collective-permute-start(bf16[10,4,24,128]{3,2,1,0:T(8,128)(2,1)S(1)} %get-tuple-element.14), channel_id=1, source_target_pairs={{1,0},{2,1},{3,2},{4,3},{5,4},{6,5},{7,6},{0,7},{9,8},{10,9},{11,1... | collective-permute-start | bytes 737288 | tf_op jit(solution)/shard_map/ppermute | solution.py:368
  6.9 5.6 %collective-permute-done.left = bf16[10,4,24,128]{3,2,1,0:T(8,128)(2,1)S(1)} collective-permute-done((bf16[10,4,24,128]{3,2,1,0:T(8,128)(2,1)S(1)}, bf16[10,4,24,128]{3,2,1,0:T(8,128)(2,1)S(1)}, u32[]{:S(2)}, u32[]{:S(2)}) %collective-permute-start) | collective-permute-done | bytes 245792 | tf_op jit(solution)/shard_map/ppermute | solution.py:367
  12.5 0.0 collective-permute-done.1.right
  12.5 0.2 shard_map.87
  12.7 3.7 %collective-permute-start.2 = (bf16[4,360,128]{2,1,0:T(8,128)(2,1)S(1)}, bf16[4,360,128]{2,1,0:T(8,128)(2,1)S(1)}, u32[]{:S(2)}, u32[]{:S(2)}) collective-permute-start(bf16[4,360,128]{2,1,0:T(8,128)(2,1)S(1)} %get-tuple-element.15), channel_id=1, source_target_pairs={{0,8},{8,16},{16,24},{24,32},{32,40},{40,48},{48,56},{56,64},{64,7... | collective-permute-start | bytes 1105928 | tf_op jit(solution)/shard_map/ppermute | solution.py:367
  16.4 0.0 collective-permute-start.3
  16.4 0.8 %convert_element_type.16 = bf16[81,64]{1,0:T(8,128)(2,1)S(1)} reshape(bf16[3,3,3,3,64]{4,3,2,1,0:T(4,128)(2,1)} %param.11) | data formatting | bytes 20736 | tf_op jit(solution)/shard_map/convert_element_type | solution.py:391
  17.2 0.8 %convert_bitcast_fusion = f32[3,3,3,3,128]{4,3,2,1,0:T(4,128)S(1)} fusion(bf16[3,3,3,128,3]{3,4,2,1,0:T(4,128)(2,1)} %param.10), kind=kLoop, calls=%fused_computation | loop fusion | flops 10368 | bytes 62208 | tf_op jit(solution)/shard_map/convert_element_type | solution.py:390
  18.0 0.0 copy-start.2
  18.0 1.2 %copy-done.2 = bf16[3,3,3,128,128]{4,3,2,1,0:T(8,128)(2,1)S(1)} copy-done((bf16[3,3,3,128,128]{4,3,2,1,0:T(8,128)(2,1)S(1)}, bf16[3,3,3,128,128]{4,3,2,1,0:T(8,128)(2,1)}, u32[]{:S(2)}) %copy-start.2) | copy-done | bytes 884760
  19.1 1.2 %copy-done.3 = bf16[3,3,3,128,128]{4,3,2,1,0:T(8,128)(2,1)S(1)} copy-done((bf16[3,3,3,128,128]{4,3,2,1,0:T(8,128)(2,1)S(1)}, bf16[3,3,3,128,128]{4,3,2,1,0:T(8,128)(2,1)}, u32[]{:S(2)}) %copy-start.3) | copy-done | bytes 884760
  20.3 1.0 %copy-done.4 = bf16[3,3,3,64,128]{4,3,2,1,0:T(8,128)(2,1)S(1)} copy-done((bf16[3,3,3,64,128]{4,3,2,1,0:T(8,128)(2,1)S(1)}, bf16[3,3,3,64,128]{4,3,2,1,0:T(8,128)(2,1)}, u32[]{:S(2)}) %copy-start.4) | copy-done | bytes 442392
  21.3 1.5 %shard_map.88 = (bf16[2,9,256,256]{3,2,1,0:T(8,128)(2,1)S(1)}, bf16[2,9,256,256]{3,2,1,0:T(8,128)(2,1)S(1)}, bf16[9,256,512]{2,1,0:T(8,128)(2,1)S(1)}, bf16[128,512]{1,0:T(8,128)(2,1)S(1)}, bf16[128,256]{1,0:T(8,128)(2,1)S(1)}) custom-call(bf16[3,9,128,128]{3,2,1,0:T(8,128)(2,1)S(1)} %bitcast.14, bf16[3,9,128,128]{3,2,1,0:T(8,128)(2,1)S(1)} %bitcast.15, ...), custom_call_target="tpu_custom_call" | custom-call | bytes 12582912 | tf_op jit(solution)/shard_map/pallas_call | solution.py:394
  22.8 0.0 collective-permute-done.2.top
  22.9 4.1 %collective-permute-done.3.bottom = bf16[4,360,128]{2,1,0:T(8,128)(2,1)S(1)} collective-permute-done((bf16[4,360,128]{2,1,0:T(8,128)(2,1)S(1)}, bf16[4,360,128]{2,1,0:T(8,128)(2,1)S(1)}, u32[]{:S(2)}, u32[]{:S(2)}) %collective-permute-start.3) | collective-permute-done | bytes 368672 | tf_op jit(solution)/shard_map/ppermute | solution.py:368
  26.9 0.0 copy-done.5
  26.9 0.0 copy-done.1
  27.0 40.5 %shard_map.89 = (bf16[4,24,16,128]{3,2,1,0:T(8,128)(2,1)}, bf16[4,16,24]{2,1,0:T(8,128)(2,1)}) custom-call(bf16[4,24,16,128]{3,2,1,0:T(8,128)(2,1)S(1)} %bitcast.13, bf16[10,4,24,128]{3,2,1,0:T(8,128)(2,1)S(1)} %collective-permute-done.left, bf16[10,4,24,128]{3,2,1,0:T(8,128)(2,1)S(1)} %collective-permute-done.1.right, ...), custom_call_target="tpu_custom_call" | custom-call | tf_op jit(solution)/shard_map/pallas_call | solution.py:403
  (4 shorter events, 0.0 us)
Async XLA Ops:
  0.6 26.3 %copy-start.5 = (f32[128]{0:T(128)S(1)}, f32[128]{0:T(128)}, u32[]{:S(2)}) copy-start(f32[128]{0:T(128)} %param.13) | copy-start | bytes 1540
  0.6 1.0 %copy-start = (bf16[1,4,24,16,128]{4,3,2,1,0:T(8,128)(2,1)S(1)}, bf16[1,4,24,16,128]{4,3,2,1,0:T(8,128)(2,1)}, u32[]{:S(2)}) copy-start(bf16[1,4,24,16,128]{4,3,2,1,0:T(8,128)(2,1)} %param.7) | copy-start | bytes 1179652
  1.6 25.3 %copy-start.1 = (bf16[1,4,24,16,128]{4,3,2,1,0:T(8,128)(2,1)S(1)}, bf16[1,4,24,16,128]{4,3,2,1,0:T(8,128)(2,1)}, u32[]{:S(2)}) copy-start(bf16[1,4,24,16,128]{4,3,2,1,0:T(8,128)(2,1)} %param.7) | copy-start | bytes 1179652
  2.0 10.5 %collective-permute-start = (bf16[10,4,24,128]{3,2,1,0:T(8,128)(2,1)S(1)}, bf16[10,4,24,128]{3,2,1,0:T(8,128)(2,1)S(1)}, u32[]{:S(2)}, u32[]{:S(2)}) collective-permute-start(bf16[10,4,24,128]{3,2,1,0:T(8,128)(2,1)S(1)} %get-tuple-element.13), channel_id=1, source_target_pairs={{0,1},{1,2},{2,3},{3,4},{4,5},{5,6},{6,7},{7,0},{8,9},{9,10},{10,1... | collective-permute-start | bytes 737288 | tf_op jit(solution)/shard_map/ppermute | solution.py:367
  3.7 8.8 %collective-permute-start.1 = (bf16[10,4,24,128]{3,2,1,0:T(8,128)(2,1)S(1)}, bf16[10,4,24,128]{3,2,1,0:T(8,128)(2,1)S(1)}, u32[]{:S(2)}, u32[]{:S(2)}) collective-permute-start(bf16[10,4,24,128]{3,2,1,0:T(8,128)(2,1)S(1)} %get-tuple-element.14), channel_id=1, source_target_pairs={{1,0},{2,1},{3,2},{4,3},{5,4},{6,5},{7,6},{0,7},{9,8},{10,9},{11,1... | collective-permute-start | bytes 737288 | tf_op jit(solution)/shard_map/ppermute | solution.py:368
  12.7 10.2 %collective-permute-start.2 = (bf16[4,360,128]{2,1,0:T(8,128)(2,1)S(1)}, bf16[4,360,128]{2,1,0:T(8,128)(2,1)S(1)}, u32[]{:S(2)}, u32[]{:S(2)}) collective-permute-start(bf16[4,360,128]{2,1,0:T(8,128)(2,1)S(1)} %get-tuple-element.15), channel_id=1, source_target_pairs={{0,8},{8,16},{16,24},{24,32},{32,40},{40,48},{48,56},{56,64},{64,7... | collective-permute-start | bytes 1105928 | tf_op jit(solution)/shard_map/ppermute | solution.py:367
  16.4 10.6 %collective-permute-start.3 = (bf16[4,360,128]{2,1,0:T(8,128)(2,1)S(1)}, bf16[4,360,128]{2,1,0:T(8,128)(2,1)S(1)}, u32[]{:S(2)}, u32[]{:S(2)}) collective-permute-start(bf16[4,360,128]{2,1,0:T(8,128)(2,1)S(1)} %get-tuple-element.16), channel_id=1, source_target_pairs={{8,0},{16,8},{24,16},{32,24},{40,32},{48,40},{56,48},{64,56},{72,6... | collective-permute-start | bytes 1105928 | tf_op jit(solution)/shard_map/ppermute | solution.py:368
  18.0 1.2 %copy-start.2 = (bf16[3,3,3,128,128]{4,3,2,1,0:T(8,128)(2,1)S(1)}, bf16[3,3,3,128,128]{4,3,2,1,0:T(8,128)(2,1)}, u32[]{:S(2)}) copy-start(bf16[3,3,3,128,128]{4,3,2,1,0:T(8,128)(2,1)} %param.8) | copy-start | bytes 2654212
  19.1 1.2 %copy-start.3 = (bf16[3,3,3,128,128]{4,3,2,1,0:T(8,128)(2,1)S(1)}, bf16[3,3,3,128,128]{4,3,2,1,0:T(8,128)(2,1)}, u32[]{:S(2)}) copy-start(bf16[3,3,3,128,128]{4,3,2,1,0:T(8,128)(2,1)} %param.9) | copy-start | bytes 2654212
  20.3 1.0 %copy-start.4 = (bf16[3,3,3,64,128]{4,3,2,1,0:T(8,128)(2,1)S(1)}, bf16[3,3,3,64,128]{4,3,2,1,0:T(8,128)(2,1)}, u32[]{:S(2)}) copy-start(bf16[3,3,3,64,128]{4,3,2,1,0:T(8,128)(2,1)} %param.12) | copy-start | bytes 1327108

commit v5 on v4

--- a/solution.py
+++ b/solution.py
@@ -27,7 +27,8 @@
 
 
 def silu(v):
-    return v * sigmoid(v)
+    half = 0.5 * v
+    return half + half * jnp.tanh(half)
 
 
 def dsilu(v):
@@ -35,7 +36,7 @@
     return s * (1.0 + v * (1.0 - s))
 
 
-def lay_out(k1, k2, ks, rgb_rows, one_rows, w1, w2, sec, rgb_w, one_w, small, sems):
+def lay_out(k1, k2, ks, rgb_rows, one_rows, w1, w2, sec, rgb_w, one_w, rgb_taps, one_taps, small, sems):
     loads = []
     for k, w in ((k1, w1), (k2, w2)):
         for far in range(2):
@@ -58,7 +59,11 @@
     for c in loads:
         c.start()
 
-    for rows, out, lanes, first in ((rgb_rows, rgb_w, 128, True), (one_rows, one_w, 64, False)):
+    mine = lax.broadcasted_iota(jnp.int32, (16, 1), 0) < 12
+    for rows, out, each, lanes, first in (
+        (rgb_rows, rgb_w, rgb_taps, 128, True),
+        (one_rows, one_w, one_taps, 64, False),
+    ):
         small[...] = jnp.zeros_like(small)
         for f in range(4):
             for t in range(4):
@@ -69,6 +74,10 @@
                             (i * 9 + n) * 3 : (i * 9 + n) * 3 + 3, 0:lanes
                         ]
         out[...] = small[:, 0 : 4 * lanes].astype(BF16)
+        each[...] = jnp.zeros_like(each)
+        for n in range(9):
+            v = small[n * 12 : n * 12 + 16, 0 : 4 * lanes]
+            each[n, 0:16] = jnp.where(mine, v, 0.0).astype(BF16)
     for c in loads:
         c.wait()
 
@@ -84,13 +93,15 @@
 
 def cut_rows(own, left, right, first, last, rows):
     low = ROWS - HALO
+    gx, nx = lax.axis_index("gx"), lax.axis_size("gx")
+    inside = (jnp.where(gx > 0, 1.0, 0.0).astype(F32), jnp.where(gx < nx - 1, 1.0, 0.0).astype(F32))
     for t in range(4):
         for y in range(HALO):
             rows[0, t, pl.ds(HALO * HALO + y, COLS, HALO), :] = own[t, y].astype(F32)
             rows[1, t, pl.ds(HALO * HALO + y, COLS, HALO), :] = own[t, low + y].astype(F32)
-        for ref, start in ((left, 0), (right, HALO + COLS)):
+        for ref, start, good in ((left, 0, inside[0]), (right, HALO + COLS, inside[1])):
             for x in range(HALO):
-                v = ref[x, t].astype(F32)
+                v = ref[x, t].astype(F32) * good
                 at = (start + x) * HALO
                 rows[0, t, at : at + HALO, :] = v[0:HALO]
                 rows[1, t, at : at + HALO, :] = v[low:ROWS]
@@ -99,7 +110,7 @@
 
 
 def kernel(
-    own, left, right, top, bottom, w1, w2, sec, rgb_w, one_w, head,
+    own, left, right, top, bottom, w1, w2, sec, rgb_w, one_w, rgb_taps, one_taps, head,
     out_ref, logit_ref,
     field, pre1, pre2, pref, taps, valid, valid_s, part, pix, mid, line, edge,
 ):
@@ -122,17 +133,14 @@
     validity(valid, TALL, HALO)
     validity(valid_s, SHORT, 2)
 
-    def spread(count, stride, tiles, mask=None):
+    def spread(count, stride, tiles, source=None):
         step = 96
 
         def body(n, _):
             r = pl.multiple_of(n * step, 32)
             for j in range(3):
-                good = None if mask is None else mask[pl.ds(r + j, step), :] > 0
                 for t in range(tiles):
-                    v = field[t, pl.ds(r + j, step), :]
-                    if good is not None:
-                        v = jnp.where(good, v, 0.0)
+                    v = field[t, pl.ds(r + j, step), :] if source is None else source[pl.ds(r + j, step), :]
                     taps[j, pl.ds(r, step), t * 128 : t * 128 + 128] = v.astype(BF16)
             return 0
 
@@ -167,16 +175,17 @@
         return 0
 
     lax.fori_loop(0, ROWS, place, 0, unroll=4)
+    one = lambda test: jnp.where(test, 1.0, 0.0).astype(F32)
     for t in range(4):
         for x in range(HALO):
-            for ref, start in ((left, 0), (right, HALO + COLS)):
+            for ref, start, good in ((left, 0, one(gx > 0)), (right, HALO + COLS, one(gx < nx - 1))):
                 at = (start + x) * TALL + HALO
-                field[t, at : at + ROWS, :] = ref[x, t].astype(F32)
-        for n, (ref, y) in enumerate(((top, 0), (bottom, HALO + ROWS))):
-            edge[n, t] = ref[t].astype(F32)
+                field[t, at : at + ROWS, :] = ref[x, t].astype(F32) * good
+        for n, (ref, y, good) in enumerate(((top, 0, one(gy > 0)), (bottom, HALO + ROWS, one(gy < ny - 1)))):
+            edge[n, t] = ref[t].astype(F32) * good
             for x in range(WIDE):
                 field[t, x * TALL + y : x * TALL + y + HALO, :] = edge[n, t, x * HALO : x * HALO + HALO, :]
-    spread(WIDE, TALL, 4, valid)
+    spread(WIDE, TALL, 4)
 
     def decode(w, pre, h, columns):
         rows = columns * TALL
@@ -223,34 +232,22 @@
             total = v if total is None else total + v
         return total
 
-    def gather_taps(count, h, flip):
+    def gather_taps(count, h, flip, stride):
         off = (HALO - h) * (TALL + 1)
         turn = lambda size: lambda n: (128 - size * (2 - n if flip else n)) % 128
         sum_columns(part, count, turn(12))
-        rows = 6 * TALL
-        lane = lax.broadcasted_iota(jnp.int32, (rows, 128), 1)
+        lane = lax.broadcasted_iota(jnp.int32, (stride, 128), 1)
 
         def body(n, _):
-            base = pl.multiple_of(n * rows, 8)
-            total = sum_rows(base, rows, turn(36))
-            good = (valid[pl.ds(base + off, rows), :] > 0) & (lane < 12)
-            pix[pl.ds(base, rows), :] = jnp.where(good, total, 0.0).astype(BF16).astype(F32)
+            for c in range(6):
+                x = jnp.minimum(n * 6 + c, count - 1)
+                base = pl.multiple_of(x * TALL, 8)
+                total = sum_rows(base, stride, turn(36))
+                good = (valid[pl.ds(base + off, stride), :] > 0) & (lane < 12)
+                pix[pl.ds(pl.multiple_of(x * stride, 8), stride), :] = jnp.where(good, total, 0.0)
             return 0
 
         lax.fori_loop(0, -(-count // 6), body, 0)
-
-    def scatter_taps(count, stride, flip):
-        turn = lambda size: lambda n: size * (2 - n if flip else n)
-        sum_columns(pix, count, turn(12))
-
-        def body(n, _):
-            for c in range(4):
-                x = n * 4 + c
-                v = sum_rows(pl.multiple_of(x * TALL, 8), stride, turn(36))
-                taps[0, pl.ds(pl.multiple_of(x * stride, 16), stride), 0:128] = v.astype(BF16)
-            return 0
-
-        lax.fori_loop(0, count // 4, body, 0)
 
     def rgb_part(n, _):
         rows = 16 * TALL
@@ -260,15 +257,15 @@
         return 0
 
     lax.fori_loop(0, width(8) // 16, rgb_part, 0)
-    gather_taps(width(7), 7, False)
-
-    scatter_taps(width(6), TALL, False)
+    gather_taps(width(7), 7, False, TALL)
+
+    spread(width(7), TALL, 1, pix)
 
     def first(n, _):
         rows = 14 * TALL
         base = pl.multiple_of(n * rows, 16)
         good = valid[pl.ds(base + 4 * (TALL + 1), rows), :] > 0
-        v = dot(taps[0, pl.ds(base, rows), 0:128], one_w[...])
+        v = dot(operand(base, rows, TALL, (0, 1)), stack(one_taps))
         for t in range(2):
             p = v[:, t * 128 : t * 128 + 128]
             pref[t, pl.ds(base, rows), :] = p
@@ -321,10 +318,11 @@
         return 0
 
     lax.fori_loop(0, 2, second_back, 0)
-    gather_taps(width(3), 3, True)
-
-    scatter_taps(width(2), SHORT, True)
-    back = dot(taps[0, 0 : width(2) * SHORT, 0:128], rgb_w[...])
+    gather_taps(width(3), 3, True, SHORT)
+
+    spread(width(3), SHORT, 1, pix)
+    flipped = jnp.concatenate([rgb_taps[8 - n] for n in range(9)], 0)
+    back = dot(operand(0, width(2) * SHORT, SHORT, (0, 1)), flipped)
     for t in range(4):
         for x in range(width(2)):
             p = pre2[t, pl.ds((x + 6) * TALL + 6, SHORT), :]
@@ -390,12 +388,12 @@
     rgb_rows = jnp.swapaxes(to_rgb, 3, 4).reshape(81, 128).astype(F32)
     one_rows = jnp.pad(disc_one.reshape(81, 64).astype(F32), ((0, 0), (0, 64)))
     p = WIDE * TALL + PAD
-    shapes = [(2, 9, 256, 256), (2, 9, 256, 256), (9, 256, 512), (128, 512), (128, 256)]
+    shapes = [(2, 9, 256, 256), (2, 9, 256, 256), (9, 256, 512), (128, 512), (128, 256), (9, 128, 512), (9, 128, 256)]
     weights = pl.pallas_call(
         lay_out,
         out_shape=[jax.ShapeDtypeStruct(n, BF16) for n in shapes],
         in_specs=[hbm, hbm, hbm, vmem, vmem],
-        out_specs=[vmem] * 5,
+        out_specs=[vmem] * 7,
         scratch_shapes=[pltpu.VMEM((128, 512), F32), pltpu.SemaphoreType.DMA((24,))],
         compiler_params=pltpu.CompilerParams(vmem_limit_bytes=16 << 20),
         cost_estimate=pl.CostEstimate(flops=0, bytes_accessed=12 << 20, transcendentals=0),
@@ -406,7 +404,7 @@
             jax.ShapeDtypeStruct((4, ROWS, COLS, 128), BF16),
             jax.ShapeDtypeStruct((4, COLS, ROWS), BF16),
         ],
-        in_specs=[vmem] * 11,
+        in_specs=[vmem] * 13,
         out_specs=[vmem, vmem],
         scratch_shapes=[
             pltpu.VMEM((4, p, 128), F32),

time: 67.9 us -> 66.5 us (0.979)
  Pallas kernels: 42.6 us -> 41.3 us
    pallas_call x1, Pallas kernels: 40.5 us -> 39.2 us  [per_device(): pl.pallas_call(kernel, out_shape=[jax.ShapeDtypeStruct((4, ROWS, COLS, 12...]
where the time goes in v5:
time: 66.5 us; the launch traced here: 66.1 us
  Pallas kernels  41.3 us (62%)
  waiting for transfers between devices  9.57 us (14%)
  starting transfers between devices  8.64 us (13%)
  local copies, waits for them, and re-layouts  5.14 us (8%)
  other arithmetic  0.76 us (1%)
  between operations  0.7 us (1%)
    pallas_call x1, Pallas kernels, per_device(): pl.pallas_call(kernel, out_shape=[jax.ShapeDtypeStruct((4, ROWS, COLS, 12...  39.2 us
    ppermute x2, waiting for transfers between devices, exchange(): before = lax.ppermute(last, axis, [(i, (i + 1) % n) for i in range(n)])  5.6 us
    ppermute x2, starting transfers between devices, exchange(): before = lax.ppermute(last, axis, [(i, (i + 1) % n) for i in range(n)])  5.42 us
    unnamed x12, local copies, waits for them, and re-layouts  4.34 us
    ppermute x2, waiting for transfers between devices, exchange(): after = lax.ppermute(first, axis, [((i + 1) % n, i) for i in range(n)])  3.97 us
    ppermute x2, starting transfers between devices, exchange(): after = lax.ppermute(first, axis, [((i + 1) % n, i) for i in range(n)])  3.22 us
    pallas_call x1, Pallas kernels, per_device(): pl.pallas_call(lay_out, out_shape=[jax.ShapeDtypeStruct(n, BF16) for n in...  1.64 us
  transfers between devices with their start and end apart: 4, of which 2 were waited for; matrix products, arithmetic and copies ran while one was open for 2% of the time, Pallas kernels for 2%

profile of v5, /device:TPU:7, one launch (start us, length us, event | category | flops | bytes accessed | tf_op | source)
XLA Modules:
  0.0 66.1 jit_solution(3380210436903708910)
XLA Ops:
  0.6 0.0 copy-start.5
  0.6 0.0 copy-start
  0.6 1.0 %copy-done = bf16[1,4,24,16,128]{4,3,2,1,0:T(8,128)(2,1)S(1)} copy-done((bf16[1,4,24,16,128]{4,3,2,1,0:T(8,128)(2,1)S(1)}, bf16[1,4,24,16,128]{4,3,2,1,0:T(8,128)(2,1)}, u32[]{:S(2)}) %copy-start) | copy-done | bytes 393240
  1.6 0.0 copy-start.1
  1.6 0.3 shard_map.86
  2.0 1.7 %collective-permute-start = (bf16[10,4,24,128]{3,2,1,0:T(8,128)(2,1)S(1)}, bf16[10,4,24,128]{3,2,1,0:T(8,128)(2,1)S(1)}, u32[]{:S(2)}, u32[]{:S(2)}) collective-permute-start(bf16[10,4,24,128]{3,2,1,0:T(8,128)(2,1)S(1)} %get-tuple-element.15), channel_id=1, source_target_pairs={{0,1},{1,2},{2,3},{3,4},{4,5},{5,6},{6,7},{7,0},{8,9},{9,10},{10,1... | collective-permute-start | bytes 737288 | tf_op jit(solution)/shard_map/ppermute | solution.py:365
  3.7 3.2 %collective-permute-start.1 = (bf16[10,4,24,128]{3,2,1,0:T(8,128)(2,1)S(1)}, bf16[10,4,24,128]{3,2,1,0:T(8,128)(2,1)S(1)}, u32[]{:S(2)}, u32[]{:S(2)}) collective-permute-start(bf16[10,4,24,128]{3,2,1,0:T(8,128)(2,1)S(1)} %get-tuple-element.16), channel_id=1, source_target_pairs={{1,0},{2,1},{3,2},{4,3},{5,4},{6,5},{7,6},{0,7},{9,8},{10,9},{11,1... | collective-permute-start | bytes 737288 | tf_op jit(solution)/shard_map/ppermute | solution.py:366
  6.9 5.6 %collective-permute-done.left = bf16[10,4,24,128]{3,2,1,0:T(8,128)(2,1)S(1)} collective-permute-done((bf16[10,4,24,128]{3,2,1,0:T(8,128)(2,1)S(1)}, bf16[10,4,24,128]{3,2,1,0:T(8,128)(2,1)S(1)}, u32[]{:S(2)}, u32[]{:S(2)}) %collective-permute-start) | collective-permute-done | bytes 245792 | tf_op jit(solution)/shard_map/ppermute | solution.py:365
  12.5 0.0 collective-permute-done.1.right
  12.5 0.2 shard_map.87
  12.7 3.7 %collective-permute-start.2 = (bf16[4,360,128]{2,1,0:T(8,128)(2,1)S(1)}, bf16[4,360,128]{2,1,0:T(8,128)(2,1)S(1)}, u32[]{:S(2)}, u32[]{:S(2)}) collective-permute-start(bf16[4,360,128]{2,1,0:T(8,128)(2,1)S(1)} %get-tuple-element.17), channel_id=1, source_target_pairs={{0,8},{8,16},{16,24},{24,32},{32,40},{40,48},{48,56},{56,64},{64,7... | collective-permute-start | bytes 1105928 | tf_op jit(solution)/shard_map/ppermute | solution.py:365
  16.4 0.0 collective-permute-start.3
  16.4 0.8 %convert_element_type.16 = bf16[81,64]{1,0:T(8,128)(2,1)S(1)} reshape(bf16[3,3,3,3,64]{4,3,2,1,0:T(4,128)(2,1)} %param.11) | data formatting | bytes 20736 | tf_op jit(solution)/shard_map/convert_element_type | solution.py:389
  17.2 0.8 %convert_bitcast_fusion = f32[3,3,3,3,128]{4,3,2,1,0:T(4,128)S(1)} fusion(bf16[3,3,3,128,3]{3,4,2,1,0:T(4,128)(2,1)} %param.10), kind=kLoop, calls=%fused_computation | loop fusion | flops 10368 | bytes 62208 | tf_op jit(solution)/shard_map/convert_element_type | solution.py:388
  18.0 0.0 copy-start.2
  18.0 1.2 %copy-done.2 = bf16[3,3,3,128,128]{4,3,2,1,0:T(8,128)(2,1)S(1)} copy-done((bf16[3,3,3,128,128]{4,3,2,1,0:T(8,128)(2,1)S(1)}, bf16[3,3,3,128,128]{4,3,2,1,0:T(8,128)(2,1)}, u32[]{:S(2)}) %copy-start.2) | copy-done | bytes 884760
  19.1 1.2 %copy-done.3 = bf16[3,3,3,128,128]{4,3,2,1,0:T(8,128)(2,1)S(1)} copy-done((bf16[3,3,3,128,128]{4,3,2,1,0:T(8,128)(2,1)S(1)}, bf16[3,3,3,128,128]{4,3,2,1,0:T(8,128)(2,1)}, u32[]{:S(2)}) %copy-start.3) | copy-done | bytes 884760
  20.3 1.0 %copy-done.4 = bf16[3,3,3,64,128]{4,3,2,1,0:T(8,128)(2,1)S(1)} copy-done((bf16[3,3,3,64,128]{4,3,2,1,0:T(8,128)(2,1)S(1)}, bf16[3,3,3,64,128]{4,3,2,1,0:T(8,128)(2,1)}, u32[]{:S(2)}) %copy-start.4) | copy-done | bytes 442392
  21.3 1.6 %shard_map.88 = (bf16[2,9,256,256]{3,2,1,0:T(8,128)(2,1)S(1)}, bf16[2,9,256,256]{3,2,1,0:T(8,128)(2,1)S(1)}, bf16[9,256,512]{2,1,0:T(8,128)(2,1)S(1)}, bf16[128,...) custom-call(bf16[3,9,128,128]{3,2,1,0:T(8,128)(2,1)S(1)} %bitcast.14, ...), custom_call_target="tpu_custom_call" | custom-call | bytes 12582912 | tf_op jit(solution)/shard_map/pallas_call | solution.py:392
  23.0 0.0 collective-permute-done.2.top
  23.0 4.0 %collective-permute-done.3.bottom = bf16[4,360,128]{2,1,0:T(8,128)(2,1)S(1)} collective-permute-done((bf16[4,360,128]{2,1,0:T(8,128)(2,1)S(1)}, bf16[4,360,128]{2,1,0:T(8,128)(2,1)S(1)}, u32[]{:S(2)}, u32[]{:S(2)}) %collective-permute-start.3) | collective-permute-done | bytes 368672 | tf_op jit(solution)/shard_map/ppermute | solution.py:366
  27.0 0.0 copy-done.5
  27.0 0.0 copy-done.1
  27.0 39.2 %shard_map.89 = (bf16[4,24,16,128]{3,2,1,0:T(8,128)(2,1)}, bf16[4,16,24]{2,1,0:T(8,128)(2,1)}) custom-call(bf16[4,24,16,128]{3,2,1,0:T(8,128)(2,1)S(1)} %bitcast.13, bf16[10,4,24,128]{3,2,1,0:T(8,128)(2,1)S(1)} %collective-permute-done.left, bf16[10,4,24,128]{3,2,1,0:T(8,128)(2,1)S(1)} %collective-permute-done.1.right, ...), custom_call_target="tpu_custom_call" | custom-call | tf_op jit(solution)/shard_map/pallas_call | solution.py:401
  (4 shorter events, 0.0 us)
Async XLA Ops:
  0.6 26.3 %copy-start.5 = (f32[128]{0:T(128)S(1)}, f32[128]{0:T(128)}, u32[]{:S(2)}) copy-start(f32[128]{0:T(128)} %param.13) | copy-start | bytes 1540
  0.6 1.0 %copy-start = (bf16[1,4,24,16,128]{4,3,2,1,0:T(8,128)(2,1)S(1)}, bf16[1,4,24,16,128]{4,3,2,1,0:T(8,128)(2,1)}, u32[]{:S(2)}) copy-start(bf16[1,4,24,16,128]{4,3,2,1,0:T(8,128)(2,1)} %param.7) | copy-start | bytes 1179652
  1.6 25.3 %copy-start.1 = (bf16[1,4,24,16,128]{4,3,2,1,0:T(8,128)(2,1)S(1)}, bf16[1,4,24,16,128]{4,3,2,1,0:T(8,128)(2,1)}, u32[]{:S(2)}) copy-start(bf16[1,4,24,16,128]{4,3,2,1,0:T(8,128)(2,1)} %param.7) | copy-start | bytes 1179652
  2.0 10.5 %collective-permute-start = (bf16[10,4,24,128]{3,2,1,0:T(8,128)(2,1)S(1)}, bf16[10,4,24,128]{3,2,1,0:T(8,128)(2,1)S(1)}, u32[]{:S(2)}, u32[]{:S(2)}) collective-permute-start(bf16[10,4,24,128]{3,2,1,0:T(8,128)(2,1)S(1)} %get-tuple-element.15), channel_id=1, source_target_pairs={{0,1},{1,2},{2,3},{3,4},{4,5},{5,6},{6,7},{7,0},{8,9},{9,10},{10,1... | collective-permute-start | bytes 737288 | tf_op jit(solution)/shard_map/ppermute | solution.py:365
  3.7 8.8 %collective-permute-start.1 = (bf16[10,4,24,128]{3,2,1,0:T(8,128)(2,1)S(1)}, bf16[10,4,24,128]{3,2,1,0:T(8,128)(2,1)S(1)}, u32[]{:S(2)}, u32[]{:S(2)}) collective-permute-start(bf16[10,4,24,128]{3,2,1,0:T(8,128)(2,1)S(1)} %get-tuple-element.16), channel_id=1, source_target_pairs={{1,0},{2,1},{3,2},{4,3},{5,4},{6,5},{7,6},{0,7},{9,8},{10,9},{11,1... | collective-permute-start | bytes 737288 | tf_op jit(solution)/shard_map/ppermute | solution.py:366
  12.7 10.3 %collective-permute-start.2 = (bf16[4,360,128]{2,1,0:T(8,128)(2,1)S(1)}, bf16[4,360,128]{2,1,0:T(8,128)(2,1)S(1)}, u32[]{:S(2)}, u32[]{:S(2)}) collective-permute-start(bf16[4,360,128]{2,1,0:T(8,128)(2,1)S(1)} %get-tuple-element.17), channel_id=1, source_target_pairs={{0,8},{8,16},{16,24},{24,32},{32,40},{40,48},{48,56},{56,64},{64,7... | collective-permute-start | bytes 1105928 | tf_op jit(solution)/shard_map/ppermute | solution.py:365
  16.4 10.6 %collective-permute-start.3 = (bf16[4,360,128]{2,1,0:T(8,128)(2,1)S(1)}, bf16[4,360,128]{2,1,0:T(8,128)(2,1)S(1)}, u32[]{:S(2)}, u32[]{:S(2)}) collective-permute-start(bf16[4,360,128]{2,1,0:T(8,128)(2,1)S(1)} %get-tuple-element.18), channel_id=1, source_target_pairs={{8,0},{16,8},{24,16},{32,24},{40,32},{48,40},{56,48},{64,56},{72,6... | collective-permute-start | bytes 1105928 | tf_op jit(solution)/shard_map/ppermute | solution.py:366
  18.0 1.2 %copy-start.2 = (bf16[3,3,3,128,128]{4,3,2,1,0:T(8,128)(2,1)S(1)}, bf16[3,3,3,128,128]{4,3,2,1,0:T(8,128)(2,1)}, u32[]{:S(2)}) copy-start(bf16[3,3,3,128,128]{4,3,2,1,0:T(8,128)(2,1)} %param.8) | copy-start | bytes 2654212
  19.1 1.2 %copy-start.3 = (bf16[3,3,3,128,128]{4,3,2,1,0:T(8,128)(2,1)S(1)}, bf16[3,3,3,128,128]{4,3,2,1,0:T(8,128)(2,1)}, u32[]{:S(2)}) copy-start(bf16[3,3,3,128,128]{4,3,2,1,0:T(8,128)(2,1)} %param.9) | copy-start | bytes 2654212
  20.3 1.0 %copy-start.4 = (bf16[3,3,3,64,128]{4,3,2,1,0:T(8,128)(2,1)S(1)}, bf16[3,3,3,64,128]{4,3,2,1,0:T(8,128)(2,1)}, u32[]{:S(2)}) copy-start(bf16[3,3,3,64,128]{4,3,2,1,0:T(8,128)(2,1)} %param.12) | copy-start | bytes 1327108

commit v6 on v5

--- a/solution.py
+++ b/solution.py
@@ -36,9 +36,9 @@
     return s * (1.0 + v * (1.0 - s))
 
 
-def lay_out(k1, k2, ks, rgb_rows, one_rows, w1, w2, sec, rgb_w, one_w, rgb_taps, one_taps, small, sems):
+def lay_out(k1, k2, ks, rgb_rows, one_rows, wide, sec, rgb_w, one_w, rgb_taps, one_taps, small, sems):
     loads = []
-    for k, w in ((k1, w1), (k2, w2)):
+    for k, w in ((k1, wide.at[0]), (k2, wide.at[1])):
         for far in range(2):
             for f in range(2):
                 for t in range(2):
@@ -110,9 +110,9 @@
 
 
 def kernel(
-    own, left, right, top, bottom, w1, w2, sec, rgb_w, one_w, rgb_taps, one_taps, head,
+    own, left, right, top, bottom, wide, sec, rgb_w, one_w, rgb_taps, one_taps, head,
     out_ref, logit_ref,
-    field, pre1, pre2, pref, taps, valid, valid_s, part, pix, mid, line, edge,
+    field, pre, res, pref, taps, valid, valid_s, part, pix, mid, line, edge,
 ):
     gy, gx = lax.axis_index("gy"), lax.axis_index("gx")
     ny, nx = lax.axis_size("gy"), lax.axis_size("gx")
@@ -187,27 +187,31 @@
                 field[t, x * TALL + y : x * TALL + y + HALO, :] = edge[n, t, x * HALO : x * HALO + HALO, :]
     spread(WIDE, TALL, 4)
 
-    def decode(w, pre, h, columns):
-        rows = columns * TALL
-        off = (HALO - h) * (TALL + 1)
+    def decode(k, _):
+        rows = 17 * TALL
+        off = (k + 1) * (TALL + 1)
 
         def body(n, _):
             base = pl.multiple_of(n * rows, 16)
             good = valid[pl.ds(base + off, rows), :] > 0
             near, far = operand(base, rows, TALL, (0, 2)), operand(base, rows, TALL, (2, 4))
-            low = dot(near, stack(w.at[0]))
-            high = dot(near, stack(w.at[1])) + dot(far, stack(w.at[0]))
+            low = dot(near, stack(wide.at[k, 0]))
+            high = dot(near, stack(wide.at[k, 1])) + dot(far, stack(wide.at[k, 0]))
             for t, (v, s) in enumerate(((low, 0), (low, 128), (high, 0), (high, 128))):
                 v = v[:, s : s + 128]
-                pre[t, pl.ds(base, rows), :] = v
+                pre[k, t, pl.ds(base, rows), :] = v
                 field[t, pl.ds(base, rows), :] = jnp.where(good, silu(v), 0.0)
             return 0
 
-        lax.fori_loop(0, width(h) // columns, body, 0)
-
-    decode(w1, pre1, 9, 17)
-    spread(width(9), TALL, 4)
-    decode(w2, pre2, 8, 16)
+        lax.fori_loop(0, 2, body, 0)
+
+        @pl.when(k == 0)
+        def _():
+            spread(width(9), TALL, 4)
+
+        return 0
+
+    lax.fori_loop(0, 2, decode, 0)
 
     def sum_columns(src, count, turn):
         rows = 6 * TALL
@@ -324,34 +328,48 @@
     flipped = jnp.concatenate([rgb_taps[8 - n] for n in range(9)], 0)
     back = dot(operand(0, width(2) * SHORT, SHORT, (0, 1)), flipped)
     for t in range(4):
-        for x in range(width(2)):
-            p = pre2[t, pl.ds((x + 6) * TALL + 6, SHORT), :]
-            g = back[x * SHORT : (x + 1) * SHORT, t * 128 : t * 128 + 128] * dsilu(p)
-            good = valid_s[pl.ds(x * SHORT, SHORT), :] > 0
-            field[t, pl.ds(x * SHORT, SHORT), :] = jnp.where(good, g, 0.0)
-    spread(width(2), SHORT, 4)
-
-    def back_conv(w, count):
-        rows = count * SHORT
+        res[t] = back[:, t * 128 : t * 128 + 128]
+
+    def temper(k, h):
+        away = 9 - k - h
+
+        def body(x, _):
+            base = pl.multiple_of(x * SHORT, 8)
+            good = valid_s[pl.ds((x + 2 - h) * SHORT + 2 - h, SHORT), :] > 0
+            for t in range(4):
+                p = pre[k, t, pl.ds((x + away) * TALL + away, SHORT), :]
+                g = res[t, pl.ds(base, SHORT), :] * dsilu(p)
+                field[t, pl.ds(base, SHORT), :] = jnp.where(good, g, 0.0)
+            return 0
+
+        lax.fori_loop(0, width(h), body, 0, unroll=2)
+
+    temper(1, 2)
+
+    def back_conv(n, _):
+        rows = width(1) * SHORT
+        spread(width(2), SHORT, 4)
+        k = 1 - n
         near, far = operand(0, rows, SHORT, (0, 2)), operand(0, rows, SHORT, (2, 4))
-        high = dot_t(far, across(w.at[0]))
-        low = dot_t(far, across(w.at[1])) + dot_t(near, across(w.at[0]))
-        return [v[:, s : s + 128] for v in (low, high) for s in (0, 128)]
-
-    back = back_conv(w2, width(1))
-    for t in range(4):
-        for x in range(width(1)):
-            p = pre1[t, pl.ds((x + 8) * TALL + 8, SHORT), :]
-            g = back[t][x * SHORT : (x + 1) * SHORT] * dsilu(p)
-            good = valid_s[pl.ds((x + 1) * SHORT + 1, SHORT), :] > 0
-            field[t, pl.ds(x * SHORT, SHORT), :] = jnp.where(good, g, 0.0)
-    spread(width(1), SHORT, 4)
-    back = back_conv(w1, width(0))
-    for t in range(4):
-        field[t, 0 : COLS * SHORT, :] = back[t]
-    for t in range(4):
-        for y in range(ROWS):
-            out_ref[t, y] = field[t, pl.ds(y, COLS, SHORT), :].astype(BF16)
+        high = dot_t(far, across(wide.at[k, 0]))
+        low = dot_t(far, across(wide.at[k, 1])) + dot_t(near, across(wide.at[k, 0]))
+        for t, (v, s) in enumerate(((low, 0), (low, 128), (high, 0), (high, 128))):
+            res[t, 0:rows, :] = v[:, s : s + 128]
+
+        @pl.when(n == 0)
+        def _():
+            temper(0, 1)
+
+        return 0
+
+    lax.fori_loop(0, 2, back_conv, 0)
+
+    def emit(y, _):
+        for t in range(4):
+            out_ref[t, y] = res[t, pl.ds(y, COLS, SHORT), :].astype(BF16)
+        return 0
+
+    lax.fori_loop(0, ROWS, emit, 0, unroll=4)
 
 
 def per_device(latent, conv_one, conv_two, to_rgb, disc_one, disc_two, disc_head):
@@ -388,12 +406,12 @@
     rgb_rows = jnp.swapaxes(to_rgb, 3, 4).reshape(81, 128).astype(F32)
     one_rows = jnp.pad(disc_one.reshape(81, 64).astype(F32), ((0, 0), (0, 64)))
     p = WIDE * TALL + PAD
-    shapes = [(2, 9, 256, 256), (2, 9, 256, 256), (9, 256, 512), (128, 512), (128, 256), (9, 128, 512), (9, 128, 256)]
+    shapes = [(2, 2, 9, 256, 256), (9, 256, 512), (128, 512), (128, 256), (9, 128, 512), (9, 128, 256)]
     weights = pl.pallas_call(
         lay_out,
         out_shape=[jax.ShapeDtypeStruct(n, BF16) for n in shapes],
         in_specs=[hbm, hbm, hbm, vmem, vmem],
-        out_specs=[vmem] * 7,
+        out_specs=[vmem] * 6,
         scratch_shapes=[pltpu.VMEM((128, 512), F32), pltpu.SemaphoreType.DMA((24,))],
         compiler_params=pltpu.CompilerParams(vmem_limit_bytes=16 << 20),
         cost_estimate=pl.CostEstimate(flops=0, bytes_accessed=12 << 20, transcendentals=0),
@@ -404,12 +422,12 @@
             jax.ShapeDtypeStruct((4, ROWS, COLS, 128), BF16),
             jax.ShapeDtypeStruct((4, COLS, ROWS), BF16),
         ],
-        in_specs=[vmem] * 13,
+        in_specs=[vmem] * 12,
         out_specs=[vmem, vmem],
         scratch_shapes=[
             pltpu.VMEM((4, p, 128), F32),
-            pltpu.VMEM((4, p, 128), F32),
-            pltpu.VMEM((4, p, 128), F32),
+            pltpu.VMEM((2, 4, p, 128), F32),
+            pltpu.VMEM((4, (COLS + 4) * SHORT, 128), F32),
             pltpu.VMEM((2, p, 128), F32),
             pltpu.VMEM((3, p, 512), BF16),
             pltpu.VMEM((p, 128), F32),
@@ -420,7 +438,7 @@
             pltpu.VMEM((4, COLS, 128), F32),
             pltpu.VMEM((2, 4, WIDE * HALO, 128), F32),
         ],
-        compiler_params=pltpu.CompilerParams(vmem_limit_bytes=34 << 20),
+        compiler_params=pltpu.CompilerParams(vmem_limit_bytes=36 << 20),
     )(x, left, right, top, bottom, *weights, disc_head.reshape(1, 128))
     return out[None], jnp.swapaxes(logits, 1, 2)[None]
 

time: 66.5 us -> 64.4 us (0.968)
  Pallas kernels: 41.3 us -> 39.2 us
    pallas_call x1, Pallas kernels: 39.2 us -> 37.1 us  [per_device(): pl.pallas_call(kernel, out_shape=[jax.ShapeDtypeStruct((4, ROWS, COLS, 12...]
  transfers between devices with their start and end apart: 4 -> 4, of which waited for: 2 -> 2; matrix products, arithmetic and copies ran while one was open for 2% -> 2% of each run, Pallas kernels for 2% -> 3%
where the time goes in v6:
time: 64.4 us; the launch traced here: 64.1 us
  Pallas kernels  39.2 us (61%)
  waiting for transfers between devices  9.57 us (15%)
  starting transfers between devices  8.64 us (13%)
  local copies, waits for them, and re-layouts  5.14 us (8%)
  other arithmetic  0.76 us (1%)
  between operations  0.7 us (1%)
    pallas_call x1, Pallas kernels, per_device(): pl.pallas_call(kernel, out_shape=[jax.ShapeDtypeStruct((4, ROWS, COLS, 12...  37.1 us
    ppermute x2, waiting for transfers between devices, exchange(): before = lax.ppermute(last, axis, [(i, (i + 1) % n) for i in range(n)])  5.6 us
    ppermute x2, starting transfers between devices, exchange(): before = lax.ppermute(last, axis, [(i, (i + 1) % n) for i in range(n)])  5.42 us
    unnamed x12, local copies, waits for them, and re-layouts  4.34 us
    ppermute x2, waiting for transfers between devices, exchange(): after = lax.ppermute(first, axis, [((i + 1) % n, i) for i in range(n)])  3.97 us
    ppermute x2, starting transfers between devices, exchange(): after = lax.ppermute(first, axis, [((i + 1) % n, i) for i in range(n)])  3.22 us
    pallas_call x1, Pallas kernels, per_device(): pl.pallas_call(lay_out, out_shape=[jax.ShapeDtypeStruct(n, BF16) for n in...  1.64 us
  transfers between devices with their start and end apart: 4, of which 2 were waited for; matrix products, arithmetic and copies ran while one was open for 2% of the time, Pallas kernels for 3%

profile of v6, /device:TPU:7, one launch (start us, length us, event | category | flops | bytes accessed | tf_op | source)
XLA Modules:
  0.0 64.1 jit_solution(6029656872314982852)
XLA Ops:
  0.6 0.0 copy-start.5
  0.6 0.0 copy-start
  0.6 1.0 %copy-done = bf16[1,4,24,16,128]{4,3,2,1,0:T(8,128)(2,1)S(1)} copy-done((bf16[1,4,24,16,128]{4,3,2,1,0:T(8,128)(2,1)S(1)}, bf16[1,4,24,16,128]{4,3,2,1,0:T(8,128)(2,1)}, u32[]{:S(2)}) %copy-start) | copy-done | bytes 393240
  1.6 0.0 copy-start.1
  1.6 0.3 shard_map.86
  2.0 1.7 %collective-permute-start = (bf16[10,4,24,128]{3,2,1,0:T(8,128)(2,1)S(1)}, bf16[10,4,24,128]{3,2,1,0:T(8,128)(2,1)S(1)}, u32[]{:S(2)}, u32[]{:S(2)}) collective-permute-start(bf16[10,4,24,128]{3,2,1,0:T(8,128)(2,1)S(1)} %get-tuple-element.14), channel_id=1, source_target_pairs={{0,1},{1,2},{2,3},{3,4},{4,5},{5,6},{6,7},{7,0},{8,9},{9,10},{10,1... | collective-permute-start | bytes 737288 | tf_op jit(solution)/shard_map/ppermute | solution.py:383
  3.7 3.2 %collective-permute-start.1 = (bf16[10,4,24,128]{3,2,1,0:T(8,128)(2,1)S(1)}, bf16[10,4,24,128]{3,2,1,0:T(8,128)(2,1)S(1)}, u32[]{:S(2)}, u32[]{:S(2)}) collective-permute-start(bf16[10,4,24,128]{3,2,1,0:T(8,128)(2,1)S(1)} %get-tuple-element.15), channel_id=1, source_target_pairs={{1,0},{2,1},{3,2},{4,3},{5,4},{6,5},{7,6},{0,7},{9,8},{10,9},{11,1... | collective-permute-start | bytes 737288 | tf_op jit(solution)/shard_map/ppermute | solution.py:384
  6.9 5.6 %collective-permute-done.left = bf16[10,4,24,128]{3,2,1,0:T(8,128)(2,1)S(1)} collective-permute-done((bf16[10,4,24,128]{3,2,1,0:T(8,128)(2,1)S(1)}, bf16[10,4,24,128]{3,2,1,0:T(8,128)(2,1)S(1)}, u32[]{:S(2)}, u32[]{:S(2)}) %collective-permute-start) | collective-permute-done | bytes 245792 | tf_op jit(solution)/shard_map/ppermute | solution.py:383
  12.5 0.0 collective-permute-done.1.right
  12.5 0.2 shard_map.87
  12.7 3.7 %collective-permute-start.2 = (bf16[4,360,128]{2,1,0:T(8,128)(2,1)S(1)}, bf16[4,360,128]{2,1,0:T(8,128)(2,1)S(1)}, u32[]{:S(2)}, u32[]{:S(2)}) collective-permute-start(bf16[4,360,128]{2,1,0:T(8,128)(2,1)S(1)} %get-tuple-element.16), channel_id=1, source_target_pairs={{0,8},{8,16},{16,24},{24,32},{32,40},{40,48},{48,56},{56,64},{64,7... | collective-permute-start | bytes 1105928 | tf_op jit(solution)/shard_map/ppermute | solution.py:383
  16.4 0.0 collective-permute-start.3
  16.4 0.8 %convert_element_type.16 = bf16[81,64]{1,0:T(8,128)(2,1)S(1)} reshape(bf16[3,3,3,3,64]{4,3,2,1,0:T(4,128)(2,1)} %param.11) | data formatting | bytes 20736 | tf_op jit(solution)/shard_map/convert_element_type | solution.py:407
  17.2 0.8 %convert_bitcast_fusion = f32[3,3,3,3,128]{4,3,2,1,0:T(4,128)S(1)} fusion(bf16[3,3,3,128,3]{3,4,2,1,0:T(4,128)(2,1)} %param.10), kind=kLoop, calls=%fused_computation | loop fusion | flops 10368 | bytes 62208 | tf_op jit(solution)/shard_map/convert_element_type | solution.py:406
  18.0 0.0 copy-start.2
  18.0 1.2 %copy-done.2 = bf16[3,3,3,128,128]{4,3,2,1,0:T(8,128)(2,1)S(1)} copy-done((bf16[3,3,3,128,128]{4,3,2,1,0:T(8,128)(2,1)S(1)}, bf16[3,3,3,128,128]{4,3,2,1,0:T(8,128)(2,1)}, u32[]{:S(2)}) %copy-start.2) | copy-done | bytes 884760
  19.1 1.2 %copy-done.3 = bf16[3,3,3,128,128]{4,3,2,1,0:T(8,128)(2,1)S(1)} copy-done((bf16[3,3,3,128,128]{4,3,2,1,0:T(8,128)(2,1)S(1)}, bf16[3,3,3,128,128]{4,3,2,1,0:T(8,128)(2,1)}, u32[]{:S(2)}) %copy-start.3) | copy-done | bytes 884760
  20.3 1.0 %copy-done.4 = bf16[3,3,3,64,128]{4,3,2,1,0:T(8,128)(2,1)S(1)} copy-done((bf16[3,3,3,64,128]{4,3,2,1,0:T(8,128)(2,1)S(1)}, bf16[3,3,3,64,128]{4,3,2,1,0:T(8,128)(2,1)}, u32[]{:S(2)}) %copy-start.4) | copy-done | bytes 442392
  21.3 1.6 %shard_map.88 = (bf16[2,2,9,256,256]{4,3,2,1,0:T(8,128)(2,1)S(1)}, bf16[9,256,512]{2,1,0:T(8,128)(2,1)S(1)}, bf16[128,512]{1,0:T(8,128)(2,1)S(1)}, bf16[128,256]...) custom-call(bf16[3,9,128,128]{3,2,1,0:T(8,128)(2,1)S(1)} %bitcast.14, ...), custom_call_target="tpu_custom_call" | custom-call | bytes 12582912 | tf_op jit(solution)/shard_map/pallas_call | solution.py:410
  23.0 0.0 collective-permute-done.2.top
  23.0 4.0 %collective-permute-done.3.bottom = bf16[4,360,128]{2,1,0:T(8,128)(2,1)S(1)} collective-permute-done((bf16[4,360,128]{2,1,0:T(8,128)(2,1)S(1)}, bf16[4,360,128]{2,1,0:T(8,128)(2,1)S(1)}, u32[]{:S(2)}, u32[]{:S(2)}) %collective-permute-start.3) | collective-permute-done | bytes 368672 | tf_op jit(solution)/shard_map/ppermute | solution.py:384
  27.0 0.0 copy-done.5
  27.0 0.0 copy-done.1
  27.0 37.1 %shard_map.89 = (bf16[4,24,16,128]{3,2,1,0:T(8,128)(2,1)}, bf16[4,16,24]{2,1,0:T(8,128)(2,1)}) custom-call(bf16[4,24,16,128]{3,2,1,0:T(8,128)(2,1)S(1)} %bitcast.13, bf16[10,4,24,128]{3,2,1,0:T(8,128)(2,1)S(1)} %collective-permute-done.left, bf16[10,4,24,128]{3,2,1,0:T(8,128)(2,1)S(1)} %collective-permute-done.1.right, ...), custom_call_target="tpu_custom_call" | custom-call | tf_op jit(solution)/shard_map/pallas_call | solution.py:419
  (4 shorter events, 0.0 us)
Async XLA Ops:
  0.6 26.3 %copy-start.5 = (f32[128]{0:T(128)S(1)}, f32[128]{0:T(128)}, u32[]{:S(2)}) copy-start(f32[128]{0:T(128)} %param.13) | copy-start | bytes 1540
  0.6 1.0 %copy-start = (bf16[1,4,24,16,128]{4,3,2,1,0:T(8,128)(2,1)S(1)}, bf16[1,4,24,16,128]{4,3,2,1,0:T(8,128)(2,1)}, u32[]{:S(2)}) copy-start(bf16[1,4,24,16,128]{4,3,2,1,0:T(8,128)(2,1)} %param.7) | copy-start | bytes 1179652
  1.6 25.3 %copy-start.1 = (bf16[1,4,24,16,128]{4,3,2,1,0:T(8,128)(2,1)S(1)}, bf16[1,4,24,16,128]{4,3,2,1,0:T(8,128)(2,1)}, u32[]{:S(2)}) copy-start(bf16[1,4,24,16,128]{4,3,2,1,0:T(8,128)(2,1)} %param.7) | copy-start | bytes 1179652
  2.0 10.5 %collective-permute-start = (bf16[10,4,24,128]{3,2,1,0:T(8,128)(2,1)S(1)}, bf16[10,4,24,128]{3,2,1,0:T(8,128)(2,1)S(1)}, u32[]{:S(2)}, u32[]{:S(2)}) collective-permute-start(bf16[10,4,24,128]{3,2,1,0:T(8,128)(2,1)S(1)} %get-tuple-element.14), channel_id=1, source_target_pairs={{0,1},{1,2},{2,3},{3,4},{4,5},{5,6},{6,7},{7,0},{8,9},{9,10},{10,1... | collective-permute-start | bytes 737288 | tf_op jit(solution)/shard_map/ppermute | solution.py:383
  3.7 8.8 %collective-permute-start.1 = (bf16[10,4,24,128]{3,2,1,0:T(8,128)(2,1)S(1)}, bf16[10,4,24,128]{3,2,1,0:T(8,128)(2,1)S(1)}, u32[]{:S(2)}, u32[]{:S(2)}) collective-permute-start(bf16[10,4,24,128]{3,2,1,0:T(8,128)(2,1)S(1)} %get-tuple-element.15), channel_id=1, source_target_pairs={{1,0},{2,1},{3,2},{4,3},{5,4},{6,5},{7,6},{0,7},{9,8},{10,9},{11,1... | collective-permute-start | bytes 737288 | tf_op jit(solution)/shard_map/ppermute | solution.py:384
  12.7 10.3 %collective-permute-start.2 = (bf16[4,360,128]{2,1,0:T(8,128)(2,1)S(1)}, bf16[4,360,128]{2,1,0:T(8,128)(2,1)S(1)}, u32[]{:S(2)}, u32[]{:S(2)}) collective-permute-start(bf16[4,360,128]{2,1,0:T(8,128)(2,1)S(1)} %get-tuple-element.16), channel_id=1, source_target_pairs={{0,8},{8,16},{16,24},{24,32},{32,40},{40,48},{48,56},{56,64},{64,7... | collective-permute-start | bytes 1105928 | tf_op jit(solution)/shard_map/ppermute | solution.py:383
  16.4 10.6 %collective-permute-start.3 = (bf16[4,360,128]{2,1,0:T(8,128)(2,1)S(1)}, bf16[4,360,128]{2,1,0:T(8,128)(2,1)S(1)}, u32[]{:S(2)}, u32[]{:S(2)}) collective-permute-start(bf16[4,360,128]{2,1,0:T(8,128)(2,1)S(1)} %get-tuple-element.17), channel_id=1, source_target_pairs={{8,0},{16,8},{24,16},{32,24},{40,32},{48,40},{56,48},{64,56},{72,6... | collective-permute-start | bytes 1105928 | tf_op jit(solution)/shard_map/ppermute | solution.py:384
  18.0 1.2 %copy-start.2 = (bf16[3,3,3,128,128]{4,3,2,1,0:T(8,128)(2,1)S(1)}, bf16[3,3,3,128,128]{4,3,2,1,0:T(8,128)(2,1)}, u32[]{:S(2)}) copy-start(bf16[3,3,3,128,128]{4,3,2,1,0:T(8,128)(2,1)} %param.8) | copy-start | bytes 2654212
  19.1 1.2 %copy-start.3 = (bf16[3,3,3,128,128]{4,3,2,1,0:T(8,128)(2,1)S(1)}, bf16[3,3,3,128,128]{4,3,2,1,0:T(8,128)(2,1)}, u32[]{:S(2)}) copy-start(bf16[3,3,3,128,128]{4,3,2,1,0:T(8,128)(2,1)} %param.9) | copy-start | bytes 2654212
  20.3 1.0 %copy-start.4 = (bf16[3,3,3,64,128]{4,3,2,1,0:T(8,128)(2,1)S(1)}, bf16[3,3,3,64,128]{4,3,2,1,0:T(8,128)(2,1)}, u32[]{:S(2)}) copy-start(bf16[3,3,3,64,128]{4,3,2,1,0:T(8,128)(2,1)} %param.12) | copy-start | bytes 1327108

commit v7 on v6

--- a/solution.py
+++ b/solution.py
@@ -36,7 +36,7 @@
     return s * (1.0 + v * (1.0 - s))
 
 
-def lay_out(k1, k2, ks, rgb_rows, one_rows, wide, sec, rgb_w, one_w, rgb_taps, one_taps, small, sems):
+def lay_out(k1, k2, ks, rgb_rows, one_rows, wide, sec, rgb_w, one_w, rgb_taps, one_taps, valid, valid_s, small, sems):
     loads = []
     for k, w in ((k1, wide.at[0]), (k2, wide.at[1])):
         for far in range(2):
@@ -59,6 +59,25 @@
     for c in loads:
         c.start()
 
+    gy, gx = lax.axis_index("gy"), lax.axis_index("gx")
+    ny, nx = lax.axis_size("gy"), lax.axis_size("gx")
+
+    def validity(ref, stride, h):
+        first_x, first_y = gx * COLS - h, gy * ROWS - h
+        y = first_y + lax.broadcasted_iota(jnp.int32, (stride, 128), 0)
+        good_y = jnp.where((y >= 0) & (y < ny * ROWS), 1.0, 0.0).astype(F32)
+
+        def body(x, _):
+            place = first_x + x
+            good_x = jnp.where((place >= 0) & (place < nx * COLS), 1.0, 0.0).astype(F32)
+            ref[pl.ds(pl.multiple_of(x * stride, 8), stride), :] = good_y * good_x
+            return 0
+
+        lax.fori_loop(0, width(h), body, 0)
+
+    validity(valid, TALL, HALO)
+    validity(valid_s, SHORT, 2)
+
     mine = lax.broadcasted_iota(jnp.int32, (16, 1), 0) < 12
     for rows, out, each, lanes, first in (
         (rgb_rows, rgb_w, rgb_taps, 128, True),
@@ -110,28 +129,12 @@
 
 
 def kernel(
-    own, left, right, top, bottom, wide, sec, rgb_w, one_w, rgb_taps, one_taps, head,
+    own, left, right, top, bottom, wide, sec, rgb_w, one_w, rgb_taps, one_taps, valid, valid_s, head,
     out_ref, logit_ref,
-    field, pre, res, pref, taps, valid, valid_s, part, pix, mid, line, edge,
+    field, pre, res, pref, taps, part, pix, mid, line, edge,
 ):
     gy, gx = lax.axis_index("gy"), lax.axis_index("gx")
     ny, nx = lax.axis_size("gy"), lax.axis_size("gx")
-
-    def validity(ref, stride, h):
-        first_x, first_y = gx * COLS - h, gy * ROWS - h
-        y = first_y + lax.broadcasted_iota(jnp.int32, (stride, 128), 0)
-        good_y = jnp.where((y >= 0) & (y < ny * ROWS), 1.0, 0.0).astype(F32)
-
-        def body(x, _):
-            place = first_x + x
-            good_x = jnp.where((place >= 0) & (place < nx * COLS), 1.0, 0.0).astype(F32)
-            ref[pl.ds(pl.multiple_of(x * stride, 8), stride), :] = good_y * good_x
-            return 0
-
-        lax.fori_loop(0, width(h), body, 0)
-
-    validity(valid, TALL, HALO)
-    validity(valid_s, SHORT, 2)
 
     def spread(count, stride, tiles, source=None):
         step = 96
@@ -409,9 +412,10 @@
     shapes = [(2, 2, 9, 256, 256), (9, 256, 512), (128, 512), (128, 256), (9, 128, 512), (9, 128, 256)]
     weights = pl.pallas_call(
         lay_out,
-        out_shape=[jax.ShapeDtypeStruct(n, BF16) for n in shapes],
+        out_shape=[jax.ShapeDtypeStruct(n, BF16) for n in shapes]
+        + [jax.ShapeDtypeStruct((WIDE * TALL + PAD, 128), F32)] * 2,
         in_specs=[hbm, hbm, hbm, vmem, vmem],
-        out_specs=[vmem] * 6,
+        out_specs=[vmem] * 8,
         scratch_shapes=[pltpu.VMEM((128, 512), F32), pltpu.SemaphoreType.DMA((24,))],
         compiler_params=pltpu.CompilerParams(vmem_limit_bytes=16 << 20),
         cost_estimate=pl.CostEstimate(flops=0, bytes_accessed=12 << 20, transcendentals=0),
@@ -422,7 +426,7 @@
             jax.ShapeDtypeStruct((4, ROWS, COLS, 128), BF16),
             jax.ShapeDtypeStruct((4, COLS, ROWS), BF16),
         ],
-        in_specs=[vmem] * 12,
+        in_specs=[vmem] * 14,
         out_specs=[vmem, vmem],
         scratch_shapes=[
             pltpu.VMEM((4, p, 128), F32),
@@ -433,8 +437,6 @@
             pltpu.VMEM((p, 128), F32),
             pltpu.VMEM((p, 128), F32),
             pltpu.VMEM((p, 128), F32),
-            pltpu.VMEM((p, 128), F32),
-            pltpu.VMEM((p, 128), F32),
             pltpu.VMEM((4, COLS, 128), F32),
             pltpu.VMEM((2, 4, WIDE * HALO, 128), F32),
         ],

time: 64.4 us -> 64 us (level)
  no operation moved by 1% of the time
where the time goes in v7:
time: 64 us; the launch traced here: 63.6 us
  Pallas kernels  39.2 us (61%)
  waiting for transfers between devices  9.16 us (14%)
  starting transfers between devices  8.64 us (14%)
  local copies, waits for them, and re-layouts  5.14 us (8%)
  other arithmetic  0.76 us (1%)
  between operations  0.7 us (1%)
    pallas_call x1, Pallas kernels, per_device(): pl.pallas_call(kernel, out_shape=[jax.ShapeDtypeStruct((4, ROWS, COLS, 12...  36.6 us
    ppermute x2, waiting for transfers between devices, exchange(): before = lax.ppermute(last, axis, [(i, (i + 1) % n) for i in range(n)])  5.6 us
    ppermute x2, starting transfers between devices, exchange(): before = lax.ppermute(last, axis, [(i, (i + 1) % n) for i in range(n)])  5.42 us
    unnamed x12, local copies, waits for them, and re-layouts  4.34 us
    ppermute x2, waiting for transfers between devices, exchange(): after = lax.ppermute(first, axis, [((i + 1) % n, i) for i in range(n)])  3.56 us
    ppermute x2, starting transfers between devices, exchange(): after = lax.ppermute(first, axis, [((i + 1) % n, i) for i in range(n)])  3.22 us
    pallas_call x1, Pallas kernels, per_device(): pl.pallas_call(lay_out, out_shape=[jax.ShapeDtypeStruct(n, BF16) for n in...  2.06 us
  transfers between devices with their start and end apart: 4, of which 2 were waited for; matrix products, arithmetic and copies ran while one was open for 2% of the time, Pallas kernels for 3%

profile of v7, /device:TPU:7, one launch (start us, length us, event | category | flops | bytes accessed | tf_op | source)
XLA Modules:
  0.0 63.6 jit_solution(5508178846418947773)
XLA Ops:
  0.6 0.0 copy-start.5
  0.6 0.0 copy-start
  0.6 1.0 %copy-done = bf16[1,4,24,16,128]{4,3,2,1,0:T(8,128)(2,1)S(1)} copy-done((bf16[1,4,24,16,128]{4,3,2,1,0:T(8,128)(2,1)S(1)}, bf16[1,4,24,16,128]{4,3,2,1,0:T(8,128)(2,1)}, u32[]{:S(2)}) %copy-start) | copy-done | bytes 393240
  1.6 0.0 copy-start.1
  1.6 0.3 shard_map.86
  2.0 1.7 %collective-permute-start = (bf16[10,4,24,128]{3,2,1,0:T(8,128)(2,1)S(1)}, bf16[10,4,24,128]{3,2,1,0:T(8,128)(2,1)S(1)}, u32[]{:S(2)}, u32[]{:S(2)}) collective-permute-start(bf16[10,4,24,128]{3,2,1,0:T(8,128)(2,1)S(1)} %get-tuple-element.16), channel_id=1, source_target_pairs={{0,1},{1,2},{2,3},{3,4},{4,5},{5,6},{6,7},{7,0},{8,9},{9,10},{10,1... | collective-permute-start | bytes 737288 | tf_op jit(solution)/shard_map/ppermute | solution.py:386
  3.7 3.2 %collective-permute-start.1 = (bf16[10,4,24,128]{3,2,1,0:T(8,128)(2,1)S(1)}, bf16[10,4,24,128]{3,2,1,0:T(8,128)(2,1)S(1)}, u32[]{:S(2)}, u32[]{:S(2)}) collective-permute-start(bf16[10,4,24,128]{3,2,1,0:T(8,128)(2,1)S(1)} %get-tuple-element.17), channel_id=1, source_target_pairs={{1,0},{2,1},{3,2},{4,3},{5,4},{6,5},{7,6},{0,7},{9,8},{10,9},{11,1... | collective-permute-start | bytes 737288 | tf_op jit(solution)/shard_map/ppermute | solution.py:387
  6.9 5.6 %collective-permute-done.left = bf16[10,4,24,128]{3,2,1,0:T(8,128)(2,1)S(1)} collective-permute-done((bf16[10,4,24,128]{3,2,1,0:T(8,128)(2,1)S(1)}, bf16[10,4,24,128]{3,2,1,0:T(8,128)(2,1)S(1)}, u32[]{:S(2)}, u32[]{:S(2)}) %collective-permute-start) | collective-permute-done | bytes 245792 | tf_op jit(solution)/shard_map/ppermute | solution.py:386
  12.5 0.0 collective-permute-done.1.right
  12.5 0.2 shard_map.87
  12.7 3.7 %collective-permute-start.2 = (bf16[4,360,128]{2,1,0:T(8,128)(2,1)S(1)}, bf16[4,360,128]{2,1,0:T(8,128)(2,1)S(1)}, u32[]{:S(2)}, u32[]{:S(2)}) collective-permute-start(bf16[4,360,128]{2,1,0:T(8,128)(2,1)S(1)} %get-tuple-element.18), channel_id=1, source_target_pairs={{0,8},{8,16},{16,24},{24,32},{32,40},{40,48},{48,56},{56,64},{64,7... | collective-permute-start | bytes 1105928 | tf_op jit(solution)/shard_map/ppermute | solution.py:386
  16.4 0.0 collective-permute-start.3
  16.4 0.8 %convert_element_type.16 = bf16[81,64]{1,0:T(8,128)(2,1)S(1)} reshape(bf16[3,3,3,3,64]{4,3,2,1,0:T(4,128)(2,1)} %param.11) | data formatting | bytes 20736 | tf_op jit(solution)/shard_map/convert_element_type | solution.py:410
  17.2 0.8 %convert_bitcast_fusion = f32[3,3,3,3,128]{4,3,2,1,0:T(4,128)S(1)} fusion(bf16[3,3,3,128,3]{3,4,2,1,0:T(4,128)(2,1)} %param.10), kind=kLoop, calls=%fused_computation | loop fusion | flops 10368 | bytes 62208 | tf_op jit(solution)/shard_map/convert_element_type | solution.py:409
  18.0 0.0 copy-start.2
  18.0 1.2 %copy-done.2 = bf16[3,3,3,128,128]{4,3,2,1,0:T(8,128)(2,1)S(1)} copy-done((bf16[3,3,3,128,128]{4,3,2,1,0:T(8,128)(2,1)S(1)}, bf16[3,3,3,128,128]{4,3,2,1,0:T(8,128)(2,1)}, u32[]{:S(2)}) %copy-start.2) | copy-done | bytes 884760
  19.1 1.2 %copy-done.3 = bf16[3,3,3,128,128]{4,3,2,1,0:T(8,128)(2,1)S(1)} copy-done((bf16[3,3,3,128,128]{4,3,2,1,0:T(8,128)(2,1)S(1)}, bf16[3,3,3,128,128]{4,3,2,1,0:T(8,128)(2,1)}, u32[]{:S(2)}) %copy-start.3) | copy-done | bytes 884760
  20.3 1.0 %copy-done.4 = bf16[3,3,3,64,128]{4,3,2,1,0:T(8,128)(2,1)S(1)} copy-done((bf16[3,3,3,64,128]{4,3,2,1,0:T(8,128)(2,1)S(1)}, bf16[3,3,3,64,128]{4,3,2,1,0:T(8,128)(2,1)}, u32[]{:S(2)}) %copy-start.4) | copy-done | bytes 442392
  21.3 2.1 %shard_map.88 = (bf16[2,2,9,256,256]{4,3,2,1,0:T(8,128)(2,1)S(1)}, bf16[9,256,512]{2,1,0:T(8,128)(2,1)S(1)}, bf16[128,512]{1,0:T(8,128)(2,1)S(1)}, bf16[128,256]...) custom-call(bf16[3,9,128,128]{3,2,1,0:T(8,128)(2,1)S(1)} %bitcast.14, ...), custom_call_target="tpu_custom_call" | custom-call | bytes 12582912 | tf_op jit(solution)/shard_map/pallas_call | solution.py:413
  23.4 0.0 collective-permute-done.2.top
  23.4 3.6 %collective-permute-done.3.bottom = bf16[4,360,128]{2,1,0:T(8,128)(2,1)S(1)} collective-permute-done((bf16[4,360,128]{2,1,0:T(8,128)(2,1)S(1)}, bf16[4,360,128]{2,1,0:T(8,128)(2,1)S(1)}, u32[]{:S(2)}, u32[]{:S(2)}) %collective-permute-start.3) | collective-permute-done | bytes 368672 | tf_op jit(solution)/shard_map/ppermute | solution.py:387
  27.0 0.0 copy-done.5
  27.0 0.0 copy-done.1
  27.0 36.6 %shard_map.89 = (bf16[4,24,16,128]{3,2,1,0:T(8,128)(2,1)}, bf16[4,16,24]{2,1,0:T(8,128)(2,1)}) custom-call(bf16[4,24,16,128]{3,2,1,0:T(8,128)(2,1)S(1)} %bitcast.13, bf16[10,4,24,128]{3,2,1,0:T(8,128)(2,1)S(1)} %collective-permute-done.left, bf16[10,4,24,128]{3,2,1,0:T(8,128)(2,1)S(1)} %collective-permute-done.1.right, ...), custom_call_target="tpu_custom_call" | custom-call | tf_op jit(solution)/shard_map/pallas_call | solution.py:423
  (4 shorter events, 0.0 us)
Async XLA Ops:
  0.6 26.3 %copy-start.5 = (f32[128]{0:T(128)S(1)}, f32[128]{0:T(128)}, u32[]{:S(2)}) copy-start(f32[128]{0:T(128)} %param.13) | copy-start | bytes 1540
  0.6 1.0 %copy-start = (bf16[1,4,24,16,128]{4,3,2,1,0:T(8,128)(2,1)S(1)}, bf16[1,4,24,16,128]{4,3,2,1,0:T(8,128)(2,1)}, u32[]{:S(2)}) copy-start(bf16[1,4,24,16,128]{4,3,2,1,0:T(8,128)(2,1)} %param.7) | copy-start | bytes 1179652
  1.6 25.3 %copy-start.1 = (bf16[1,4,24,16,128]{4,3,2,1,0:T(8,128)(2,1)S(1)}, bf16[1,4,24,16,128]{4,3,2,1,0:T(8,128)(2,1)}, u32[]{:S(2)}) copy-start(bf16[1,4,24,16,128]{4,3,2,1,0:T(8,128)(2,1)} %param.7) | copy-start | bytes 1179652
  2.0 10.5 %collective-permute-start = (bf16[10,4,24,128]{3,2,1,0:T(8,128)(2,1)S(1)}, bf16[10,4,24,128]{3,2,1,0:T(8,128)(2,1)S(1)}, u32[]{:S(2)}, u32[]{:S(2)}) collective-permute-start(bf16[10,4,24,128]{3,2,1,0:T(8,128)(2,1)S(1)} %get-tuple-element.16), channel_id=1, source_target_pairs={{0,1},{1,2},{2,3},{3,4},{4,5},{5,6},{6,7},{7,0},{8,9},{9,10},{10,1... | collective-permute-start | bytes 737288 | tf_op jit(solution)/shard_map/ppermute | solution.py:386
  3.7 8.8 %collective-permute-start.1 = (bf16[10,4,24,128]{3,2,1,0:T(8,128)(2,1)S(1)}, bf16[10,4,24,128]{3,2,1,0:T(8,128)(2,1)S(1)}, u32[]{:S(2)}, u32[]{:S(2)}) collective-permute-start(bf16[10,4,24,128]{3,2,1,0:T(8,128)(2,1)S(1)} %get-tuple-element.17), channel_id=1, source_target_pairs={{1,0},{2,1},{3,2},{4,3},{5,4},{6,5},{7,6},{0,7},{9,8},{10,9},{11,1... | collective-permute-start | bytes 737288 | tf_op jit(solution)/shard_map/ppermute | solution.py:387
  12.7 10.7 %collective-permute-start.2 = (bf16[4,360,128]{2,1,0:T(8,128)(2,1)S(1)}, bf16[4,360,128]{2,1,0:T(8,128)(2,1)S(1)}, u32[]{:S(2)}, u32[]{:S(2)}) collective-permute-start(bf16[4,360,128]{2,1,0:T(8,128)(2,1)S(1)} %get-tuple-element.18), channel_id=1, source_target_pairs={{0,8},{8,16},{16,24},{24,32},{32,40},{40,48},{48,56},{56,64},{64,7... | collective-permute-start | bytes 1105928 | tf_op jit(solution)/shard_map/ppermute | solution.py:386
  16.4 10.6 %collective-permute-start.3 = (bf16[4,360,128]{2,1,0:T(8,128)(2,1)S(1)}, bf16[4,360,128]{2,1,0:T(8,128)(2,1)S(1)}, u32[]{:S(2)}, u32[]{:S(2)}) collective-permute-start(bf16[4,360,128]{2,1,0:T(8,128)(2,1)S(1)} %get-tuple-element.19), channel_id=1, source_target_pairs={{8,0},{16,8},{24,16},{32,24},{40,32},{48,40},{56,48},{64,56},{72,6... | collective-permute-start | bytes 1105928 | tf_op jit(solution)/shard_map/ppermute | solution.py:387
  18.0 1.2 %copy-start.2 = (bf16[3,3,3,128,128]{4,3,2,1,0:T(8,128)(2,1)S(1)}, bf16[3,3,3,128,128]{4,3,2,1,0:T(8,128)(2,1)}, u32[]{:S(2)}) copy-start(bf16[3,3,3,128,128]{4,3,2,1,0:T(8,128)(2,1)} %param.8) | copy-start | bytes 2654212
  19.1 1.2 %copy-start.3 = (bf16[3,3,3,128,128]{4,3,2,1,0:T(8,128)(2,1)S(1)}, bf16[3,3,3,128,128]{4,3,2,1,0:T(8,128)(2,1)}, u32[]{:S(2)}) copy-start(bf16[3,3,3,128,128]{4,3,2,1,0:T(8,128)(2,1)} %param.9) | copy-start | bytes 2654212
  20.3 1.0 %copy-start.4 = (bf16[3,3,3,64,128]{4,3,2,1,0:T(8,128)(2,1)S(1)}, bf16[3,3,3,64,128]{4,3,2,1,0:T(8,128)(2,1)}, u32[]{:S(2)}) copy-start(bf16[3,3,3,64,128]{4,3,2,1,0:T(8,128)(2,1)} %param.12) | copy-start | bytes 1327108
